TPU v7x, 32 devices: a whole 2x2x4 slice. The times are simulated.
32 devices in a mesh: group: 2 (over y), dp: 4 (over z), tensor: 4 (over x, core).
Axes of the slice: x: 2, y: 2, z: 4, core: 2. Of those that a mesh axis runs over, the one named last changes fastest.
Arguments:
- tokens: bfloat16 [5120, 8192], P(('group', 'dp'), 'tensor'), parts along dimension 0, may hold values from -6 to 6
- base_weight: bfloat16 [8192, 1024], P('tensor'), may hold values from -0.0625 to 0.0625
- down_basis: bfloat16 [8192, 256], P('tensor'), may hold values from -0.0625 to 0.0625
- up_basis: bfloat16 [256, 1024], P(None, 'tensor'), may hold values from -0.375 to 0.375
- core_bank: bfloat16 [2048, 256, 256], P('dp', 'tensor'), may hold values from -0.375 to 0.375
- request_adapter: int32 [32], P('group'), parts along dimension 0, may hold values from 0 to 2047, as said below
- request_length: int32 [32], P('group'), parts along dimension 0, may hold values from 1 to 320, as said below
- core_slot: int32 [4096], P('group'), parts along dimension 0, may hold values from 0 to 2047, as said below
Outputs:
- projected: bfloat16 [5120, 1024], P(('group', 'dp'), 'tensor'), parts along dimension 0
There are 2 independent parts, one for each index of `group`. A program takes and returns all parts, laid end to end along the dimension named above; an argument that names none is the same for every part. Nothing has to cross between parts.
Inputs may be any that keep to these rules, and one draw needn't show every extreme that they name: `request_length`: requests are numbered home by home: requests k * 4 to (k + 1) * 4 - 1 lie in the rows of index k of dp and their lengths sum to 640; each index of dp has a request of length 320. `request_adapter`: the owner of an adapter is core_slot // 512. The requests of one index of dp use adapters of distinct owners, and in every draw one owner serves a request of length 320 of every index of dp. `core_slot`: A permutation.
All inputs are finite; a program needn't handle non-finite values.
Results may differ from a plain program's by a relative error of at most 0.0048.
Values may be sent and summed in bfloat16 or wider, within the bound.
No kernel may reach another device: no remote copies, remote signals or barrier semaphores. Data moves between devices by JAX's collectives and lax.ppermute only.
A program may use at most 128 MiB of HBM per device.

v0:
```python
import jax
import jax.numpy as jnp
from jax import lax
from jax.sharding import PartitionSpec as P


def local(
    tokens, base_weight, down_basis, up_basis, core_bank, request_adapter, request_length, core_slot
):
    tok_rows = tokens.shape[0]
    owners = lax.axis_size("dp")
    self_index = lax.axis_index("dp")
    per_owner = core_bank.shape[0]
    req_dev = request_length.shape[0] // owners
    base_part = jnp.dot(tokens, base_weight, preferred_element_type=jnp.float32)
    hidden_part = jnp.dot(tokens, down_basis, preferred_element_type=jnp.float32)
    base_share, hidden_share = (
        lax.psum_scatter(base_part, "tensor", scatter_dimension=1, tiled=True),
        lax.psum_scatter(hidden_part, "tensor", scatter_dimension=1, tiled=True),
    )
    hidden_slice = hidden_share.astype(jnp.bfloat16)
    adapter_slot = core_slot[request_adapter]
    adapter_owner = adapter_slot // per_owner
    local_slot = adapter_slot % per_owner
    owner_grid = adapter_owner.reshape(owners, req_dev)
    slot_grid = local_slot.reshape(owners, req_dev)
    own_lengths = lax.dynamic_slice_in_dim(request_length, self_index * req_dev, req_dev)
    own_owners = lax.dynamic_slice_in_dim(adapter_owner, self_index * req_dev, req_dev)
    request_ends = jnp.cumsum(own_lengths)
    starts = request_ends - own_lengths
    positions = jnp.arange(tok_rows, dtype=jnp.int32)
    member = (positions[:, None] >= starts[None, :]) & (positions[:, None] < request_ends[None, :])
    owned_here = owner_grid == self_index
    bank_index = jnp.sum(jnp.where(owned_here, slot_grid, 0), axis=1)
    chosen = jnp.take(core_bank, bank_index, axis=0)
    most_len = 2 * tok_rows // req_dev
    to_owner = own_owners[None, :] == jnp.arange(owners, dtype=jnp.int32)[:, None]
    req_start = jnp.sum(jnp.where(to_owner, starts[None, :], 0), axis=1)
    req_length = jnp.sum(jnp.where(to_owner, own_lengths[None, :], 0), axis=1)
    offsets = jnp.arange(most_len, dtype=jnp.int32)
    row_index = jnp.clip(req_start[:, None] + offsets[None, :], 0, tok_rows - 1)
    live_rows = (offsets[None, :] < req_length[:, None]).astype(jnp.bfloat16)
    packed = jnp.take(hidden_slice, row_index, axis=0) * live_rows[:, :, None]
    partial_rows = jnp.einsum(
        "hmr,hrc->hmc",
        lax.all_to_all(packed, "dp", split_axis=0, concat_axis=0, tiled=True),
        chosen,
        preferred_element_type=jnp.float32,
    )
    returned = lax.all_to_all(partial_rows, "dp", split_axis=0, concat_axis=0, tiled=True)
    row_owner = jnp.sum(jnp.where(member, own_owners[None, :], 0), axis=1)
    row_start = jnp.sum(jnp.where(member, starts[None, :], 0), axis=1)
    core_part = returned[row_owner, positions - row_start]
    core_sum = lax.psum(core_part, "tensor")
    core_out = core_sum.astype(jnp.bfloat16)
    lifted = jnp.dot(core_out, up_basis, preferred_element_type=jnp.float32)
    return (base_share + lifted).astype(jnp.bfloat16)


def solution(mesh):
    in_specs = (
        P(("group", "dp"), "tensor"),
        P("tensor", None),
        P("tensor", None),
        P(None, "tensor"),
        P("dp", "tensor", None),
        P("group"),
        P("group"),
        P("group"),
    )
    out_specs = P(("group", "dp"), "tensor")
    return jax.shard_map(local, mesh=mesh, in_specs=in_specs, out_specs=out_specs, check_vma=False)
```

profile of v0, /device:TPU:0, one launch (start us, length us, event | category | flops | bytes accessed | tf_op | source)
XLA Modules:
  0.0 128.2 jit_solution(2675566705538013334)
XLA Ops:
  6.5 0.0 copy-start
  6.5 0.0 reduce-scatter.5.cloned.1.call-start
  6.5 1.7 %copy-done = bf16[640,2048]{1,0:T(8,128)(2,1)S(1)} copy-done((bf16[640,2048]{1,0:T(8,128)(2,1)S(1)}, bf16[640,2048]{1,0:T(8,128)(2,1)}, u32[]{:S(2)}) %copy-start) | copy-done | bytes 2621464
  8.3 3.1 %fusion.21 = f32[640,256]{0,1:T(8,128)} fusion(bf16[640,2048]{1,0:T(8,128)(2,1)S(1)} %copy-done, bf16[2048,256]{1,0:T(8,128)(2,1)} %param.10), kind=kOutput, calls=%fused_computation.58 | convolution fusion | flops 671088640 | bytes 4325376 | tf_op jit(solution)/shard_map/dot_general | solution.py:16
  11.4 0.0 reduce-scatter.5.cloned.1.call-update
  11.4 0.0 reduce-scatter.3.cloned.1.call-start
  11.4 6.6 %fusion.20 = f32[640,1024]{1,0:T(8,128)} fusion(bf16[640,2048]{1,0:T(8,128)(2,1)S(1)} %copy-done, bf16[2048,1024]{1,0:T(8,128)(2,1)} %param.9), kind=kOutput, calls=%fused_computation.57 | convolution fusion | flops 2684354560 | bytes 9437184 | tf_op jit(solution)/shard_map/dot_general | solution.py:15
  18.0 0.0 copy-start.4
  18.0 0.0 copy-start.1
  18.0 0.0 copy-start.3
  18.0 0.0 reduce-scatter.3.cloned.1.call-update
  18.0 0.6 copy-done.4
  18.7 0.0 copy-done.1
  18.7 0.7 gather_fusion
  19.4 0.1 gather.18
  19.5 0.0 copy-done.3
  19.5 0.1 dynamic_slice.7
  19.5 0.1 dynamic_slice.6
  19.6 0.1 dynamic-slice_bitcast_fusion
  19.7 0.2 reduce-window.8
  19.9 0.1 bitcast_subtract_fusion
  20.0 0.2 select_reduce_fusion.2
  20.1 0.1 compare_select_fusion
  20.2 0.1 reshape.174
  20.3 0.1 fusion.16
  20.4 0.1 fusion.7
  20.5 16.2 %reduce-scatter.5.cloned.1.call-done = f32[640,64]{0,1:T(8,128)} async-done(((f32[640,256]{0,1:T(8,128)}), f32[640,64]{0,1:T(8,128)}) %reduce-scatter.5.cloned.1.call-update) | async-done | bytes 163856 | tf_op jit(solution)/shard_map/reduce_scatter | solution.py:19
  36.7 0.9 convert_element_type.16
  37.7 0.2 copy.13
  37.8 2.8 %gather_fusion.1 = bf16[1280,64]{1,0:T(8,128)(2,1)S(1)} fusion(bf16[640,64]{1,0:T(8,128)(2,1)S(1)} %copy.13, s32[2048]{0:T(1024)S(1)} %pad_clamp_fusion), kind=kCustom, calls=%fused_computation.1 | custom fusion | bytes 332800 | tf_op jit(solution)/shard_map/jit(_take)/gather | solution.py:43
  40.6 0.2 copy.14
  40.8 0.7 select_multiply_fusion
  41.5 4.6 %all-to-all-start = ((bf16[4,320,64]{1,2,0:T(8,128)(2,1)}), bf16[4,320,64]{1,2,0:T(8,128)(2,1)S(1)}, u32[]{:S(2)}, u32[]{:S(2)}) async-start(bf16[4,320,64]{1,2,0:T(8,128)(2,1)} %select_multiply_fusion), calls=%async_computation.2 | async-start | bytes 393216 | tf_op jit(solution)/shard_map/all_to_all | solution.py:46
  46.1 7.1 %gather_fusion.2 = bf16[4,64,256]{2,1,0:T(8,128)(2,1)S(1)} fusion(bf16[512,64,256]{2,1,0:T(8,128)(2,1)} %param.12, s32[1024]{0:T(1024)S(1)} %pad_clamp_fusion.1), kind=kCustom, calls=%fused_computation.2 | custom fusion | bytes 262160 | tf_op jit(solution)/shard_map/jit(_take)/gather | solution.py:35
  53.2 0.4 all-to-all-done
  53.6 1.5 %fusion.2 = f32[4,320,256]{2,1,0:T(8,128)} fusion(bf16[4,320,64]{1,2,0:T(8,128)(2,1)S(1)} %all-to-all-done, bf16[4,64,256]{2,1,0:T(8,128)(2,1)S(1)} %gather_fusion.2, pred[4]{0:T(512)(128)(4,1)S(1)} %compare_and_fusion.1), kind=kOutput, calls=%fused_computation.8 | convolution fusion | flops 42008576 | bytes 1605636 | tf_op jit(solution)/shard_map/hmr,hrc->hmc/dot_general | solution.py:44
  55.1 4.6 %all-to-all-start.1 = ((f32[4,320,256]{2,1,0:T(8,128)}), f32[4,320,256]{2,1,0:T(8,128)}, u32[]{:S(2)}, u32[]{:S(2)}) async-start(f32[4,320,256]{2,1,0:T(8,128)} %fusion.2), calls=%async_computation.3 | async-start | bytes 2621440 | tf_op jit(solution)/shard_map/all_to_all | solution.py:50
  59.7 0.1 select_reduce_fusion.1
  59.9 0.0 copy-start.2
  59.9 31.0 %all-to-all-done.1 = f32[4,320,256]{2,1,0:T(8,128)} async-done(((f32[4,320,256]{2,1,0:T(8,128)}), f32[4,320,256]{2,1,0:T(8,128)}, u32[]{:S(2)}, u32[]{:S(2)}) %all-to-all-start.1) | async-done | bytes 1310752 | tf_op jit(solution)/shard_map/all_to_all | solution.py:50
  90.9 10.8 %gather_fusion.3 = f32[640,256]{1,0:T(8,128)S(1)} fusion(f32[4,320,256]{2,1,0:T(8,128)} %all-to-all-done.1, s32[640]{0:T(1024)S(1)} %fusion.13), kind=kCustom, calls=%fused_computation.3 | custom fusion | bytes 1315840 | tf_op jit(solution)/shard_map/gather | solution.py:53
  101.6 17.5 %all-reduce.1 = bf16[640,256]{1,0:T(8,128)(2,1)} all-reduce(f32[640,256]{1,0:T(8,128)S(1)} %gather_fusion.3), channel_id=1, replica_groups=mesh['group'=2,'dp'=4,'tensor'=4] {'tensor'}, use_global_device_ids=true, to_apply=%region_8.9 | all-reduce | flops 163840 | bytes 983040 | tf_op jit(solution)/shard_map/psum | solution.py:54
  119.2 0.0 reduce-scatter.3.cloned.1.call-done
  119.2 0.0 copy-done.2
  119.2 2.2 %fusion = bf16[640,256]{1,0:T(8,128)(2,1)} fusion(f32[640,256]{1,0:T(8,128)} %reduce-scatter.3.cloned.1.call-done, bf16[256,256]{1,0:T(8,128)(2,1)S(1)} %copy-done.2, bf16[640,256]{1,0:T(8,128)(2,1)} %all-reduce.1), kind=kOutput, calls=%fused_computation.5 | convolution fusion | flops 84213760 | bytes 1441792 | tf_op jit(solution)/shard_map/dot_general | solution.py:56
  (8 shorter events, 0.1 us)
Async XLA Ops:
  6.5 1.7 %copy-start = (bf16[640,2048]{1,0:T(8,128)(2,1)S(1)}, bf16[640,2048]{1,0:T(8,128)(2,1)}, u32[]{:S(2)}) copy-start(bf16[640,2048]{1,0:T(8,128)(2,1)} %param.8) | copy-start | bytes 7864324
  6.5 30.2 %reduce-scatter.5.cloned.1.call-start = ((), (), s32[]{:S(2)}) async-start(), calls=%async_computation.5 | async-start | bytes 819200 | tf_op jit(solution)/shard_map/reduce_scatter | solution.py:19
  11.4 107.8 %reduce-scatter.3.cloned.1.call-start = ((), (), s32[]{:S(2)}) async-start(), calls=%async_computation.4 | async-start | bytes 3276800 | tf_op jit(solution)/shard_map/reduce_scatter | solution.py:18
  18.0 0.7 copy-start.4
  18.0 0.7 copy-start.1
  18.0 1.4 %copy-start.3 = (s32[16]{0:T(128)S(1)}, s32[16]{0:T(128)}, u32[]{:S(2)}) copy-start(s32[16]{0:T(128)} %param.14) | copy-start | bytes 196
  41.5 12.1 %all-to-all-start = ((bf16[4,320,64]{1,2,0:T(8,128)(2,1)}), bf16[4,320,64]{1,2,0:T(8,128)(2,1)S(1)}, u32[]{:S(2)}, u32[]{:S(2)}) async-start(bf16[4,320,64]{1,2,0:T(8,128)(2,1)} %select_multiply_fusion), calls=%async_computation.2 | async-start | bytes 393216 | tf_op jit(solution)/shard_map/all_to_all | solution.py:46
  55.1 35.7 %all-to-all-start.1 = ((f32[4,320,256]{2,1,0:T(8,128)}), f32[4,320,256]{2,1,0:T(8,128)}, u32[]{:S(2)}, u32[]{:S(2)}) async-start(f32[4,320,256]{2,1,0:T(8,128)} %fusion.2), calls=%async_computation.3 | async-start | bytes 2621440 | tf_op jit(solution)/shard_map/all_to_all | solution.py:50
  59.9 59.3 %copy-start.2 = (bf16[256,256]{1,0:T(8,128)(2,1)S(1)}, bf16[256,256]{1,0:T(8,128)(2,1)}, u32[]{:S(2)}) copy-start(bf16[256,256]{1,0:T(8,128)(2,1)} %param.11) | copy-start | bytes 393220
Sparse Core Ops, SparseCore 0:
  11.5 25.1 reduce-scatter.4
  39.3 34.6 reduce-scatter.2
where the time goes:
time: 129 us; the launch traced here: 128 us
  waiting for transfers between devices  47.7 us (37%)
  local copies, waits for them, and re-layouts  24.5 us (19%)
  blocking collectives  17.5 us (14%)
  between operations  13.5 us (10%)
  matrix products  13.3 us (10%)
  starting transfers between devices  9.25 us (7%)
  other arithmetic  2.5 us (2%)
    all_to_all x1, waiting for transfers between devices, local(): lax.all_to_all(partial_rows, 'dp', split_axis=0, concat_axis=0, tiled=True)  31 us
    psum x1, blocking collectives, local(): core_sum = lax.psum(core_part, 'tensor')  17.5 us
    reduce_scatter x1, waiting for transfers between devices, local(): lax.psum_scatter(hidden_part, 'tensor', scatter_dimension=1, tiled=True)  16.2 us
    gather x1, local copies, waits for them, and re-layouts, local(): core_part = returned[row_owner, positions - row_start]  10.8 us
    gather x1, local copies, waits for them, and re-layouts, local(): chosen = jnp.take(core_bank, bank_index, axis=0)  7.06 us
    dot_general x1, matrix products, local(): base_part = jnp.dot(tokens, base_weight, preferred_element_type=jnp.float32)  6.56 us
    all_to_all x1, starting transfers between devices, local(): lax.all_to_all(partial_rows, 'dp', split_axis=0, concat_axis=0, tiled=True)  4.62 us
    all_to_all x1, starting transfers between devices, local(): lax.all_to_all(packed, 'dp', split_axis=0, concat_axis=0, tiled=True)  4.58 us
  transfers between devices with their start and end apart: 4, of which 3 were waited for; matrix products, arithmetic and copies ran while one was open for 25% of the time, Pallas kernels for 0%

commit v1 on v0

v1 whole, which is shorter than its diff:
```python
import functools

import jax
import jax.numpy as jnp
from jax import lax
from jax.experimental import pallas as pl
from jax.experimental.pallas import tpu as pltpu
from jax.sharding import PartitionSpec as P

F32 = jnp.float32
BF16 = jnp.bfloat16
CORES = 2
LANES = 128
VMEM_LIMIT = 40 * 1024 * 1024

ANY = pl.BlockSpec(memory_space=pl.ANY)
SMEM = pl.BlockSpec(memory_space=pltpu.SMEM)
VMEM = pl.BlockSpec(memory_space=pltpu.VMEM)


def params():
    return pltpu.CompilerParams(vmem_limit_bytes=VMEM_LIMIT)


def row_chunks(rows, parts):
    size = rows // parts
    return [(i * size, size) for i in range(parts)]


def hidden_kernel(
    sizes, place, adapters, lengths, slots, bank, tokens, down, *rest
):
    owners, req_dev, per_owner, width, block, parts = sizes
    picks, (send, keep, table) = rest[:owners], rest[owners : owners + 3]
    tok_buf, down_buf, tok_sem, down_sem, pick_sem = rest[owners + 3 :]
    chunks = row_chunks(tok_buf.shape[0], parts)
    down_copy = pltpu.make_async_copy(down, down_buf, down_sem)
    down_copy.start()
    tok_copies = []
    for i, (at, size) in enumerate(chunks):
        copy = pltpu.make_async_copy(
            tokens.at[pl.ds(at, size)], tok_buf.at[pl.ds(at, size)], tok_sem.at[i]
        )
        copy.start()
        tok_copies.append(copy)
    me, core = place[0], place[1] % CORES
    pick_copies = []
    for shift in range(owners):
        home = (me + shift) % owners
        index = jnp.int32(0)
        for q in range(req_dev):
            slot = slots[adapters[home * req_dev + q]]
            index = jnp.where(slot // per_owner == me, slot % per_owner, index)
        copy = pltpu.make_async_copy(bank.at[index], picks[shift], pick_sem.at[shift])
        copy.start()
        pick_copies.append(copy)
    for shift in range(owners):
        table[0, shift] = 0
        table[1, shift] = 0
    start = jnp.int32(0)
    for q in range(req_dev):
        owner = slots[adapters[me * req_dev + q]] // per_owner
        shift = (me - owner + owners) % owners
        end = start + lengths[me * req_dev + q]
        table[0, shift] = start
        table[1, shift] = end
        start = end
    down_copy.wait()
    for i, (at, size) in enumerate(chunks):
        tok_copies[i].wait()
        part = jnp.dot(
            tok_buf[at : at + size, :], down_buf[...], preferred_element_type=F32
        )
        halves = [
            jnp.concatenate(
                [part[:, (CORES * x + c) * block : (CORES * x + c + 1) * block] for x in range(width)],
                axis=1,
            )
            for c in range(CORES)
        ]
        send[at : at + size, :] = jnp.where(core == 0, halves[1], halves[0]).astype(BF16)
        keep[at : at + size, :] = jnp.where(core == 0, halves[0], halves[1])
    for copy in pick_copies:
        copy.wait()


def chip_kernel(width, block, place, keep, got, *rest):
    sends, own = rest[:-1], rest[-1]
    x = place[1] // CORES
    total = keep[...] + got[...].astype(F32)
    pieces = [total[:, i * block : (i + 1) * block] for i in range(width)]

    def piece(index):
        out = pieces[0]
        for i in range(1, width):
            out = jnp.where(index == i, pieces[i], out)
        return out

    own[...] = piece(x)
    pack = LANES // block
    rows = total.shape[0] // pack
    for shift in range(1, width):
        part = piece((x + shift) % width).astype(BF16)
        sends[shift - 1][...] = jnp.concatenate(
            [part[i * rows : (i + 1) * rows] for i in range(pack)], axis=1
        )


def core_kernel(width, block, owners, table, own, *rest):
    gots, cores, (part32, part16) = rest[: width - 1], rest[width - 1 : width - 1 + owners], rest[-2:]
    pack = LANES // block
    total = own[...]
    for got in gots:
        packed = got[...].astype(F32)
        total = total + jnp.concatenate(
            [packed[:, i * block : (i + 1) * block] for i in range(pack)], axis=0
        )
    rows = total.shape[0]
    at = lax.broadcasted_iota(jnp.int32, (rows, block), 0)
    hidden = total.astype(BF16).astype(F32)
    spread = [
        jnp.where((at >= table[0, s]) & (at < table[1, s]), hidden, 0.0) for s in range(owners)
    ]
    lhs = jnp.concatenate(spread, axis=1).astype(BF16)
    rhs = jnp.concatenate([core[...] for core in cores], axis=0)
    part = jnp.dot(lhs, rhs, preferred_element_type=F32)
    part32[...] = part
    part16[...] = part.astype(BF16)


def base_kernel(width, parts, place, tokens, weight, keep, send, tok_buf, w_buf, tok_sem, w_sem):
    x, core = place[1] // CORES, place[1] % CORES
    out_block = keep.shape[2]
    chunks = row_chunks(tok_buf.shape[0], parts)
    order = [(s % width, o) for s in range(1, width + 1) for o in (1, 0)]
    w_copies, tok_copies = [], []
    for i, (shift, other) in enumerate(order):
        block = ((x + shift) % width) * CORES + (core + other) % CORES
        w_copies.append(
            pltpu.make_async_copy(
                weight.at[:, pl.ds(pl.multiple_of(block * out_block, out_block), out_block)],
                w_buf.at[i],
                w_sem.at[i],
            )
        )
    for i, (at, size) in enumerate(chunks):
        tok_copies.append(
            pltpu.make_async_copy(
                tokens.at[pl.ds(at, size)], tok_buf.at[pl.ds(at, size)], tok_sem.at[i]
            )
        )
    w_copies[0].start()
    for copy in tok_copies:
        copy.start()
    for copy in w_copies[1:]:
        copy.start()
    for i, (shift, other) in enumerate(order):
        w_copies[i].wait()
        for j, (at, size) in enumerate(chunks):
            if i == 0:
                tok_copies[j].wait()
            part = jnp.dot(
                tok_buf[at : at + size, :], w_buf[i], preferred_element_type=F32
            )
            if other:
                send[shift, at : at + size, :] = part.astype(BF16)
            else:
                keep[shift, at : at + size, :] = part


def far_kernel(at, size, shift, part32, got_part, up, keep, got_base, out):
    core_out = (part32[...] + got_part[...].astype(F32)).astype(BF16)
    lifted = jnp.dot(core_out, up[...], preferred_element_type=F32)
    out[...] = (keep[0] + got_base[0].astype(F32) + lifted).astype(BF16)


def near_kernel(part32, got_part, up, keep, got_base, out):
    core_out = (part32[...] + got_part[...].astype(F32)).astype(BF16)
    lifted = jnp.dot(core_out, up[...], preferred_element_type=F32)
    out[...] = keep[0] + got_base[0].astype(F32) + lifted


def final_kernel(rows_of, near, *rest):
    gots, out = rest[:-1], rest[-1]
    for i, (at, size) in enumerate(rows_of):
        total = near[at : at + size, :]
        for got in gots[i :: len(rows_of)]:
            total = total + got[...].astype(F32)
        out[at : at + size, :] = total.astype(BF16)


def local(
    tokens, base_weight, down_basis, up_basis, core_bank, request_adapter, request_length, core_slot
):
    rows, depth = tokens.shape
    out_cols, rank = base_weight.shape[1], down_basis.shape[1]
    owners, tensor = lax.axis_size("dp"), lax.axis_size("tensor")
    width = tensor // CORES
    out_block, block = out_cols // tensor, rank // tensor
    per_owner = core_bank.shape[0]
    req_dev = request_length.shape[0] // owners
    place = jnp.stack([lax.axis_index("dp"), lax.axis_index("tensor")]).astype(jnp.int32)

    def pair(a):
        return lax.ppermute(a, "tensor", [(i, i ^ 1) for i in range(tensor)])

    def along_x(a, shift):
        return lax.ppermute(
            a, "tensor", [(i, (i + shift * CORES) % tensor) for i in range(tensor)]
        )

    def along_dp(a, shift):
        return lax.ppermute(a, "dp", [(i, (i + shift) % owners) for i in range(owners)])

    ups = [up_basis] + [along_x(up_basis, -s) for s in range(1, width)]

    parts = 4
    outs = pl.pallas_call(
        functools.partial(
            hidden_kernel, (owners, req_dev, per_owner, width, block, parts)
        ),
        out_shape=[jax.ShapeDtypeStruct((block, rank), BF16)] * owners
        + [
            jax.ShapeDtypeStruct((rows, width * block), BF16),
            jax.ShapeDtypeStruct((rows, width * block), F32),
            jax.ShapeDtypeStruct((2, owners), jnp.int32),
        ],
        in_specs=[SMEM] * 4 + [ANY] * 3,
        out_specs=[VMEM] * (owners + 2) + [SMEM],
        scratch_shapes=[
            pltpu.VMEM((rows, depth), BF16),
            pltpu.VMEM((depth, rank), BF16),
            pltpu.SemaphoreType.DMA((parts,)),
            pltpu.SemaphoreType.DMA,
            pltpu.SemaphoreType.DMA((owners,)),
        ],
        compiler_params=params(),
        cost_estimate=pl.CostEstimate(
            flops=2 * rows * depth * rank, bytes_accessed=2 * depth * (rows + rank), transcendentals=0
        ),
        name="hidden",
    )(place, request_adapter, request_length, core_slot, core_bank, tokens, down_basis)
    picks, (send, keep, table) = outs[:owners], outs[owners:]
    got = pair(send)
    cores = [picks[0]] + [along_dp(picks[s], s) for s in range(1, owners)]

    pack = LANES // block
    outs = pl.pallas_call(
        functools.partial(chip_kernel, width, block),
        out_shape=[jax.ShapeDtypeStruct((rows // pack, LANES), BF16)] * (width - 1)
        + [jax.ShapeDtypeStruct((rows, block), F32)],
        in_specs=[SMEM, VMEM, VMEM],
        out_specs=[VMEM] * width,
        compiler_params=params(),
        name="chip_sum",
    )(place, keep, got)
    hidden_gots = [along_x(outs[s - 1], s) for s in range(1, width)]

    keep_base, send_base = pl.pallas_call(
        functools.partial(base_kernel, width, parts),
        out_shape=[
            jax.ShapeDtypeStruct((width, rows, out_block), F32),
            jax.ShapeDtypeStruct((width, rows, out_block), BF16),
        ],
        in_specs=[SMEM] + [ANY] * 2,
        out_specs=[VMEM] * 2,
        scratch_shapes=[
            pltpu.VMEM((rows, depth), BF16),
            pltpu.VMEM((tensor, depth, out_block), BF16),
            pltpu.SemaphoreType.DMA((parts,)),
            pltpu.SemaphoreType.DMA((tensor,)),
        ],
        compiler_params=params(),
        cost_estimate=pl.CostEstimate(
            flops=2 * rows * depth * out_cols,
            bytes_accessed=2 * depth * (rows + out_cols) + 6 * width * rows * out_block,
            transcendentals=0,
        ),
        name="base",
    )(place, tokens, base_weight)
    got_base = pair(send_base)

    part32, part16 = pl.pallas_call(
        functools.partial(core_kernel, width, block, owners),
        out_shape=[
            jax.ShapeDtypeStruct((rows, rank), F32),
            jax.ShapeDtypeStruct((rows, rank), BF16),
        ],
        in_specs=[SMEM] + [VMEM] * (width + owners),
        out_specs=[VMEM] * 2,
        compiler_params=params(),
        name="core_product",
    )(table, outs[-1], *hidden_gots, *cores)
    got_part = pair(part16)

    halves = 2
    size = rows // halves
    far_gots = []
    for shift in range(1, width):
        for i in range(halves):
            at_rows = pl.BlockSpec((size, rank), functools.partial(lambda i, g: (i, 0), i))
            at_block = pl.BlockSpec(
                (1, size, out_block), functools.partial(lambda s, i, g: (s, i, 0), shift, i)
            )
            far = pl.pallas_call(
                functools.partial(far_kernel, i * size, size, shift),
                grid=(1,),
                out_shape=jax.ShapeDtypeStruct((size, out_block), BF16),
                in_specs=[
                    at_rows,
                    at_rows,
                    pl.BlockSpec((rank, out_block), lambda g: (0, 0)),
                    at_block,
                    at_block,
                ],
                out_specs=pl.BlockSpec((size, out_block), lambda g: (0, 0)),
                compiler_params=params(),
                name="far",
            )(part32, got_part, ups[shift], keep_base, got_base)
            far_gots.append(along_x(far, shift))

    near_block = pl.BlockSpec((1, rows, out_block), lambda g: (0, 0, 0))
    whole_rows = pl.BlockSpec((rows, rank), lambda g: (0, 0))
    near = pl.pallas_call(
        near_kernel,
        grid=(1,),
        out_shape=jax.ShapeDtypeStruct((rows, out_block), F32),
        in_specs=[
            whole_rows,
            whole_rows,
            pl.BlockSpec((rank, out_block), lambda g: (0, 0)),
            near_block,
            near_block,
        ],
        out_specs=pl.BlockSpec((rows, out_block), lambda g: (0, 0)),
        compiler_params=params(),
        name="near",
    )(part32, got_part, up_basis, keep_base, got_base)

    return pl.pallas_call(
        functools.partial(final_kernel, row_chunks(rows, halves)),
        out_shape=jax.ShapeDtypeStruct((rows, out_block), BF16),
        in_specs=[VMEM] * (1 + len(far_gots)),
        out_specs=VMEM,
        compiler_params=params(),
        name="final",
    )(near, *far_gots)


def solution(mesh):
    in_specs = (
        P(("group", "dp"), "tensor"),
        P("tensor", None),
        P("tensor", None),
        P(None, "tensor"),
        P("dp", "tensor", None),
        P("group"),
        P("group"),
        P("group"),
    )
    out_specs = P(("group", "dp"), "tensor")
    return jax.shard_map(local, mesh=mesh, in_specs=in_specs, out_specs=out_specs, check_vma=False)
```

time: 129 us -> 46.4 us (0.36)
  waiting for transfers between devices: 47.7 us -> 15.9 us
  local copies, waits for them, and re-layouts: 24.5 us -> 3.95 us
  blocking collectives: 17.5 us -> 0 us
  Pallas kernels: 0 us -> 14.5 us
  between operations: 13.5 us -> 0.1 us
  matrix products: 13.3 us -> 0 us
  starting transfers between devices: 9.25 us -> 11.7 us
  other arithmetic: 2.5 us -> 0.07 us
    all_to_all x2 -> x0, waiting for transfers between devices: 31.4 us -> none  [the longest x1 31 us: local(): lax.all_to_all(partial_rows, 'dp', split_axis=0, concat_axis=0, tiled=True)]
    gather x6 -> x0, local copies, waits for them, and re-layouts: 21.6 us -> none  [the longest x1 10.8 us: local(): core_part = returned[row_owner, positions - row_start]]
    psum x1 -> x0, blocking collectives: 17.5 us -> none  [local(): core_sum = lax.psum(core_part, 'tensor')]
    reduce_scatter x2 -> x0, waiting for transfers between devices: 16.2 us -> none  [the longest x1 16.2 us: local(): lax.psum_scatter(hidden_part, 'tensor', scatter_dimension=1, tiled=True)]
    ppermute x0 -> x10, waiting for transfers between devices: none -> 15.9 us  [the longest x4 12 us: along_x(): lax.ppermute(a, 'tensor', [(i, (i + shift * CORES) % tensor) for i in ran...]
    pallas_call x0 -> x8, Pallas kernels: none -> 14.5 us  [the longest x1 6.52 us: local(): pl.pallas_call(functools.partial(base_kernel, width, parts), out_shape=[j...]
    dot_general x4 -> x0, matrix products: 13.3 us -> none  [the longest x1 6.56 us: local(): base_part = jnp.dot(tokens, base_weight, preferred_element_type=jnp.float32)]
    ppermute x0 -> x10, starting transfers between devices: none -> 11.7 us  [the longest x3 5.51 us: along_dp(): lax.ppermute(a, 'dp', [(i, (i + shift) % owners) for i in range(owners)])]
  transfers between devices with their start and end apart: 4 -> 10, of which waited for: 3 -> 7; matrix products, arithmetic and copies ran while one was open for 25% -> 0% of each run, Pallas kernels for 0% -> 15%
where the time goes in v1:
time: 46.4 us; the launch traced here: 46.2 us
  waiting for transfers between devices  15.9 us (34%)
  Pallas kernels  14.5 us (31%)
  starting transfers between devices  11.7 us (25%)
  local copies, waits for them, and re-layouts  3.95 us (9%)
    ppermute x4, waiting for transfers between devices, along_x(): lax.ppermute(a, 'tensor', [(i, (i + shift * CORES) % tensor) for i in ran...  12 us
    pallas_call x1, Pallas kernels, local(): pl.pallas_call(functools.partial(base_kernel, width, parts), out_shape=[j...  6.52 us
    ppermute x3, starting transfers between devices, along_dp(): lax.ppermute(a, 'dp', [(i, (i + shift) % owners) for i in range(owners)])  5.51 us
    ppermute x4, starting transfers between devices, along_x(): lax.ppermute(a, 'tensor', [(i, (i + shift * CORES) % tensor) for i in ran...  5.49 us
    pallas_call x1, Pallas kernels, local(): pl.pallas_call(functools.partial(hidden_kernel, (owners, req_dev, per_own...  4.68 us
    unnamed x16, local copies, waits for them, and re-layouts  3.95 us
    ppermute x3, waiting for transfers between devices, along_dp(): lax.ppermute(a, 'dp', [(i, (i + shift) % owners) for i in range(owners)])  2.57 us
    ppermute x3, waiting for transfers between devices, pair(): return lax.ppermute(a, 'tensor', [(i, i ^ 1) for i in range(tensor)])  1.35 us
  transfers between devices with their start and end apart: 10, of which 7 were waited for; matrix products, arithmetic and copies ran while one was open for 0% of the time, Pallas kernels for 15%

profile of v1, /device:TPU:0, one launch (start us, length us, event | category | flops | bytes accessed | tf_op | source)
XLA Modules:
  0.0 46.2 jit_solution(757197139979734965)
XLA Ops:
  0.0 0.1 pad_add_fusion.place
  0.1 0.0 copy-start
  0.1 1.7 %copy-done = bf16[640,2048]{1,0:T(8,128)(2,1)S(1)} copy-done((bf16[640,2048]{1,0:T(8,128)(2,1)S(1)}, bf16[640,2048]{1,0:T(8,128)(2,1)}, u32[]{:S(2)}) %copy-start) | copy-done | bytes 2621464
  1.8 0.0 copy-start.7
  1.8 2.2 %copy-done.7 = bf16[2048,1024]{1,0:T(8,128)(2,1)S(1)} copy-done((bf16[2048,1024]{1,0:T(8,128)(2,1)S(1)}, bf16[2048,1024]{1,0:T(8,128)(2,1)}, u32[]{:S(2)}) %copy-start.7) | copy-done | bytes 4194328
  4.0 0.0 copy-start.1
  4.0 0.0 copy-start.2
  4.0 0.0 copy-start.4
  4.0 0.0 copy-start.5
  4.0 0.0 copy-start.6
  4.0 6.5 %base.1 = (f32[2,640,256]{2,1,0:T(8,128)S(1)}, bf16[2,640,256]{2,1,0:T(8,128)(2,1)S(1)}) custom-call(s32[2]{0:T(128)S(1)} %pad_add_fusion.place, bf16[640,2048]{1,0:T(8,128)(2,1)S(1)} %copy-done, bf16[2048,1024]{1,0:T(8,128)(2,1)S(1)} %copy-done.7), custom_call_target="tpu_custom_call" | custom-call | flops 2684354560 | bytes 8781824 | tf_op jit(solution)/shard_map/base/pallas_call | solution.py:259
  10.6 0.0 copy-start.3
  10.6 0.5 %collective-permute-start.6 = (bf16[2,640,256]{2,1,0:T(8,128)(2,1)S(1)}, bf16[2,640,256]{2,1,0:T(8,128)(2,1)S(1)}, u32[]{:S(2)}, u32[]{:S(2)}) collective-permute-start(bf16[2,640,256]{2,1,0:T(8,128)(2,1)S(1)} %get-tuple-element.30), channel_id=1, source_target_pairs={{0,1},{1,0},{2,3},{3,2},{4,5},{5,4},{6,7},{7,6},{8,9},{9,8},{10,11... | collective-permute-start | bytes 1966088 | tf_op jit(solution)/shard_map/ppermute | solution.py:205
  11.1 0.0 copy-done.1
  11.1 0.0 copy-done.2
  11.1 0.0 copy-done.4
  11.1 0.0 copy-done.5
  11.1 0.0 copy-done.6
  11.1 4.7 %hidden.1 = (bf16[64,256]{1,0:T(8,128)(2,1)S(1)}, bf16[64,256]{1,0:T(8,128)(2,1)S(1)}, bf16[64,256]{1,0:T(8,128)(2,1)S(1)}, bf16[64,256]{1,0:T(8,128)(2,1)S(1)},...) custom-call(s32[2]{0:T(128)S(1)} %pad_add_fusion.place, s32[16]{0:T(128)S(1)} %copy-done.5, ...), custom_call_target="tpu_custom_call" | custom-call | flops 671088640 | bytes 3670016 | tf_op jit(solution)/shard_map/hidden/pallas_call | solution.py:218
  15.8 0.1 collective-permute-start
  15.9 1.3 %collective-permute-done.got = bf16[640,128]{1,0:T(8,128)(2,1)S(1)} collective-permute-done((bf16[640,128]{1,0:T(8,128)(2,1)S(1)}, bf16[640,128]{1,0:T(8,128)(2,1)S(1)}, u32[]{:S(2)}, u32[]{:S(2)}) %collective-permute-start) | collective-permute-done | bytes 163872 | tf_op jit(solution)/shard_map/ppermute | solution.py:205
  17.3 0.8 %chip_sum.1 = (bf16[320,128]{1,0:T(8,128)(2,1)S(1)}, f32[640,64]{1,0:T(8,128)S(1)}) custom-call(s32[2]{0:T(128)S(1)} %pad_add_fusion.place, f32[640,128]{1,0:T(8,128)S(1)} %get-tuple-element.19.keep, bf16[640,128]{1,0:T(8,128)(2,1)S(1)} %collective-permute-done.got), custom_call_target="tpu_custom_call" | custom-call | tf_op jit(solution)/shard_map/chip_sum/pallas_call | solution.py:248
  18.1 2.7 %collective-permute-start.1 = (bf16[320,128]{1,0:T(8,128)(2,1)S(1)}, bf16[320,128]{1,0:T(8,128)(2,1)S(1)}, u32[]{:S(2)}, u32[]{:S(2)}) collective-permute-start(bf16[320,128]{1,0:T(8,128)(2,1)S(1)} %get-tuple-element.22), channel_id=1, source_target_pairs={{0,2},{1,3},{2,0},{3,1},{4,6},{5,7},{6,4},{7,5},{8,10},{9,11},{10,... | collective-permute-start | bytes 245768 | tf_op jit(solution)/shard_map/ppermute | solution.py:208
  20.8 1.6 %collective-permute-start.2 = (bf16[64,256]{1,0:T(8,128)(2,1)S(1)}, bf16[64,256]{1,0:T(8,128)(2,1)S(1)}, u32[]{:S(2)}, u32[]{:S(2)}) collective-permute-start(bf16[64,256]{1,0:T(8,128)(2,1)S(1)} %get-tuple-element.24), channel_id=1, source_target_pairs={{0,4},{4,8},{8,12},{12,0},{1,5},{5,9},{9,13},{13,1},{2,6},{6,10},{... | collective-permute-start | bytes 98312 | tf_op jit(solution)/shard_map/ppermute | solution.py:213
  22.3 2.6 %collective-permute-start.3 = (bf16[64,256]{1,0:T(8,128)(2,1)S(1)}, bf16[64,256]{1,0:T(8,128)(2,1)S(1)}, u32[]{:S(2)}, u32[]{:S(2)}) collective-permute-start(bf16[64,256]{1,0:T(8,128)(2,1)S(1)} %get-tuple-element.25), channel_id=1, source_target_pairs={{0,8},{4,12},{8,0},{12,4},{1,9},{5,13},{9,1},{13,5},{2,10},{6,14},... | collective-permute-start | bytes 98312 | tf_op jit(solution)/shard_map/ppermute | solution.py:213
  24.9 1.3 %collective-permute-start.4 = (bf16[64,256]{1,0:T(8,128)(2,1)S(1)}, bf16[64,256]{1,0:T(8,128)(2,1)S(1)}, u32[]{:S(2)}, u32[]{:S(2)}) collective-permute-start(bf16[64,256]{1,0:T(8,128)(2,1)S(1)} %get-tuple-element.26), channel_id=1, source_target_pairs={{0,12},{4,0},{8,4},{12,8},{1,13},{5,1},{9,5},{13,9},{2,14},{6,2},{... | collective-permute-start | bytes 98312 | tf_op jit(solution)/shard_map/ppermute | solution.py:213
  26.3 0.2 collective-permute-done.2.rest_2_
  26.5 1.2 %collective-permute-done.3.rest_3_ = bf16[64,256]{1,0:T(8,128)(2,1)S(1)} collective-permute-done((bf16[64,256]{1,0:T(8,128)(2,1)S(1)}, bf16[64,256]{1,0:T(8,128)(2,1)S(1)}, u32[]{:S(2)}, u32[]{:S(2)}) %collective-permute-start.3) | collective-permute-done | bytes 32800 | tf_op jit(solution)/shard_map/ppermute | solution.py:213
  27.7 1.2 %collective-permute-done.4.rest_4_ = bf16[64,256]{1,0:T(8,128)(2,1)S(1)} collective-permute-done((bf16[64,256]{1,0:T(8,128)(2,1)S(1)}, bf16[64,256]{1,0:T(8,128)(2,1)S(1)}, u32[]{:S(2)}, u32[]{:S(2)}) %collective-permute-start.4) | collective-permute-done | bytes 32800 | tf_op jit(solution)/shard_map/ppermute | solution.py:213
  28.8 0.0 collective-permute-done.1.rest_0_
  28.8 1.0 %core_product.1 = (f32[640,256]{1,0:T(8,128)S(1)}, bf16[640,256]{1,0:T(8,128)(2,1)S(1)}) custom-call(s32[2,4]{1,0:T(2,128)S(1)} %get-tuple-element.18.table, f32[640,64]{1,0:T(8,128)S(1)} %get-tuple-element.21.own, bf16[320,128]{1,0:T(8,128)(2,1)S(1)} %collective-permute-done.1.rest_0_, bf16[64,256]{1,0:T(8,128)(2,1)S(1)} %get-tuple-element.23.rest_1_, ...), custom_call_target="tpu_custom_call" | custom-call | tf_op jit(solution)/shard_map/core_product/pallas_call | solution.py:283
  29.9 0.1 collective-permute-start.5
  30.0 0.0 copy-done.3
  30.0 0.6 %collective-permute-start.7 = (bf16[256,256]{1,0:T(8,128)(2,1)S(1)}, bf16[256,256]{1,0:T(8,128)(2,1)S(1)}, u32[]{:S(2)}, u32[]{:S(2)}) collective-permute-start(bf16[256,256]{1,0:T(8,128)(2,1)S(1)} %copy-done.3), channel_id=1, source_target_pairs={{0,2},{1,3},{2,0},{3,1},{4,6},{5,7},{6,4},{7,5},{8,10},{9,11},{10,... | collective-permute-start | bytes 393224 | tf_op jit(solution)/shard_map/ppermute | solution.py:208
  30.6 5.3 %collective-permute-done.7.up = bf16[256,256]{1,0:T(8,128)(2,1)S(1)} collective-permute-done((bf16[256,256]{1,0:T(8,128)(2,1)S(1)}, bf16[256,256]{1,0:T(8,128)(2,1)S(1)}, u32[]{:S(2)}, u32[]{:S(2)}) %collective-permute-start.7) | collective-permute-done | bytes 131104 | tf_op jit(solution)/shard_map/ppermute | solution.py:208
  35.9 0.0 collective-permute-done.5.got_part
  35.9 0.0 collective-permute-done.6.got_base
  35.9 0.2 far.2
  36.1 0.6 %collective-permute-start.8 = (bf16[320,256]{1,0:T(8,128)(2,1)S(1)}, bf16[320,256]{1,0:T(8,128)(2,1)S(1)}, u32[]{:S(2)}, u32[]{:S(2)}) collective-permute-start(bf16[320,256]{1,0:T(8,128)(2,1)S(1)} %far.2), channel_id=1, source_target_pairs={{0,2},{1,3},{2,0},{3,1},{4,6},{5,7},{6,4},{7,5},{8,10},{9,11},{10,... | collective-permute-start | bytes 491528 | tf_op jit(solution)/shard_map/ppermute | solution.py:208
  36.7 0.2 far.3
  36.9 1.5 %collective-permute-start.9 = (bf16[320,256]{1,0:T(8,128)(2,1)S(1)}, bf16[320,256]{1,0:T(8,128)(2,1)S(1)}, u32[]{:S(2)}, u32[]{:S(2)}) collective-permute-start(bf16[320,256]{1,0:T(8,128)(2,1)S(1)} %far.3), channel_id=1, source_target_pairs={{0,2},{1,3},{2,0},{3,1},{4,6},{5,7},{6,4},{7,5},{8,10},{9,11},{10,... | collective-permute-start | bytes 491528 | tf_op jit(solution)/shard_map/ppermute | solution.py:208
  38.5 0.3 near.1
  38.7 4.5 %collective-permute-done.8.rest_0_ = bf16[320,256]{1,0:T(8,128)(2,1)S(1)} collective-permute-done((bf16[320,256]{1,0:T(8,128)(2,1)S(1)}, bf16[320,256]{1,0:T(8,128)(2,1)S(1)}, u32[]{:S(2)}, u32[]{:S(2)}) %collective-permute-start.8) | collective-permute-done | bytes 163872 | tf_op jit(solution)/shard_map/ppermute | solution.py:208
  43.3 2.1 %collective-permute-done.9.rest_1_ = bf16[320,256]{1,0:T(8,128)(2,1)S(1)} collective-permute-done((bf16[320,256]{1,0:T(8,128)(2,1)S(1)}, bf16[320,256]{1,0:T(8,128)(2,1)S(1)}, u32[]{:S(2)}, u32[]{:S(2)}) %collective-permute-start.9) | collective-permute-done | bytes 163872 | tf_op jit(solution)/shard_map/ppermute | solution.py:208
  45.4 0.8 %final.1 = bf16[640,256]{1,0:T(8,128)(2,1)} custom-call(f32[640,256]{1,0:T(8,128)S(1)} %near.1, bf16[320,256]{1,0:T(8,128)(2,1)S(1)} %collective-permute-done.8.rest_0_, bf16[320,256]{1,0:T(8,128)(2,1)S(1)} %collective-permute-done.9.rest_1_), custom_call_target="tpu_custom_call" | custom-call | tf_op jit(solution)/shard_map/final/pallas_call | solution.py:340
Async XLA Ops:
  0.1 1.7 %copy-start = (bf16[640,2048]{1,0:T(8,128)(2,1)S(1)}, bf16[640,2048]{1,0:T(8,128)(2,1)}, u32[]{:S(2)}) copy-start(bf16[640,2048]{1,0:T(8,128)(2,1)} %tokens.3) | copy-start | bytes 7864324
  1.8 2.2 %copy-start.7 = (bf16[2048,1024]{1,0:T(8,128)(2,1)S(1)}, bf16[2048,1024]{1,0:T(8,128)(2,1)}, u32[]{:S(2)}) copy-start(bf16[2048,1024]{1,0:T(8,128)(2,1)} %weight.1) | copy-start | bytes 12582916
  4.0 7.1 %copy-start.1 = (bf16[640,2048]{1,0:T(8,128)(2,1)S(1)}, bf16[640,2048]{1,0:T(8,128)(2,1)}, u32[]{:S(2)}) copy-start(bf16[640,2048]{1,0:T(8,128)(2,1)} %tokens.3) | copy-start | bytes 7864324
  4.0 7.1 %copy-start.2 = (bf16[2048,256]{1,0:T(8,128)(2,1)S(1)}, bf16[2048,256]{1,0:T(8,128)(2,1)}, u32[]{:S(2)}) copy-start(bf16[2048,256]{1,0:T(8,128)(2,1)} %down.1) | copy-start | bytes 3145732
  4.0 7.1 %copy-start.4 = (s32[2048]{0:T(1024)S(1)}, s32[2048]{0:T(1024)}, u32[]{:S(2)}) copy-start(s32[2048]{0:T(1024)} %slots.1) | copy-start | bytes 24580
  4.0 7.1 %copy-start.5 = (s32[16]{0:T(128)S(1)}, s32[16]{0:T(128)}, u32[]{:S(2)}) copy-start(s32[16]{0:T(128)} %adapters.1) | copy-start | bytes 196
  4.0 7.1 %copy-start.6 = (s32[16]{0:T(128)S(1)}, s32[16]{0:T(128)}, u32[]{:S(2)}) copy-start(s32[16]{0:T(128)} %lengths.1) | copy-start | bytes 196
  10.6 19.4 %copy-start.3 = (bf16[256,256]{1,0:T(8,128)(2,1)S(1)}, bf16[256,256]{1,0:T(8,128)(2,1)}, u32[]{:S(2)}) copy-start(bf16[256,256]{1,0:T(8,128)(2,1)} %up.1) | copy-start | bytes 393220
  10.6 25.3 %collective-permute-start.6 = (bf16[2,640,256]{2,1,0:T(8,128)(2,1)S(1)}, bf16[2,640,256]{2,1,0:T(8,128)(2,1)S(1)}, u32[]{:S(2)}, u32[]{:S(2)}) collective-permute-start(bf16[2,640,256]{2,1,0:T(8,128)(2,1)S(1)} %get-tuple-element.30), channel_id=1, source_target_pairs={{0,1},{1,0},{2,3},{3,2},{4,5},{5,4},{6,7},{7,6},{8,9},{9,8},{10,11... | collective-permute-start | bytes 1966088 | tf_op jit(solution)/shard_map/ppermute | solution.py:205
  15.8 1.5 %collective-permute-start = (bf16[640,128]{1,0:T(8,128)(2,1)S(1)}, bf16[640,128]{1,0:T(8,128)(2,1)S(1)}, u32[]{:S(2)}, u32[]{:S(2)}) collective-permute-start(bf16[640,128]{1,0:T(8,128)(2,1)S(1)} %get-tuple-element.20), channel_id=1, source_target_pairs={{0,1},{1,0},{2,3},{3,2},{4,5},{5,4},{6,7},{7,6},{8,9},{9,8},{10,11... | collective-permute-start | bytes 491528 | tf_op jit(solution)/shard_map/ppermute | solution.py:205
  18.1 10.8 %collective-permute-start.1 = (bf16[320,128]{1,0:T(8,128)(2,1)S(1)}, bf16[320,128]{1,0:T(8,128)(2,1)S(1)}, u32[]{:S(2)}, u32[]{:S(2)}) collective-permute-start(bf16[320,128]{1,0:T(8,128)(2,1)S(1)} %get-tuple-element.22), channel_id=1, source_target_pairs={{0,2},{1,3},{2,0},{3,1},{4,6},{5,7},{6,4},{7,5},{8,10},{9,11},{10,... | collective-permute-start | bytes 245768 | tf_op jit(solution)/shard_map/ppermute | solution.py:208
  20.8 5.7 %collective-permute-start.2 = (bf16[64,256]{1,0:T(8,128)(2,1)S(1)}, bf16[64,256]{1,0:T(8,128)(2,1)S(1)}, u32[]{:S(2)}, u32[]{:S(2)}) collective-permute-start(bf16[64,256]{1,0:T(8,128)(2,1)S(1)} %get-tuple-element.24), channel_id=1, source_target_pairs={{0,4},{4,8},{8,12},{12,0},{1,5},{5,9},{9,13},{13,1},{2,6},{6,10},{... | collective-permute-start | bytes 98312 | tf_op jit(solution)/shard_map/ppermute | solution.py:213
  22.3 5.3 %collective-permute-start.3 = (bf16[64,256]{1,0:T(8,128)(2,1)S(1)}, bf16[64,256]{1,0:T(8,128)(2,1)S(1)}, u32[]{:S(2)}, u32[]{:S(2)}) collective-permute-start(bf16[64,256]{1,0:T(8,128)(2,1)S(1)} %get-tuple-element.25), channel_id=1, source_target_pairs={{0,8},{4,12},{8,0},{12,4},{1,9},{5,13},{9,1},{13,5},{2,10},{6,14},... | collective-permute-start | bytes 98312 | tf_op jit(solution)/shard_map/ppermute | solution.py:213
  24.9 3.9 %collective-permute-start.4 = (bf16[64,256]{1,0:T(8,128)(2,1)S(1)}, bf16[64,256]{1,0:T(8,128)(2,1)S(1)}, u32[]{:S(2)}, u32[]{:S(2)}) collective-permute-start(bf16[64,256]{1,0:T(8,128)(2,1)S(1)} %get-tuple-element.26), channel_id=1, source_target_pairs={{0,12},{4,0},{8,4},{12,8},{1,13},{5,1},{9,5},{13,9},{2,14},{6,2},{... | collective-permute-start | bytes 98312 | tf_op jit(solution)/shard_map/ppermute | solution.py:213
  29.9 6.0 %collective-permute-start.5 = (bf16[640,256]{1,0:T(8,128)(2,1)S(1)}, bf16[640,256]{1,0:T(8,128)(2,1)S(1)}, u32[]{:S(2)}, u32[]{:S(2)}) collective-permute-start(bf16[640,256]{1,0:T(8,128)(2,1)S(1)} %get-tuple-element.28), channel_id=1, source_target_pairs={{0,1},{1,0},{2,3},{3,2},{4,5},{5,4},{6,7},{7,6},{8,9},{9,8},{10,11... | collective-permute-start | bytes 983048 | tf_op jit(solution)/shard_map/ppermute | solution.py:205
  30.0 5.9 %collective-permute-start.7 = (bf16[256,256]{1,0:T(8,128)(2,1)S(1)}, bf16[256,256]{1,0:T(8,128)(2,1)S(1)}, u32[]{:S(2)}, u32[]{:S(2)}) collective-permute-start(bf16[256,256]{1,0:T(8,128)(2,1)S(1)} %copy-done.3), channel_id=1, source_target_pairs={{0,2},{1,3},{2,0},{3,1},{4,6},{5,7},{6,4},{7,5},{8,10},{9,11},{10,... | collective-permute-start | bytes 393224 | tf_op jit(solution)/shard_map/ppermute | solution.py:208
  36.1 7.2 %collective-permute-start.8 = (bf16[320,256]{1,0:T(8,128)(2,1)S(1)}, bf16[320,256]{1,0:T(8,128)(2,1)S(1)}, u32[]{:S(2)}, u32[]{:S(2)}) collective-permute-start(bf16[320,256]{1,0:T(8,128)(2,1)S(1)} %far.2), channel_id=1, source_target_pairs={{0,2},{1,3},{2,0},{3,1},{4,6},{5,7},{6,4},{7,5},{8,10},{9,11},{10,... | collective-permute-start | bytes 491528 | tf_op jit(solution)/shard_map/ppermute | solution.py:208
  36.9 8.5 %collective-permute-start.9 = (bf16[320,256]{1,0:T(8,128)(2,1)S(1)}, bf16[320,256]{1,0:T(8,128)(2,1)S(1)}, u32[]{:S(2)}, u32[]{:S(2)}) collective-permute-start(bf16[320,256]{1,0:T(8,128)(2,1)S(1)} %far.3), channel_id=1, source_target_pairs={{0,2},{1,3},{2,0},{3,1},{4,6},{5,7},{6,4},{7,5},{8,10},{9,11},{10,... | collective-permute-start | bytes 491528 | tf_op jit(solution)/shard_map/ppermute | solution.py:208

commit v2 on v0

v2 whole, which is shorter than its diff:
```python
import functools

import jax
import jax.numpy as jnp
from jax import lax
from jax.experimental import pallas as pl
from jax.experimental.pallas import tpu as pltpu
from jax.sharding import PartitionSpec as P

F32 = jnp.float32
BF16 = jnp.bfloat16
CORES = 2
MIB = 1024 * 1024

ANY = pl.BlockSpec(memory_space=pl.ANY)
SMEM = pl.BlockSpec(memory_space=pltpu.SMEM)
VMEM = pl.BlockSpec(memory_space=pltpu.VMEM)


def params(mib=8):
    return pltpu.CompilerParams(vmem_limit_bytes=mib * MIB)


def cost(flops, read):
    return pl.CostEstimate(flops=flops, bytes_accessed=read, transcendentals=0)


def ordered(arrays, *after):
    count = len(arrays)
    return pl.pallas_call(
        lambda *refs: None,
        out_shape=[jax.ShapeDtypeStruct(a.shape, a.dtype) for a in arrays],
        in_specs=[ANY] * (count + len(after)),
        out_specs=[ANY] * count,
        input_output_aliases={i: i for i in range(count)},
        compiler_params=params(1),
        cost_estimate=cost(0, 0),
        name="ordered",
    )(*arrays, *after)


def pick_kernel(sizes, adapters, lengths, slots, bank, after, *rest):
    owners, req_dev, per_owner = sizes
    picks, (table, sem, int_sem) = rest[:owners], rest[owners : owners + 3]
    copies = [
        pltpu.make_async_copy(a, b, int_sem.at[i])
        for i, (a, b) in enumerate(zip((adapters, lengths, slots), rest[owners + 3 :]))
    ]
    for copy in copies:
        copy.start()
    for copy in copies:
        copy.wait()
    adapters, lengths, slots = rest[owners + 3 :]
    me = lax.axis_index("dp")
    copies = []
    for shift in range(owners):
        home = (me + shift) % owners
        index = jnp.int32(0)
        for q in range(req_dev):
            slot = slots[adapters[home * req_dev + q]]
            index = jnp.where(slot // per_owner == me, slot % per_owner, index)
        copy = pltpu.make_async_copy(bank.at[index], picks[shift], sem.at[shift])
        copy.start()
        copies.append(copy)
    for shift in range(owners):
        table[0, shift] = 0
        table[1, shift] = 0
    start = jnp.int32(0)
    for q in range(req_dev):
        owner = slots[adapters[me * req_dev + q]] // per_owner
        shift = (me - owner + owners) % owners
        end = start + lengths[me * req_dev + q]
        table[0, shift] = start
        table[1, shift] = end
        start = end
    for copy in copies:
        copy.wait()


def pack_kernel(owners, *refs):
    far, out = refs[owners], refs[-1]
    cols = far.shape[2]
    block, rank = refs[0].shape
    for s in range(owners):
        for at in range(0, rank, cols):
            out[pl.ds((s * (rank // cols) + at // cols) * block, block), :] = refs[s][:, at : at + cols]
    first = owners * block * rank // cols
    rows = far.shape[1]
    for i in range(far.shape[0]):
        out[pl.ds(first + i * rows, rows), :] = far[i]


def sum_kernel(keep, *rest):
    gots, out = rest[:-1], rest[-1]
    total = keep[...]
    for got in gots:
        total = total + got[: total.shape[0], :].astype(F32)
    out[...] = total


def block_product(width, shift, other, tokens, weight):
    me = lax.axis_index("tensor")
    x, core = me // CORES, me % CORES
    out_block = weight.shape[1] // (width * CORES)
    block = ((x + shift) % width) * CORES + (core + other) % CORES
    columns = pl.ds(pl.multiple_of(block * out_block, out_block), out_block)
    return jnp.dot(tokens[...], weight[:, columns], preferred_element_type=F32)


def far_base_kernel(width, tokens, weight, after, send, keep):
    for shift in range(1, width):
        send[shift - 1] = block_product(width, shift, 1, tokens, weight).astype(BF16)
        keep[shift - 1] = block_product(width, shift, 0, tokens, weight)


def near_base_kernel(width, tokens, weight, after, send, keep):
    send[...] = block_product(width, 0, 1, tokens, weight)
    keep[...] = block_product(width, 0, 0, tokens, weight)


def far_kernel(width, halves, table, hidden, got_hidden, mine, others, *rest):
    ups, keep, rest = rest[: width - 1], rest[width - 1], rest[width + 1 :]
    outs, core_out, rhs = rest[:-2], rest[-2], rest[-1]
    core = lax.axis_index("tensor") % CORES
    owners = table.shape[1]
    rank, cols = core_out.shape[1], outs[0].shape[1]
    block = hidden.shape[1] // CORES
    for s in range(owners):
        for packed, at in ((mine, core), (others, 1 - core)):
            to = pl.ds(pl.multiple_of((s * CORES + at) * block, block), block)
            for i in range(rank // cols):
                rhs[to, i * cols : (i + 1) * cols] = packed[
                    pl.ds((s * (rank // cols) + i) * block, block), :
                ]
    total = (hidden[...] + got_hidden[...]).astype(BF16).astype(F32)
    row = lax.broadcasted_iota(jnp.int32, total.shape, 0)
    lhs = jnp.concatenate(
        [
            jnp.where((row >= table[0, s]) & (row < table[1, s]), total, 0.0).astype(BF16)
            for s in range(owners)
        ],
        axis=1,
    )
    part = jnp.dot(lhs, rhs[...], preferred_element_type=F32).astype(BF16)
    core_out[...] = part
    rows = part.shape[0]
    size = rows // halves
    first = owners * block * rank // cols
    for i in range(width - 1):
        up = jnp.concatenate(
            [ups[i][pl.ds(at, rank), :] for at in range(rows, ups[i].shape[0], rank)], axis=1
        )
        lifted = jnp.dot(part, up, preferred_element_type=F32)
        got = others[pl.ds(first + i * rows, rows), :].astype(F32)
        sent = (keep[i] + got + lifted).astype(BF16)
        for j in range(halves):
            outs[i * halves + j][...] = sent[j * size : (j + 1) * size]


def near_kernel(up, keep, got, part, out):
    lifted = jnp.dot(part[...], up[...], preferred_element_type=F32)
    out[...] = keep[...] + got[...] + lifted


def final_kernel(halves, near, *rest):
    gots, out = rest[:-1], rest[-1]
    size = near.shape[0] // halves
    for i in range(halves):
        rows = pl.ds(i * size, size)
        total = near[rows, :]
        for got in gots[i::halves]:
            total = total + got[...].astype(F32)
        out[rows, :] = total.astype(BF16)


def local(
    tokens, base_weight, down_basis, up_basis, core_bank, request_adapter, request_length, core_slot
):
    rows, depth = tokens.shape
    out_cols, rank = base_weight.shape[1], down_basis.shape[1]
    owners, tensor = lax.axis_size("dp"), lax.axis_size("tensor")
    width = tensor // CORES
    out_block, block = out_cols // tensor, rank // tensor
    cols = CORES * block
    per_owner = core_bank.shape[0]
    req_dev = request_length.shape[0] // owners
    def pair(a):
        return lax.ppermute(a, "tensor", [(i, i ^ 1) for i in range(tensor)])

    def along_x(a, shift):
        return lax.ppermute(
            a, "tensor", [(i, (i + shift * CORES) % tensor) for i in range(tensor)]
        )

    def along_dp(a, shift):
        return lax.ppermute(a, "dp", [(i, (i + shift) % owners) for i in range(owners)])

    up_parts = [up_basis[:, at : at + cols] for at in range(0, out_block, cols)]

    chip = lax.axis_index("tensor") // CORES
    part = jnp.dot(tokens, down_basis, preferred_element_type=F32)
    keep = lax.dynamic_slice_in_dim(part, chip * cols, cols, axis=1)
    gots = []
    for shift in range(1, width):
        at = (chip + shift) % width * cols
        send = lax.dynamic_slice_in_dim(part, at, cols, axis=1).astype(BF16)
        gots.append(along_x(jnp.concatenate([send] + up_parts, axis=0), shift))

    outs = pl.pallas_call(
        functools.partial(pick_kernel, (owners, req_dev, per_owner)),
        out_shape=[jax.ShapeDtypeStruct((block, rank), BF16)] * owners
        + [jax.ShapeDtypeStruct((2, owners), jnp.int32)],
        in_specs=[ANY] * 5,
        out_specs=[VMEM] * owners + [SMEM],
        scratch_shapes=[
            pltpu.SemaphoreType.DMA((owners,)),
            pltpu.SemaphoreType.DMA((3,)),
            pltpu.SMEM(request_adapter.shape, jnp.int32),
            pltpu.SMEM(request_length.shape, jnp.int32),
            pltpu.SMEM(core_slot.shape, jnp.int32),
        ],
        compiler_params=params(38),
        cost_estimate=cost(0, 8 * MIB),
        name="pick",
    )(request_adapter, request_length, core_slot, core_bank, keep)
    table = outs[-1]
    mine = [outs[0]] + [along_dp(outs[s], s) for s in range(1, owners)]

    hidden = pl.pallas_call(
        sum_kernel,
        out_shape=jax.ShapeDtypeStruct((rows, cols), F32),
        in_specs=[VMEM] * width,
        out_specs=VMEM,
        compiler_params=params(),
        cost_estimate=cost(0, rows * cols * 10),
        name="hidden_sum",
    )(keep, *gots)
    got_hidden = pair(hidden)

    def base(kernel, dtypes, lead, after, name):
        shape = lead + (rows, out_block)
        blocks = CORES * (lead[0] if lead else 1)
        return pl.pallas_call(
            functools.partial(kernel, width),
            out_shape=[jax.ShapeDtypeStruct(shape, dtype) for dtype in dtypes],
            in_specs=[VMEM] * 2 + [ANY],
            out_specs=[VMEM] * 2,
            compiler_params=params(),
            cost_estimate=cost(
                2 * rows * depth * out_block * blocks, 2 * depth * (rows + out_block * blocks)
            ),
            name=name,
        )(tokens, base_weight, after)

    far_send, far_keep = base(far_base_kernel, (BF16, F32), (width - 1,), outs[0], "far_base")

    packed = pl.pallas_call(
        functools.partial(pack_kernel, owners),
        out_shape=jax.ShapeDtypeStruct(
            (owners * block * rank // out_block + (width - 1) * rows, out_block), BF16
        ),
        in_specs=[VMEM] * (owners + 1),
        out_specs=VMEM,
        compiler_params=params(),
        cost_estimate=cost(0, 0),
        name="pack",
    )(*mine, far_send)
    got_packed = pair(packed)
    near_send, near_keep = base(near_base_kernel, (F32, F32), (), packed, "near_base")

    halves = 2
    size = rows // halves
    outs = pl.pallas_call(
        functools.partial(far_kernel, width, halves),
        out_shape=[jax.ShapeDtypeStruct((size, out_block), BF16)] * (halves * (width - 1))
        + [jax.ShapeDtypeStruct((rows, rank), BF16)],
        in_specs=[SMEM] + [VMEM] * (4 + width) + [ANY],
        out_specs=[VMEM] * (halves * (width - 1) + 1),
        scratch_shapes=[pltpu.VMEM((owners * cols, rank), BF16)],
        compiler_params=params(),
        cost_estimate=cost(2 * rows * (owners * cols * rank + rank * out_block), rows * out_block * 10),
        name="far",
    )(table, hidden, got_hidden, packed, got_packed, *gots[::-1], far_keep, near_keep)
    core_out = outs[-1]
    order = [along_x(outs[i], i // halves + 1) for i in range(halves * (width - 1))]

    (near_send,) = ordered([near_send], core_out)
    near_got = pair(near_send)
    near = pl.pallas_call(
        near_kernel,
        out_shape=jax.ShapeDtypeStruct((rows, out_block), F32),
        in_specs=[VMEM] * 4,
        out_specs=VMEM,
        compiler_params=params(),
        cost_estimate=cost(2 * rows * rank * out_block, rows * out_block * 12),
        name="near",
    )(up_basis, near_keep, near_got, core_out)

    return pl.pallas_call(
        functools.partial(final_kernel, halves),
        out_shape=jax.ShapeDtypeStruct((rows, out_block), BF16),
        in_specs=[VMEM] * (1 + len(order)),
        out_specs=VMEM,
        compiler_params=params(),
        cost_estimate=cost(0, rows * out_block * 8),
        name="final",
    )(near, *order)


def solution(mesh):
    in_specs = (
        P(("group", "dp"), "tensor"),
        P("tensor", None),
        P("tensor", None),
        P(None, "tensor"),
        P("dp", "tensor", None),
        P("group"),
        P("group"),
        P("group"),
    )
    out_specs = P(("group", "dp"), "tensor")
    return jax.shard_map(local, mesh=mesh, in_specs=in_specs, out_specs=out_specs, check_vma=False)
```

time: 129 us -> 32.6 us (0.25)
  waiting for transfers between devices: 47.7 us -> 8.81 us
  local copies, waits for them, and re-layouts: 24.5 us -> 1.35 us
  blocking collectives: 17.5 us -> 0 us
  between operations: 13.5 us -> 0.19 us
  matrix products: 13.3 us -> 2.62 us
  Pallas kernels: 0 us -> 8.01 us
  other arithmetic: 2.5 us -> 0.02 us
  starting transfers between devices: 9.25 us -> 11.4 us
    all_to_all x2 -> x0, waiting for transfers between devices: 31.4 us -> none  [the longest x1 31 us: local(): lax.all_to_all(partial_rows, 'dp', split_axis=0, concat_axis=0, tiled=True)]
    gather x6 -> x0, local copies, waits for them, and re-layouts: 21.6 us -> none  [the longest x1 10.8 us: local(): core_part = returned[row_owner, positions - row_start]]
    psum x1 -> x0, blocking collectives: 17.5 us -> none  [local(): core_sum = lax.psum(core_part, 'tensor')]
    reduce_scatter x2 -> x0, waiting for transfers between devices: 16.2 us -> none  [the longest x1 16.2 us: local(): lax.psum_scatter(hidden_part, 'tensor', scatter_dimension=1, tiled=True)]
    ppermute x0 -> x9, starting transfers between devices: none -> 11.4 us  [the longest x3 5.57 us: along_dp(): lax.ppermute(a, 'dp', [(i, (i + shift) % owners) for i in range(owners)])]
    dot_general x4 -> x1, matrix products: 13.3 us -> 2.62 us  [local(): part = jnp.dot(tokens, down_basis, preferred_element_type=F32)]
    all_to_all x2 -> x0, starting transfers between devices: 9.2 us -> none  [the longest x1 4.62 us: local(): lax.all_to_all(partial_rows, 'dp', split_axis=0, concat_axis=0, tiled=True)]
    ppermute x0 -> x9, waiting for transfers between devices: none -> 8.81 us  [the longest x3 7.69 us: along_x(): lax.ppermute(a, 'tensor', [(i, (i + shift * CORES) % tensor) for i in ran...]
  transfers between devices with their start and end apart: 4 -> 9, of which waited for: 3 -> 4; matrix products, arithmetic and copies ran while one was open for 25% -> 0% of each run, Pallas kernels for 0% -> 19%
where the time goes in v2:
time: 32.6 us; the launch traced here: 32.4 us
  starting transfers between devices  11.4 us (35%)
  waiting for transfers between devices  8.81 us (27%)
  Pallas kernels  8.01 us (25%)
  matrix products  2.62 us (8%)
  local copies, waits for them, and re-layouts  1.35 us (4%)
    ppermute x3, waiting for transfers between devices, along_x(): lax.ppermute(a, 'tensor', [(i, (i + shift * CORES) % tensor) for i in ran...  7.69 us
    ppermute x3, starting transfers between devices, along_dp(): lax.ppermute(a, 'dp', [(i, (i + shift) % owners) for i in range(owners)])  5.57 us
    ppermute x3, starting transfers between devices, along_x(): lax.ppermute(a, 'tensor', [(i, (i + shift * CORES) % tensor) for i in ran...  5.04 us
    pallas_call x2, Pallas kernels, base(): pl.pallas_call(functools.partial(kernel, width), out_shape=[jax.ShapeDtyp...  3.07 us
    pallas_call x1, Pallas kernels, local(): pl.pallas_call(functools.partial(pick_kernel, (owners, req_dev, per_owner...  2.71 us
    dot_general x1, matrix products, local(): part = jnp.dot(tokens, down_basis, preferred_element_type=F32)  2.62 us
    pallas_call x1, Pallas kernels, local(): pl.pallas_call(functools.partial(far_kernel, width, halves), out_shape=[j...  1.13 us
    ppermute x3, waiting for transfers between devices, along_dp(): lax.ppermute(a, 'dp', [(i, (i + shift) % owners) for i in range(owners)])  1 us
  transfers between devices with their start and end apart: 9, of which 4 were waited for; matrix products, arithmetic and copies ran while one was open for 0% of the time, Pallas kernels for 19%

profile of v2, /device:TPU:0, one launch (start us, length us, event | category | flops | bytes accessed | tf_op | source)
XLA Modules:
  0.0 32.4 jit_solution(7025853866725602931)
XLA Ops:
  0.0 0.0 copy-start
  0.0 1.0 %fusion = (bf16[256,128]{1,0:T(8,128)(2,1)S(1)}, bf16[256,128]{1,0:T(8,128)(2,1)S(1)}) fusion(bf16[256,256]{1,0:T(8,128)(2,1)} %up.1), kind=kLoop, calls=%fused_computation.3 | loop fusion | bytes 262144 | tf_op jit(solution)/shard_map/slice | solution.py:198
  1.0 0.3 copy-done
  1.3 0.0 copy-start.4
  1.3 0.0 copy-start.5
  1.3 0.0 copy-start.6
  1.3 2.6 %fusion.1 = f32[640,256]{1,0:T(8,128)S(1)} fusion(bf16[640,2048]{1,0:T(8,128)(2,1)} %tokens.3, bf16[2048,256]{1,0:T(8,128)(2,1)S(1)} %copy-done), kind=kOutput, calls=%fused_computation.4 | convolution fusion | flops 671088640 | bytes 4325376 | tf_op jit(solution)/shard_map/dot_general | solution.py:201
  4.0 3.0 %collective-permute-start.3 = (bf16[1152,128]{1,0:T(8,128)(2,1)S(1)}, bf16[1152,128]{1,0:T(8,128)(2,1)S(1)}, u32[]{:S(2)}, u32[]{:S(2)}) collective-permute-start(bf16[1152,128]{1,0:T(8,128)(2,1)S(1)} %pad_maximum_fusion), channel_id=1, source_target_pairs={{0,2},{1,3},{2,0},{3,1},{4,6},{5,7},{6,4},{7,5},{8,10},{9,11},{10,... | collective-permute-start | bytes 884744 | tf_op jit(solution)/shard_map/ppermute | solution.py:191
  7.0 0.0 copy-done.4
  7.0 0.0 copy-done.5
  7.0 0.0 copy-done.6
  7.1 0.0 copy-start.1
  7.1 0.0 copy-start.2
  7.1 2.7 %pick.1 = (bf16[64,256]{1,0:T(8,128)(2,1)S(1)}, bf16[64,256]{1,0:T(8,128)(2,1)S(1)}, bf16[64,256]{1,0:T(8,128)(2,1)S(1)}, bf16[64,256]{1,0:T(8,128)(2,1)S(1)}, s32[2,4]{1,0:T(2,128)S(1)}) custom-call(s32[16]{0:T(128)S(1)} %copy-done.5, s32[16]{0:T(128)S(1)} %copy-done.6, s32[2048]{0:T(1024)S(1)} %copy-done.4, bf16[512,64,256]{2,1,0:T(8,128)(2,1)} %bank.1, ...), custom_call_target="tpu_custom_call" | custom-call | bytes 8388608 | tf_op jit(solution)/shard_map/pick/pallas_call | solution.py:209
  9.8 1.6 %collective-permute-start = (bf16[64,256]{1,0:T(8,128)(2,1)S(1)}, bf16[64,256]{1,0:T(8,128)(2,1)S(1)}, u32[]{:S(2)}, u32[]{:S(2)}) collective-permute-start(bf16[64,256]{1,0:T(8,128)(2,1)S(1)} %get-tuple-element.18), channel_id=1, source_target_pairs={{0,4},{4,8},{8,12},{12,0},{1,5},{5,9},{9,13},{13,1},{2,6},{6,10},{... | collective-permute-start | bytes 98312 | tf_op jit(solution)/shard_map/ppermute | solution.py:196
  11.4 2.6 %collective-permute-start.1 = (bf16[64,256]{1,0:T(8,128)(2,1)S(1)}, bf16[64,256]{1,0:T(8,128)(2,1)S(1)}, u32[]{:S(2)}, u32[]{:S(2)}) collective-permute-start(bf16[64,256]{1,0:T(8,128)(2,1)S(1)} %get-tuple-element.19), channel_id=1, source_target_pairs={{0,8},{4,12},{8,0},{12,4},{1,9},{5,13},{9,1},{13,5},{2,10},{6,14},... | collective-permute-start | bytes 98312 | tf_op jit(solution)/shard_map/ppermute | solution.py:196
  14.0 1.3 %collective-permute-start.2 = (bf16[64,256]{1,0:T(8,128)(2,1)S(1)}, bf16[64,256]{1,0:T(8,128)(2,1)S(1)}, u32[]{:S(2)}, u32[]{:S(2)}) collective-permute-start(bf16[64,256]{1,0:T(8,128)(2,1)S(1)} %get-tuple-element.20), channel_id=1, source_target_pairs={{0,12},{4,0},{8,4},{12,8},{1,13},{5,1},{9,5},{13,9},{2,14},{6,2},{... | collective-permute-start | bytes 98312 | tf_op jit(solution)/shard_map/ppermute | solution.py:196
  15.4 0.0 copy-done.1
  15.4 0.0 copy-done.2
  15.4 1.5 %far_base.1 = (bf16[1,640,256]{2,1,0:T(8,128)(2,1)S(1)}, f32[1,640,256]{2,1,0:T(8,128)S(1)}) custom-call(bf16[640,2048]{1,0:T(8,128)(2,1)S(1)} %copy-done.2, bf16[2048,1024]{1,0:T(8,128)(2,1)S(1)} %copy-done.1, bf16[64,256]{1,0:T(8,128)(2,1)S(1)} %get-tuple-element.17.after.refs_0_), custom_call_target="tpu_custom_call" | custom-call | flops 1342177280 | bytes 4718592 | tf_op jit(solution)/shard_map/far_base/pallas_call | solution.py:243
  16.9 0.0 collective-permute-done.refs_1_
  16.9 0.0 collective-permute-done.1.refs_2_
  16.9 1.0 %collective-permute-done.2.refs_3_ = bf16[64,256]{1,0:T(8,128)(2,1)S(1)} collective-permute-done((bf16[64,256]{1,0:T(8,128)(2,1)S(1)}, bf16[64,256]{1,0:T(8,128)(2,1)S(1)}, u32[]{:S(2)}, u32[]{:S(2)}) %collective-permute-start.2) | collective-permute-done | bytes 32800 | tf_op jit(solution)/shard_map/ppermute | solution.py:196
  18.0 0.1 collective-permute-start.5
  18.0 0.0 collective-permute-done.3.rest_0_
  18.1 0.6 %collective-permute-start.4 = (f32[640,128]{1,0:T(8,128)S(1)}, f32[640,128]{1,0:T(8,128)S(1)}, u32[]{:S(2)}, u32[]{:S(2)}) collective-permute-start(f32[640,128]{1,0:T(8,128)S(1)} %hidden_sum.1.hidden), channel_id=1, source_target_pairs={{0,1},{1,0},{2,3},{3,2},{4,5},{5,4},{6,7},{7,6},{8,9},{9,8},{10,11... | collective-permute-start | bytes 983048 | tf_op jit(solution)/shard_map/ppermute | solution.py:188
  18.7 1.5 %near_base.1 = (f32[640,256]{1,0:T(8,128)S(1)}, f32[640,256]{1,0:T(8,128)S(1)}) custom-call(bf16[640,2048]{1,0:T(8,128)(2,1)S(1)} %copy-done.2, bf16[2048,1024]{1,0:T(8,128)(2,1)S(1)} %copy-done.1, bf16[896,256]{1,0:T(8,128)(2,1)S(1)} %pack.1.after.mine), custom_call_target="tpu_custom_call" | custom-call | flops 1342177280 | bytes 4718592 | tf_op jit(solution)/shard_map/near_base/pallas_call | solution.py:243
  20.2 0.0 copy-start.3
  20.2 0.0 collective-permute-done.5.others
  20.2 0.1 collective-permute-done.4.got_hidden
  20.3 1.1 %far.1 = (bf16[320,256]{1,0:T(8,128)(2,1)S(1)}, bf16[320,256]{1,0:T(8,128)(2,1)S(1)}, bf16[640,256]{1,0:T(8,128)(2,1)S(1)}) custom-call(s32[2,4]{1,0:T(2,128)S(1)} %get-tuple-element.24.table, f32[640,128]{1,0:T(8,128)S(1)} %hidden_sum.1.hidden, f32[640,128]{1,0:T(8,128)S(1)} %collective-permute-done.4.got_hidden, bf16[896,256]{1,0:T(8,128)(2,1)S(1)} %pack.1.after.mine, ...), custom_call_target="tpu_custom_call" | custom-call | flops 251658240 | bytes 1638400 | tf_op jit(solution)/shard_map/far/pallas_call | solution.py:273
  21.5 0.2 collective-permute-start.6
  21.7 0.5 %collective-permute-start.7 = (bf16[320,256]{1,0:T(8,128)(2,1)S(1)}, bf16[320,256]{1,0:T(8,128)(2,1)S(1)}, u32[]{:S(2)}, u32[]{:S(2)}) collective-permute-start(bf16[320,256]{1,0:T(8,128)(2,1)S(1)} %get-tuple-element.27), channel_id=1, source_target_pairs={{0,2},{1,3},{2,0},{3,1},{4,6},{5,7},{6,4},{7,5},{8,10},{9,11},{10,... | collective-permute-start | bytes 491528 | tf_op jit(solution)/shard_map/ppermute | solution.py:191
  22.2 1.5 %collective-permute-start.8 = (bf16[320,256]{1,0:T(8,128)(2,1)S(1)}, bf16[320,256]{1,0:T(8,128)(2,1)S(1)}, u32[]{:S(2)}, u32[]{:S(2)}) collective-permute-start(bf16[320,256]{1,0:T(8,128)(2,1)S(1)} %get-tuple-element.28), channel_id=1, source_target_pairs={{0,2},{1,3},{2,0},{3,1},{4,6},{5,7},{6,4},{7,5},{8,10},{9,11},{10,... | collective-permute-start | bytes 491528 | tf_op jit(solution)/shard_map/ppermute | solution.py:191
  23.7 0.0 collective-permute-done.6.got
  23.7 0.0 copy-done.3
  23.7 0.2 near.1
  24.0 4.7 %collective-permute-done.7.rest_0_ = bf16[320,256]{1,0:T(8,128)(2,1)S(1)} collective-permute-done((bf16[320,256]{1,0:T(8,128)(2,1)S(1)}, bf16[320,256]{1,0:T(8,128)(2,1)S(1)}, u32[]{:S(2)}, u32[]{:S(2)}) %collective-permute-start.7) | collective-permute-done | bytes 163872 | tf_op jit(solution)/shard_map/ppermute | solution.py:191
  28.7 3.0 %collective-permute-done.8.rest_1_ = bf16[320,256]{1,0:T(8,128)(2,1)S(1)} collective-permute-done((bf16[320,256]{1,0:T(8,128)(2,1)S(1)}, bf16[320,256]{1,0:T(8,128)(2,1)S(1)}, u32[]{:S(2)}, u32[]{:S(2)}) %collective-permute-start.8) | collective-permute-done | bytes 163872 | tf_op jit(solution)/shard_map/ppermute | solution.py:191
  31.7 0.8 %final.1 = bf16[640,256]{1,0:T(8,128)(2,1)} custom-call(f32[640,256]{1,0:T(8,128)S(1)} %near.1, bf16[320,256]{1,0:T(8,128)(2,1)S(1)} %collective-permute-done.7.rest_0_, bf16[320,256]{1,0:T(8,128)(2,1)S(1)} %collective-permute-done.8.rest_1_), custom_call_target="tpu_custom_call" | custom-call | bytes 1310720 | tf_op jit(solution)/shard_map/final/pallas_call | solution.py:299
  (6 shorter events, 0.1 us)
Async XLA Ops:
  0.0 1.3 %copy-start = (bf16[2048,256]{1,0:T(8,128)(2,1)S(1)}, bf16[2048,256]{1,0:T(8,128)(2,1)}, u32[]{:S(2)}) copy-start(bf16[2048,256]{1,0:T(8,128)(2,1)} %param.10) | copy-start | bytes 3145732
  1.3 5.7 %copy-start.4 = (s32[2048]{0:T(1024)S(1)}, s32[2048]{0:T(1024)}, u32[]{:S(2)}) copy-start(s32[2048]{0:T(1024)} %slots.1) | copy-start | bytes 24580
  1.3 5.7 %copy-start.5 = (s32[16]{0:T(128)S(1)}, s32[16]{0:T(128)}, u32[]{:S(2)}) copy-start(s32[16]{0:T(128)} %adapters.1) | copy-start | bytes 196
  1.3 5.8 %copy-start.6 = (s32[16]{0:T(128)S(1)}, s32[16]{0:T(128)}, u32[]{:S(2)}) copy-start(s32[16]{0:T(128)} %lengths.1) | copy-start | bytes 196
  4.0 14.1 %collective-permute-start.3 = (bf16[1152,128]{1,0:T(8,128)(2,1)S(1)}, bf16[1152,128]{1,0:T(8,128)(2,1)S(1)}, u32[]{:S(2)}, u32[]{:S(2)}) collective-permute-start(bf16[1152,128]{1,0:T(8,128)(2,1)S(1)} %pad_maximum_fusion), channel_id=1, source_target_pairs={{0,2},{1,3},{2,0},{3,1},{4,6},{5,7},{6,4},{7,5},{8,10},{9,11},{10,... | collective-permute-start | bytes 884744 | tf_op jit(solution)/shard_map/ppermute | solution.py:191
  7.1 8.3 %copy-start.1 = (bf16[2048,1024]{1,0:T(8,128)(2,1)S(1)}, bf16[2048,1024]{1,0:T(8,128)(2,1)}, u32[]{:S(2)}) copy-start(bf16[2048,1024]{1,0:T(8,128)(2,1)} %weight.3) | copy-start | bytes 12582916
  7.1 8.3 %copy-start.2 = (bf16[640,2048]{1,0:T(8,128)(2,1)S(1)}, bf16[640,2048]{1,0:T(8,128)(2,1)}, u32[]{:S(2)}) copy-start(bf16[640,2048]{1,0:T(8,128)(2,1)} %tokens.3) | copy-start | bytes 7864324
  9.8 7.1 %collective-permute-start = (bf16[64,256]{1,0:T(8,128)(2,1)S(1)}, bf16[64,256]{1,0:T(8,128)(2,1)S(1)}, u32[]{:S(2)}, u32[]{:S(2)}) collective-permute-start(bf16[64,256]{1,0:T(8,128)(2,1)S(1)} %get-tuple-element.18), channel_id=1, source_target_pairs={{0,4},{4,8},{8,12},{12,0},{1,5},{5,9},{9,13},{13,1},{2,6},{6,10},{... | collective-permute-start | bytes 98312 | tf_op jit(solution)/shard_map/ppermute | solution.py:196
  11.4 5.5 %collective-permute-start.1 = (bf16[64,256]{1,0:T(8,128)(2,1)S(1)}, bf16[64,256]{1,0:T(8,128)(2,1)S(1)}, u32[]{:S(2)}, u32[]{:S(2)}) collective-permute-start(bf16[64,256]{1,0:T(8,128)(2,1)S(1)} %get-tuple-element.19), channel_id=1, source_target_pairs={{0,8},{4,12},{8,0},{12,4},{1,9},{5,13},{9,1},{13,5},{2,10},{6,14},... | collective-permute-start | bytes 98312 | tf_op jit(solution)/shard_map/ppermute | solution.py:196
  14.0 3.9 %collective-permute-start.2 = (bf16[64,256]{1,0:T(8,128)(2,1)S(1)}, bf16[64,256]{1,0:T(8,128)(2,1)S(1)}, u32[]{:S(2)}, u32[]{:S(2)}) collective-permute-start(bf16[64,256]{1,0:T(8,128)(2,1)S(1)} %get-tuple-element.20), channel_id=1, source_target_pairs={{0,12},{4,0},{8,4},{12,8},{1,13},{5,1},{9,5},{13,9},{2,14},{6,2},{... | collective-permute-start | bytes 98312 | tf_op jit(solution)/shard_map/ppermute | solution.py:196
  18.0 2.2 %collective-permute-start.5 = (bf16[896,256]{1,0:T(8,128)(2,1)S(1)}, bf16[896,256]{1,0:T(8,128)(2,1)S(1)}, u32[]{:S(2)}, u32[]{:S(2)}) collective-permute-start(bf16[896,256]{1,0:T(8,128)(2,1)S(1)} %pack.1.after.mine), channel_id=1, source_target_pairs={{0,1},{1,0},{2,3},{3,2},{4,5},{5,4},{6,7},{7,6},{8,9},{9,8},{10,11... | collective-permute-start | bytes 1376264 | tf_op jit(solution)/shard_map/ppermute | solution.py:188
  18.1 2.2 %collective-permute-start.4 = (f32[640,128]{1,0:T(8,128)S(1)}, f32[640,128]{1,0:T(8,128)S(1)}, u32[]{:S(2)}, u32[]{:S(2)}) collective-permute-start(f32[640,128]{1,0:T(8,128)S(1)} %hidden_sum.1.hidden), channel_id=1, source_target_pairs={{0,1},{1,0},{2,3},{3,2},{4,5},{5,4},{6,7},{7,6},{8,9},{9,8},{10,11... | collective-permute-start | bytes 983048 | tf_op jit(solution)/shard_map/ppermute | solution.py:188
  20.2 3.5 %copy-start.3 = (bf16[256,256]{1,0:T(8,128)(2,1)S(1)}, bf16[256,256]{1,0:T(8,128)(2,1)}, u32[]{:S(2)}) copy-start(bf16[256,256]{1,0:T(8,128)(2,1)} %up.1) | copy-start | bytes 393220
  21.5 2.2 %collective-permute-start.6 = (f32[640,256]{1,0:T(8,128)S(1)}, f32[640,256]{1,0:T(8,128)S(1)}, u32[]{:S(2)}, u32[]{:S(2)}) collective-permute-start(f32[640,256]{1,0:T(8,128)S(1)} %ordered.1), channel_id=1, source_target_pairs={{0,1},{1,0},{2,3},{3,2},{4,5},{5,4},{6,7},{7,6},{8,9},{9,8},{10,11... | collective-permute-start | bytes 1966088 | tf_op jit(solution)/shard_map/ppermute | solution.py:188
  21.7 7.0 %collective-permute-start.7 = (bf16[320,256]{1,0:T(8,128)(2,1)S(1)}, bf16[320,256]{1,0:T(8,128)(2,1)S(1)}, u32[]{:S(2)}, u32[]{:S(2)}) collective-permute-start(bf16[320,256]{1,0:T(8,128)(2,1)S(1)} %get-tuple-element.27), channel_id=1, source_target_pairs={{0,2},{1,3},{2,0},{3,1},{4,6},{5,7},{6,4},{7,5},{8,10},{9,11},{10,... | collective-permute-start | bytes 491528 | tf_op jit(solution)/shard_map/ppermute | solution.py:191
  22.2 9.4 %collective-permute-start.8 = (bf16[320,256]{1,0:T(8,128)(2,1)S(1)}, bf16[320,256]{1,0:T(8,128)(2,1)S(1)}, u32[]{:S(2)}, u32[]{:S(2)}) collective-permute-start(bf16[320,256]{1,0:T(8,128)(2,1)S(1)} %get-tuple-element.28), channel_id=1, source_target_pairs={{0,2},{1,3},{2,0},{3,1},{4,6},{5,7},{6,4},{7,5},{8,10},{9,11},{10,... | collective-permute-start | bytes 491528 | tf_op jit(solution)/shard_map/ppermute | solution.py:191

commit v3 on v2

v3 whole, which is shorter than its diff:
```python
import functools
import math

import jax
import jax.numpy as jnp
from jax import lax
from jax.experimental import pallas as pl
from jax.experimental.pallas import tpu as pltpu
from jax.sharding import PartitionSpec as P

F32 = jnp.float32
BF16 = jnp.bfloat16
CORES = 2
MIB = 1024 * 1024

ANY = pl.BlockSpec(memory_space=pl.ANY)
VMEM = pl.BlockSpec(memory_space=pltpu.VMEM)


def params(mib=8):
    return pltpu.CompilerParams(vmem_limit_bytes=mib * MIB)


def cost(flops, read):
    return pl.CostEstimate(flops=flops, bytes_accessed=read, transcendentals=0)


def ordered(arrays, *after, read=0):
    count = len(arrays)
    return pl.pallas_call(
        lambda *refs: None,
        out_shape=[jax.ShapeDtypeStruct(a.shape, a.dtype) for a in arrays],
        in_specs=[ANY] * (count + len(after)),
        out_specs=[ANY] * count,
        input_output_aliases={i: i for i in range(count)},
        compiler_params=params(1),
        cost_estimate=cost(0, read),
        name="ordered",
    )(*arrays, *after)


def split_kernel(width, part, up, *rest):
    sends, keep = rest[:-1], rest[-1]
    x = lax.axis_index("tensor") // CORES
    rows, cols = keep.shape
    rank, out_block = up.shape
    pieces = [part[:, i * cols : (i + 1) * cols] for i in range(width)]

    def piece(index):
        out = pieces[0]
        for i in range(1, width):
            out = jnp.where(index == i, pieces[i], out)
        return out

    keep[...] = piece(x)
    for shift in range(1, width):
        send = sends[shift - 1]
        send[:rows, :] = piece((x + shift) % width).astype(BF16)
        for i in range(out_block // cols):
            send[pl.ds(rows + i * rank, rank), :] = up[:, i * cols : (i + 1) * cols]


def pick_kernel(sizes, adapters, lengths, slots, bank, after, *rest):
    owners, req_dev, per_owner = sizes
    picks, (table, sem, int_sem) = rest[:owners], rest[owners : owners + 3]
    copies = [
        pltpu.make_async_copy(a, b, int_sem.at[i])
        for i, (a, b) in enumerate(zip((adapters, lengths, slots), rest[owners + 3 :]))
    ]
    for copy in copies:
        copy.start()
    for copy in copies:
        copy.wait()
    adapters, lengths, slots = rest[owners + 3 :]
    me = lax.axis_index("dp")
    copies = []
    for shift in range(owners):
        home = me ^ shift
        index = jnp.int32(0)
        for q in range(req_dev):
            slot = slots[adapters[home * req_dev + q]]
            index = jnp.where(slot // per_owner == me, slot % per_owner, index)
        copy = pltpu.make_async_copy(bank.at[index], picks[shift], sem.at[shift])
        copy.start()
        copies.append(copy)
    start = jnp.int32(0)
    at = lax.broadcasted_iota(jnp.int32, table.shape, 0)
    lane = lax.broadcasted_iota(jnp.int32, table.shape, 1)
    bounds = jnp.zeros(table.shape, jnp.int32)
    for q in range(req_dev):
        shift = (slots[adapters[me * req_dev + q]] // per_owner) ^ me
        end = start + lengths[me * req_dev + q]
        bounds = jnp.where(at == shift, jnp.where(lane == 0, start, end), bounds)
        start = end
    table[...] = bounds
    for copy in copies:
        copy.wait()


def pack_kernel(order, *refs):
    out = refs[-1]
    for i, s in enumerate(order):
        out[s] = refs[i][...]


def sum_kernel(keep, *rest):
    gots, (out, send) = rest[:-2], rest[-2:]
    total = keep[...]
    for got in gots:
        total = total + got[: total.shape[0], :].astype(F32)
    out[...] = total
    send[...] = total.astype(BF16)


def block_product(width, shift, other, tokens, weight):
    me = lax.axis_index("tensor")
    x, core = me // CORES, me % CORES
    out_block = weight.shape[1] // (width * CORES)
    block = ((x + shift) % width) * CORES + (core + other) % CORES
    columns = pl.ds(pl.multiple_of(block * out_block, out_block), out_block)
    return jnp.dot(tokens[...], weight[:, columns], preferred_element_type=F32)


def far_base_kernel(width, owners, tokens, weight, table, keep, mask, *sends):
    rows, cols = tokens.shape[0], mask.shape[1] // owners
    row = lax.broadcasted_iota(jnp.int32, (rows, cols), 0)
    for s in range(owners):
        inside = (row >= table[s : s + 1, 0:1]) & (row < table[s : s + 1, 1:2])
        mask[:, s * cols : (s + 1) * cols] = jnp.where(inside, 1.0, 0.0).astype(BF16)
    size = sends[0].shape[1]
    for shift in range(1, width):
        other = block_product(width, shift, 1, tokens, weight).astype(BF16)
        for i, send in enumerate(sends):
            send[shift - 1] = other[i * size : (i + 1) * size]
        keep[shift - 1] = block_product(width, shift, 0, tokens, weight)


def near_base_kernel(width, tokens, weight, after, keep, *sends):
    other = block_product(width, 0, 1, tokens, weight).astype(BF16)
    size = sends[0].shape[0]
    for i, send in enumerate(sends):
        send[...] = other[i * size : (i + 1) * size]
    keep[...] = block_product(width, 0, 0, tokens, weight)


def far_kernel(width, halves, mask, hidden, got_hidden, mine, others, *rest):
    ups, keep, rest = rest[: width - 1], rest[width - 1], rest[width:]
    gots, rest = rest[: -halves * (width - 1) - 2], rest[-halves * (width - 1) - 2 :]
    outs, core_out, rhs = rest[:-2], rest[-2], rest[-1]
    core = lax.axis_index("tensor") % CORES
    owners = mask.shape[1] // hidden.shape[1]
    rank = core_out.shape[1]
    block = hidden.shape[1] // CORES
    owners = mask.shape[1] // hidden.shape[1]
    for s in range(owners):
        for cores, at in ((mine, core), (others, 1 - core)):
            rhs[pl.ds(pl.multiple_of((s * CORES + at) * block, block), block), :] = cores[s]
    total = (hidden[...] + got_hidden[...].astype(F32)).astype(BF16)
    lhs = jnp.concatenate([total] * owners, axis=1) * mask[...]
    part = jnp.dot(lhs, rhs[...], preferred_element_type=F32).astype(BF16)
    core_out[...] = part
    rows = part.shape[0]
    size = rows // halves
    for i in range(width - 1):
        up = jnp.concatenate(
            [ups[i][pl.ds(at, rank), :] for at in range(rows, ups[i].shape[0], rank)], axis=1
        )
        lifted = jnp.dot(part, up, preferred_element_type=F32)
        got = jnp.concatenate([a[i] for a in gots], axis=0).astype(F32)
        sent = (keep[i] + got + lifted).astype(BF16)
        for j in range(halves):
            outs[i * halves + j][...] = sent[j * size : (j + 1) * size]


def near_kernel(up, keep, part, *rest):
    gots, out = rest[:-1], rest[-1]
    lifted = jnp.dot(part[...], up[...], preferred_element_type=F32)
    got = jnp.concatenate([a[...] for a in gots], axis=0).astype(F32)
    out[...] = keep[...] + got + lifted


def final_kernel(halves, near, *rest):
    gots, out = rest[:-1], rest[-1]
    size = near.shape[0] // halves
    for i in range(halves):
        rows = pl.ds(i * size, size)
        total = near[rows, :]
        for got in gots[i::halves]:
            total = total + got[...].astype(F32)
        out[rows, :] = total.astype(BF16)


def local(
    tokens, base_weight, down_basis, up_basis, core_bank, request_adapter, request_length, core_slot
):
    rows, depth = tokens.shape
    out_cols, rank = base_weight.shape[1], down_basis.shape[1]
    owners, tensor = lax.axis_size("dp"), lax.axis_size("tensor")
    width = tensor // CORES
    out_block, block = out_cols // tensor, rank // tensor
    cols = CORES * block
    per_owner = core_bank.shape[0]
    req_dev = request_length.shape[0] // owners
    def pair(a):
        return lax.ppermute(a, "tensor", [(i, i ^ 1) for i in range(tensor)])

    def along_x(a, shift):
        return lax.ppermute(
            a, "tensor", [(i, (i + shift * CORES) % tensor) for i in range(tensor)]
        )

    def along_dp(a, shift):
        return lax.ppermute(a, "dp", [(i, i ^ shift) for i in range(owners)])

    part = jnp.dot(tokens, down_basis, preferred_element_type=F32)
    outs = pl.pallas_call(
        functools.partial(split_kernel, width),
        out_shape=[jax.ShapeDtypeStruct((rows + rank * out_block // cols, cols), BF16)] * (width - 1)
        + [jax.ShapeDtypeStruct((rows, cols), F32)],
        in_specs=[VMEM] * 2,
        out_specs=[VMEM] * width,
        compiler_params=params(),
        cost_estimate=cost(0, 0),
        name="split",
    )(part, up_basis)
    keep = outs[-1]
    gots = [along_x(outs[s - 1], s) for s in range(1, width)]

    outs = pl.pallas_call(
        functools.partial(pick_kernel, (owners, req_dev, per_owner)),
        out_shape=[jax.ShapeDtypeStruct((block, rank), BF16)] * owners
        + [jax.ShapeDtypeStruct((max(owners, 8), 128), jnp.int32)],
        in_specs=[ANY] * 5,
        out_specs=[VMEM] * (owners + 1),
        scratch_shapes=[
            pltpu.SemaphoreType.DMA((owners,)),
            pltpu.SemaphoreType.DMA((3,)),
            pltpu.SMEM(request_adapter.shape, jnp.int32),
            pltpu.SMEM(request_length.shape, jnp.int32),
            pltpu.SMEM(core_slot.shape, jnp.int32),
        ],
        compiler_params=params(38),
        cost_estimate=cost(0, 2 * MIB),
        name="pick",
    )(request_adapter, request_length, core_slot, core_bank, keep)
    table = outs[-1]
    picks = ordered(outs[:-1], read=30 * MIB)
    order = sorted(range(1, owners), key=lambda s: -s.bit_length())
    mine = [picks[0]] + [along_dp(picks[s], s) for s in order]

    hidden, hidden_send = pl.pallas_call(
        sum_kernel,
        out_shape=[jax.ShapeDtypeStruct((rows, cols), dtype) for dtype in (F32, BF16)],
        in_specs=[VMEM] * width,
        out_specs=[VMEM] * 2,
        compiler_params=params(),
        cost_estimate=cost(0, rows * cols * 10),
        name="hidden_sum",
    )(keep, *gots)
    got_hidden = pair(hidden_send)

    def base(kernel, shapes, after, name):
        blocks = math.prod(shapes[0].shape[:-2]) * CORES
        return pl.pallas_call(
            kernel,
            out_shape=shapes,
            in_specs=[VMEM] * 3,
            out_specs=[VMEM] * len(shapes),
            compiler_params=params(),
            cost_estimate=cost(
                2 * rows * depth * out_block * blocks, 2 * depth * (rows + out_block * blocks)
            ),
            name=name,
        )(tokens, base_weight, after)

    parts = 2
    far_keep, mask, *far_send = base(
        functools.partial(far_base_kernel, width, owners),
        [
            jax.ShapeDtypeStruct((width - 1, rows, out_block), F32),
            jax.ShapeDtypeStruct((rows, owners * cols), BF16),
        ]
        + [jax.ShapeDtypeStruct((width - 1, rows // parts, out_block), BF16)] * parts,
        ordered([table], picks[0])[0],
        "far_base",
    )

    near_keep, *near_send = base(
        functools.partial(near_base_kernel, width),
        [jax.ShapeDtypeStruct((rows, out_block), F32)]
        + [jax.ShapeDtypeStruct((rows // parts, out_block), BF16)] * parts,
        ordered([hidden], far_keep)[0],
        "near_base",
    )

    packed = pl.pallas_call(
        functools.partial(pack_kernel, [0] + order),
        out_shape=jax.ShapeDtypeStruct((owners, block, rank), BF16),
        in_specs=[VMEM] * owners + [ANY],
        out_specs=VMEM,
        compiler_params=params(),
        cost_estimate=cost(0, 0),
        name="pack",
    )(*mine, near_keep)
    got_packed = pair(packed)
    far_got = [pair(a) for a in far_send]

    halves = 1
    size = rows // halves
    outs = pl.pallas_call(
        functools.partial(far_kernel, width, halves),
        out_shape=[jax.ShapeDtypeStruct((size, out_block), BF16)] * (halves * (width - 1))
        + [jax.ShapeDtypeStruct((rows, rank), BF16)],
        in_specs=[VMEM] * (5 + width + parts),
        out_specs=[VMEM] * (halves * (width - 1) + 1),
        scratch_shapes=[pltpu.VMEM((owners * cols, rank), BF16)],
        compiler_params=params(),
        cost_estimate=cost(2 * rows * (owners * cols * rank + rank * out_block), rows * out_block * 10),
        name="far",
    )(mask, hidden, got_hidden, packed, got_packed, *gots[::-1], far_keep, *far_got)
    core_out = outs[-1]
    far_gots = [along_x(outs[i], i // halves + 1) for i in range(halves * (width - 1))]

    near_got = [pair(a) for a in ordered(near_send, core_out)]
    near = pl.pallas_call(
        near_kernel,
        out_shape=jax.ShapeDtypeStruct((rows, out_block), F32),
        in_specs=[VMEM] * (3 + parts),
        out_specs=VMEM,
        compiler_params=params(),
        cost_estimate=cost(2 * rows * rank * out_block, rows * out_block * 12),
        name="near",
    )(up_basis, near_keep, core_out, *near_got)

    return pl.pallas_call(
        functools.partial(final_kernel, halves),
        out_shape=jax.ShapeDtypeStruct((rows, out_block), BF16),
        in_specs=[VMEM] * (1 + len(far_gots)),
        out_specs=VMEM,
        compiler_params=params(),
        cost_estimate=cost(0, rows * out_block * 8),
        name="final",
    )(near, *far_gots)


def solution(mesh):
    in_specs = (
        P(("group", "dp"), "tensor"),
        P("tensor", None),
        P("tensor", None),
        P(None, "tensor"),
        P("dp", "tensor", None),
        P("group"),
        P("group"),
        P("group"),
    )
    out_specs = P(("group", "dp"), "tensor")
    return jax.shard_map(local, mesh=mesh, in_specs=in_specs, out_specs=out_specs, check_vma=False)
```

time: 32.6 us -> 30.8 us (0.945)
  starting transfers between devices: 11.4 us -> 9.56 us
  waiting for transfers between devices: 8.81 us -> 9.66 us
  Pallas kernels: 8.01 us -> 7.37 us
    ppermute x3 -> x6, waiting for transfers between devices: 0.12 us -> 2.11 us  [pair(): return lax.ppermute(a, 'tensor', [(i, i ^ 1) for i in range(tensor)])]
    ppermute x3 -> x2, starting transfers between devices: 5.04 us -> 3.62 us  [along_x(): lax.ppermute(a, 'tensor', [(i, (i + shift * CORES) % tensor) for i in ran...]
    ppermute x3, starting transfers between devices: 5.57 us -> 4.23 us  [along_dp(): return lax.ppermute(a, 'dp', [(i, i ^ shift) for i in range(owners)])]
    ppermute x3, waiting for transfers between devices: 1 us -> 0.01 us  [along_dp(): return lax.ppermute(a, 'dp', [(i, i ^ shift) for i in range(owners)])]
    slice x1 -> x0, local copies, waits for them, and re-layouts: 0.97 us -> none  [local(): up_parts = [up_basis[:, at:at + cols] for at in range(0, out_block, cols)]]
    unnamed x14 -> x15, local copies, waits for them, and re-layouts: 0.33 us -> 1.25 us
    ppermute x3 -> x6, starting transfers between devices: 0.83 us -> 1.71 us  [pair(): return lax.ppermute(a, 'tensor', [(i, i ^ 1) for i in range(tensor)])]
    pallas_call x1, Pallas kernels: 2.71 us -> 2.03 us  [local(): pl.pallas_call(functools.partial(pick_kernel, (owners, req_dev, per_owner...]
  transfers between devices with their start and end apart: 9 -> 11, of which waited for: 4 -> 4; matrix products, arithmetic and copies ran while one was open for 0% -> 0% of each run, Pallas kernels for 19% -> 19%
where the time goes in v3:
time: 30.8 us; the launch traced here: 30.6 us
  waiting for transfers between devices  9.66 us (31%)
  starting transfers between devices  9.56 us (31%)
  Pallas kernels  7.37 us (24%)
  matrix products  2.58 us (8%)
  local copies, waits for them, and re-layouts  1.25 us (4%)
    ppermute x2, waiting for transfers between devices, along_x(): lax.ppermute(a, 'tensor', [(i, (i + shift * CORES) % tensor) for i in ran...  7.54 us
    ppermute x3, starting transfers between devices, along_dp(): return lax.ppermute(a, 'dp', [(i, i ^ shift) for i in range(owners)])  4.23 us
    ppermute x2, starting transfers between devices, along_x(): lax.ppermute(a, 'tensor', [(i, (i + shift * CORES) % tensor) for i in ran...  3.62 us
    pallas_call x2, Pallas kernels, base(): pl.pallas_call(kernel, out_shape=shapes, in_specs=[VMEM] * 3, out_specs=[...  3.58 us
    dot_general x1, matrix products, local(): part = jnp.dot(tokens, down_basis, preferred_element_type=F32)  2.58 us
    ppermute x6, waiting for transfers between devices, pair(): return lax.ppermute(a, 'tensor', [(i, i ^ 1) for i in range(tensor)])  2.11 us
    pallas_call x1, Pallas kernels, local(): pl.pallas_call(functools.partial(pick_kernel, (owners, req_dev, per_owner...  2.03 us
    ppermute x6, starting transfers between devices, pair(): return lax.ppermute(a, 'tensor', [(i, i ^ 1) for i in range(tensor)])  1.71 us
  transfers between devices with their start and end apart: 11, of which 4 were waited for; matrix products, arithmetic and copies ran while one was open for 0% of the time, Pallas kernels for 19%

profile of v3, /device:TPU:0, one launch (start us, length us, event | category | flops | bytes accessed | tf_op | source)
XLA Modules:
  0.0 30.6 jit_solution(1772835203724836175)
XLA Ops:
  0.0 0.0 copy-start
  0.0 0.0 copy-start.3
  0.0 0.0 copy-start.4
  0.0 0.0 copy-start.6
  0.0 0.0 copy-start.5
  0.0 1.2 %copy-done = bf16[2048,256]{1,0:T(8,128)(2,1)S(1)} copy-done((bf16[2048,256]{1,0:T(8,128)(2,1)S(1)}, bf16[2048,256]{1,0:T(8,128)(2,1)}, u32[]{:S(2)}) %copy-start) | copy-done | bytes 1048600
  1.2 2.6 %fusion.part = f32[640,256]{1,0:T(8,128)S(1)} fusion(bf16[640,2048]{1,0:T(8,128)(2,1)} %tokens.3, bf16[2048,256]{1,0:T(8,128)(2,1)S(1)} %copy-done), kind=kOutput, calls=%fused_computation | convolution fusion | flops 671088640 | bytes 4325376 | tf_op jit(solution)/shard_map/dot_general | solution.py:215
  3.8 0.0 copy-done.3
  3.8 0.1 split.1
  3.9 3.0 %collective-permute-start = (bf16[1152,128]{1,0:T(8,128)(2,1)S(1)}, bf16[1152,128]{1,0:T(8,128)(2,1)S(1)}, u32[]{:S(2)}, u32[]{:S(2)}) collective-permute-start(bf16[1152,128]{1,0:T(8,128)(2,1)S(1)} %get-tuple-element.30), channel_id=1, source_target_pairs={{0,2},{1,3},{2,0},{3,1},{4,6},{5,7},{6,4},{7,5},{8,10},{9,11},{10,... | collective-permute-start | bytes 884744 | tf_op jit(solution)/shard_map/ppermute | solution.py:208
  6.9 0.0 copy-done.4
  6.9 0.0 copy-done.6
  6.9 0.0 copy-done.5
  6.9 0.0 copy-start.1
  7.0 0.0 copy-start.2
  7.0 2.0 %pick.1 = (bf16[64,256]{1,0:T(8,128)(2,1)S(1)}, bf16[64,256]{1,0:T(8,128)(2,1)S(1)}, bf16[64,256]{1,0:T(8,128)(2,1)S(1)}, bf16[64,256]{1,0:T(8,128)(2,1)S(1)}, s32[8,128]{1,0:T(8,128)S(1)}) custom-call(s32[16]{0:T(128)S(1)} %copy-done.5, s32[16]{0:T(128)S(1)} %copy-done.6, s32[2048]{0:T(1024)S(1)} %copy-done.4, bf16[512,64,256]{2,1,0:T(8,128)(2,1)} %bank.1, ...), custom_call_target="tpu_custom_call" | custom-call | bytes 2097152 | tf_op jit(solution)/shard_map/pick/pallas_call | solution.py:229
  9.0 2.7 %collective-permute-start.2 = (bf16[64,256]{1,0:T(8,128)(2,1)S(1)}, bf16[64,256]{1,0:T(8,128)(2,1)S(1)}, u32[]{:S(2)}, u32[]{:S(2)}) collective-permute-start(bf16[64,256]{1,0:T(8,128)(2,1)S(1)} %get-tuple-element.42), channel_id=1, source_target_pairs={{0,8},{4,12},{8,0},{12,4},{1,9},{5,13},{9,1},{13,5},{2,10},{6,14},... | collective-permute-start | bytes 98312 | tf_op jit(solution)/shard_map/ppermute | solution.py:213
  11.7 1.3 %collective-permute-start.3 = (bf16[64,256]{1,0:T(8,128)(2,1)S(1)}, bf16[64,256]{1,0:T(8,128)(2,1)S(1)}, u32[]{:S(2)}, u32[]{:S(2)}) collective-permute-start(bf16[64,256]{1,0:T(8,128)(2,1)S(1)} %get-tuple-element.43), channel_id=1, source_target_pairs={{0,12},{4,8},{8,4},{12,0},{1,13},{5,9},{9,5},{13,1},{2,14},{6,10},... | collective-permute-start | bytes 98312 | tf_op jit(solution)/shard_map/ppermute | solution.py:213
  13.0 0.2 collective-permute-start.4
  13.3 0.0 copy-done.1
  13.3 0.0 copy-done.2
  13.3 2.0 %far_base.1 = (f32[1,640,256]{2,1,0:T(8,128)S(1)}, bf16[640,512]{1,0:T(8,128)(2,1)S(1)}, bf16[1,320,256]{2,1,0:T(8,128)(2,1)S(1)}, bf16[1,320,256]{2,1,0:T(8,128)(2,1)S(1)}) custom-call(bf16[640,2048]{1,0:T(8,128)(2,1)S(1)} %copy-done.2, bf16[2048,1024]{1,0:T(8,128)(2,1)S(1)} %copy-done.1, s32[8,128]{1,0:T(8,128)S(1)} %ordered.5.table), custom_call_target="tpu_custom_call" | custom-call | flops 1342177280 | bytes 4718592 | tf_op jit(solution)/shard_map/far_base/pallas_call | solution.py:264
  15.3 0.1 collective-permute-start.6
  15.4 0.0 collective-permute-done.rest_0_
  15.4 0.5 %collective-permute-start.7 = (bf16[1,320,256]{2,1,0:T(8,128)(2,1)S(1)}, bf16[1,320,256]{2,1,0:T(8,128)(2,1)S(1)}, u32[]{:S(2)}, u32[]{:S(2)}) collective-permute-start(bf16[1,320,256]{2,1,0:T(8,128)(2,1)S(1)} %get-tuple-element.46), channel_id=1, source_target_pairs={{0,1},{1,0},{2,3},{3,2},{4,5},{5,4},{6,7},{7,6},{8,9},{9,8},{10,11... | collective-permute-start | bytes 491528 | tf_op jit(solution)/shard_map/ppermute | solution.py:205
  16.0 0.0 collective-permute-done.2.refs_1_
  16.0 0.2 collective-permute-start.1
  16.1 1.5 %near_base.1 = (f32[640,256]{1,0:T(8,128)S(1)}, bf16[320,256]{1,0:T(8,128)(2,1)S(1)}, bf16[320,256]{1,0:T(8,128)(2,1)S(1)}) custom-call(bf16[640,2048]{1,0:T(8,128)(2,1)S(1)} %copy-done.2, bf16[2048,1024]{1,0:T(8,128)(2,1)S(1)} %copy-done.1, f32[640,128]{1,0:T(8,128)S(1)} %ordered.6.after), custom_call_target="tpu_custom_call" | custom-call | flops 1342177280 | bytes 4718592 | tf_op jit(solution)/shard_map/near_base/pallas_call | solution.py:264
  17.7 0.0 collective-permute-done.3.refs_2_
  17.7 0.0 collective-permute-done.4.refs_3_
  17.7 0.5 %collective-permute-start.5 = (bf16[4,64,256]{2,1,0:T(8,128)(2,1)S(1)}, bf16[4,64,256]{2,1,0:T(8,128)(2,1)S(1)}, u32[]{:S(2)}, u32[]{:S(2)}) collective-permute-start(bf16[4,64,256]{2,1,0:T(8,128)(2,1)S(1)} %pack.1.mine), channel_id=1, source_target_pairs={{0,1},{1,0},{2,3},{3,2},{4,5},{5,4},{6,7},{7,6},{8,9},{9,8},{10,11... | collective-permute-start | bytes 393224 | tf_op jit(solution)/shard_map/ppermute | solution.py:205
  18.2 0.0 collective-permute-done.6.rest_2_
  18.2 0.0 collective-permute-done.7.rest_3_
  18.2 1.0 %collective-permute-done.5.others = bf16[4,64,256]{2,1,0:T(8,128)(2,1)S(1)} collective-permute-done((bf16[4,64,256]{2,1,0:T(8,128)(2,1)S(1)}, bf16[4,64,256]{2,1,0:T(8,128)(2,1)S(1)}, u32[]{:S(2)}, u32[]{:S(2)}) %collective-permute-start.5) | collective-permute-done | bytes 131104 | tf_op jit(solution)/shard_map/ppermute | solution.py:205
  19.2 0.0 collective-permute-done.1.got_hidden
  19.2 0.6 %far.1 = (bf16[640,256]{1,0:T(8,128)(2,1)S(1)}, bf16[640,256]{1,0:T(8,128)(2,1)S(1)}) custom-call(bf16[640,512]{1,0:T(8,128)(2,1)S(1)} %get-tuple-element.40.mask, f32[640,128]{1,0:T(8,128)S(1)} %get-tuple-element.31.hidden, bf16[640,128]{1,0:T(8,128)(2,1)S(1)} %collective-permute-done.1.got_hidden, bf16[4,64,256]{2,1,0:T(8,128)(2,1)S(1)} %pack.1.mine, ...), custom_call_target="tpu_custom_call" | custom-call | flops 251658240 | bytes 1638400 | tf_op jit(solution)/shard_map/far/pallas_call | solution.py:310
  19.8 0.6 %collective-permute-start.10 = (bf16[640,256]{1,0:T(8,128)(2,1)S(1)}, bf16[640,256]{1,0:T(8,128)(2,1)S(1)}, u32[]{:S(2)}, u32[]{:S(2)}) collective-permute-start(bf16[640,256]{1,0:T(8,128)(2,1)S(1)} %get-tuple-element.52), channel_id=1, source_target_pairs={{0,2},{1,3},{2,0},{3,1},{4,6},{5,7},{6,4},{7,5},{8,10},{9,11},{10,... | collective-permute-start | bytes 983048 | tf_op jit(solution)/shard_map/ppermute | solution.py:208
  20.4 0.1 collective-permute-start.8
  20.5 0.4 %collective-permute-start.9 = (bf16[320,256]{1,0:T(8,128)(2,1)S(1)}, bf16[320,256]{1,0:T(8,128)(2,1)S(1)}, u32[]{:S(2)}, u32[]{:S(2)}) collective-permute-start(bf16[320,256]{1,0:T(8,128)(2,1)S(1)} %get-tuple-element.51), channel_id=1, source_target_pairs={{0,1},{1,0},{2,3},{3,2},{4,5},{5,4},{6,7},{7,6},{8,9},{9,8},{10,11... | collective-permute-start | bytes 491528 | tf_op jit(solution)/shard_map/ppermute | solution.py:205
  20.9 0.9 %collective-permute-done.8.rest_0_ = bf16[320,256]{1,0:T(8,128)(2,1)S(1)} collective-permute-done((bf16[320,256]{1,0:T(8,128)(2,1)S(1)}, bf16[320,256]{1,0:T(8,128)(2,1)S(1)}, u32[]{:S(2)}, u32[]{:S(2)}) %collective-permute-start.8) | collective-permute-done | bytes 163872 | tf_op jit(solution)/shard_map/ppermute | solution.py:205
  21.8 0.2 collective-permute-done.9.rest_1_
  22.0 0.2 near.1
  22.3 7.5 %collective-permute-done.10.rest_0_ = bf16[640,256]{1,0:T(8,128)(2,1)S(1)} collective-permute-done((bf16[640,256]{1,0:T(8,128)(2,1)S(1)}, bf16[640,256]{1,0:T(8,128)(2,1)S(1)}, u32[]{:S(2)}, u32[]{:S(2)}) %collective-permute-start.10) | collective-permute-done | bytes 327712 | tf_op jit(solution)/shard_map/ppermute | solution.py:208
  29.8 0.8 %final.1 = bf16[640,256]{1,0:T(8,128)(2,1)} custom-call(f32[640,256]{1,0:T(8,128)S(1)} %near.1, bf16[640,256]{1,0:T(8,128)(2,1)S(1)} %collective-permute-done.10.rest_0_), custom_call_target="tpu_custom_call" | custom-call | bytes 1310720 | tf_op jit(solution)/shard_map/final/pallas_call | solution.py:335
  (7 shorter events, 0.1 us)
Async XLA Ops:
  0.0 1.2 %copy-start = (bf16[2048,256]{1,0:T(8,128)(2,1)S(1)}, bf16[2048,256]{1,0:T(8,128)(2,1)}, u32[]{:S(2)}) copy-start(bf16[2048,256]{1,0:T(8,128)(2,1)} %param.10) | copy-start | bytes 3145732
  0.0 3.8 %copy-start.3 = (bf16[256,256]{1,0:T(8,128)(2,1)S(1)}, bf16[256,256]{1,0:T(8,128)(2,1)}, u32[]{:S(2)}) copy-start(bf16[256,256]{1,0:T(8,128)(2,1)} %up.3) | copy-start | bytes 393220
  0.0 6.9 %copy-start.4 = (s32[2048]{0:T(1024)S(1)}, s32[2048]{0:T(1024)}, u32[]{:S(2)}) copy-start(s32[2048]{0:T(1024)} %slots.1) | copy-start | bytes 24580
  0.0 6.9 %copy-start.6 = (s32[16]{0:T(128)S(1)}, s32[16]{0:T(128)}, u32[]{:S(2)}) copy-start(s32[16]{0:T(128)} %lengths.1) | copy-start | bytes 196
  0.0 6.9 %copy-start.5 = (s32[16]{0:T(128)S(1)}, s32[16]{0:T(128)}, u32[]{:S(2)}) copy-start(s32[16]{0:T(128)} %adapters.1) | copy-start | bytes 196
  3.9 11.5 %collective-permute-start = (bf16[1152,128]{1,0:T(8,128)(2,1)S(1)}, bf16[1152,128]{1,0:T(8,128)(2,1)S(1)}, u32[]{:S(2)}, u32[]{:S(2)}) collective-permute-start(bf16[1152,128]{1,0:T(8,128)(2,1)S(1)} %get-tuple-element.30), channel_id=1, source_target_pairs={{0,2},{1,3},{2,0},{3,1},{4,6},{5,7},{6,4},{7,5},{8,10},{9,11},{10,... | collective-permute-start | bytes 884744 | tf_op jit(solution)/shard_map/ppermute | solution.py:208
  6.9 6.3 %copy-start.1 = (bf16[2048,1024]{1,0:T(8,128)(2,1)S(1)}, bf16[2048,1024]{1,0:T(8,128)(2,1)}, u32[]{:S(2)}) copy-start(bf16[2048,1024]{1,0:T(8,128)(2,1)} %weight.3) | copy-start | bytes 12582916
  7.0 6.3 %copy-start.2 = (bf16[640,2048]{1,0:T(8,128)(2,1)S(1)}, bf16[640,2048]{1,0:T(8,128)(2,1)}, u32[]{:S(2)}) copy-start(bf16[640,2048]{1,0:T(8,128)(2,1)} %tokens.3) | copy-start | bytes 7864324
  9.0 7.0 %collective-permute-start.2 = (bf16[64,256]{1,0:T(8,128)(2,1)S(1)}, bf16[64,256]{1,0:T(8,128)(2,1)S(1)}, u32[]{:S(2)}, u32[]{:S(2)}) collective-permute-start(bf16[64,256]{1,0:T(8,128)(2,1)S(1)} %get-tuple-element.42), channel_id=1, source_target_pairs={{0,8},{4,12},{8,0},{12,4},{1,9},{5,13},{9,1},{13,5},{2,10},{6,14},... | collective-permute-start | bytes 98312 | tf_op jit(solution)/shard_map/ppermute | solution.py:213
  11.7 6.0 %collective-permute-start.3 = (bf16[64,256]{1,0:T(8,128)(2,1)S(1)}, bf16[64,256]{1,0:T(8,128)(2,1)S(1)}, u32[]{:S(2)}, u32[]{:S(2)}) collective-permute-start(bf16[64,256]{1,0:T(8,128)(2,1)S(1)} %get-tuple-element.43), channel_id=1, source_target_pairs={{0,12},{4,8},{8,4},{12,0},{1,13},{5,9},{9,5},{13,1},{2,14},{6,10},... | collective-permute-start | bytes 98312 | tf_op jit(solution)/shard_map/ppermute | solution.py:213
  13.0 4.7 %collective-permute-start.4 = (bf16[64,256]{1,0:T(8,128)(2,1)S(1)}, bf16[64,256]{1,0:T(8,128)(2,1)S(1)}, u32[]{:S(2)}, u32[]{:S(2)}) collective-permute-start(bf16[64,256]{1,0:T(8,128)(2,1)S(1)} %get-tuple-element.44), channel_id=1, source_target_pairs={{0,4},{4,0},{8,12},{12,8},{1,5},{5,1},{9,13},{13,9},{2,6},{6,2},{1... | collective-permute-start | bytes 98312 | tf_op jit(solution)/shard_map/ppermute | solution.py:213
  15.3 2.9 %collective-permute-start.6 = (bf16[1,320,256]{2,1,0:T(8,128)(2,1)S(1)}, bf16[1,320,256]{2,1,0:T(8,128)(2,1)S(1)}, u32[]{:S(2)}, u32[]{:S(2)}) collective-permute-start(bf16[1,320,256]{2,1,0:T(8,128)(2,1)S(1)} %get-tuple-element.45), channel_id=1, source_target_pairs={{0,1},{1,0},{2,3},{3,2},{4,5},{5,4},{6,7},{7,6},{8,9},{9,8},{10,11... | collective-permute-start | bytes 491528 | tf_op jit(solution)/shard_map/ppermute | solution.py:205
  15.4 2.8 %collective-permute-start.7 = (bf16[1,320,256]{2,1,0:T(8,128)(2,1)S(1)}, bf16[1,320,256]{2,1,0:T(8,128)(2,1)S(1)}, u32[]{:S(2)}, u32[]{:S(2)}) collective-permute-start(bf16[1,320,256]{2,1,0:T(8,128)(2,1)S(1)} %get-tuple-element.46), channel_id=1, source_target_pairs={{0,1},{1,0},{2,3},{3,2},{4,5},{5,4},{6,7},{7,6},{8,9},{9,8},{10,11... | collective-permute-start | bytes 491528 | tf_op jit(solution)/shard_map/ppermute | solution.py:205
  16.0 3.2 %collective-permute-start.1 = (bf16[640,128]{1,0:T(8,128)(2,1)S(1)}, bf16[640,128]{1,0:T(8,128)(2,1)S(1)}, u32[]{:S(2)}, u32[]{:S(2)}) collective-permute-start(bf16[640,128]{1,0:T(8,128)(2,1)S(1)} %get-tuple-element.41), channel_id=1, source_target_pairs={{0,1},{1,0},{2,3},{3,2},{4,5},{5,4},{6,7},{7,6},{8,9},{9,8},{10,11... | collective-permute-start | bytes 491528 | tf_op jit(solution)/shard_map/ppermute | solution.py:205
  17.7 1.5 %collective-permute-start.5 = (bf16[4,64,256]{2,1,0:T(8,128)(2,1)S(1)}, bf16[4,64,256]{2,1,0:T(8,128)(2,1)S(1)}, u32[]{:S(2)}, u32[]{:S(2)}) collective-permute-start(bf16[4,64,256]{2,1,0:T(8,128)(2,1)S(1)} %pack.1.mine), channel_id=1, source_target_pairs={{0,1},{1,0},{2,3},{3,2},{4,5},{5,4},{6,7},{7,6},{8,9},{9,8},{10,11... | collective-permute-start | bytes 393224 | tf_op jit(solution)/shard_map/ppermute | solution.py:205
  19.8 10.0 %collective-permute-start.10 = (bf16[640,256]{1,0:T(8,128)(2,1)S(1)}, bf16[640,256]{1,0:T(8,128)(2,1)S(1)}, u32[]{:S(2)}, u32[]{:S(2)}) collective-permute-start(bf16[640,256]{1,0:T(8,128)(2,1)S(1)} %get-tuple-element.52), channel_id=1, source_target_pairs={{0,2},{1,3},{2,0},{3,1},{4,6},{5,7},{6,4},{7,5},{8,10},{9,11},{10,... | collective-permute-start | bytes 983048 | tf_op jit(solution)/shard_map/ppermute | solution.py:208
  20.4 1.4 %collective-permute-start.8 = (bf16[320,256]{1,0:T(8,128)(2,1)S(1)}, bf16[320,256]{1,0:T(8,128)(2,1)S(1)}, u32[]{:S(2)}, u32[]{:S(2)}) collective-permute-start(bf16[320,256]{1,0:T(8,128)(2,1)S(1)} %get-tuple-element.50), channel_id=1, source_target_pairs={{0,1},{1,0},{2,3},{3,2},{4,5},{5,4},{6,7},{7,6},{8,9},{9,8},{10,11... | collective-permute-start | bytes 491528 | tf_op jit(solution)/shard_map/ppermute | solution.py:205
  20.5 1.6 %collective-permute-start.9 = (bf16[320,256]{1,0:T(8,128)(2,1)S(1)}, bf16[320,256]{1,0:T(8,128)(2,1)S(1)}, u32[]{:S(2)}, u32[]{:S(2)}) collective-permute-start(bf16[320,256]{1,0:T(8,128)(2,1)S(1)} %get-tuple-element.51), channel_id=1, source_target_pairs={{0,1},{1,0},{2,3},{3,2},{4,5},{5,4},{6,7},{7,6},{8,9},{9,8},{10,11... | collective-permute-start | bytes 491528 | tf_op jit(solution)/shard_map/ppermute | solution.py:205

commit v4 on v3

--- a/solution.py
+++ b/solution.py
@@ -1,5 +1,4 @@
 import functools
-import math
 
 import jax
 import jax.numpy as jnp
@@ -121,12 +120,7 @@
     return jnp.dot(tokens[...], weight[:, columns], preferred_element_type=F32)
 
 
-def far_base_kernel(width, owners, tokens, weight, table, keep, mask, *sends):
-    rows, cols = tokens.shape[0], mask.shape[1] // owners
-    row = lax.broadcasted_iota(jnp.int32, (rows, cols), 0)
-    for s in range(owners):
-        inside = (row >= table[s : s + 1, 0:1]) & (row < table[s : s + 1, 1:2])
-        mask[:, s * cols : (s + 1) * cols] = jnp.where(inside, 1.0, 0.0).astype(BF16)
+def far_base_kernel(width, tokens, weight, after, keep, *sends):
     size = sends[0].shape[1]
     for shift in range(1, width):
         other = block_product(width, shift, 1, tokens, weight).astype(BF16)
@@ -135,11 +129,19 @@
         keep[shift - 1] = block_product(width, shift, 0, tokens, weight)
 
 
-def near_base_kernel(width, tokens, weight, after, keep, *sends):
+def near_send_kernel(width, owners, tokens, weight, table, after, mask, *sends):
+    rows, cols = tokens.shape[0], mask.shape[1] // owners
+    row = lax.broadcasted_iota(jnp.int32, (rows, cols), 0)
+    for s in range(owners):
+        inside = (row >= table[s : s + 1, 0:1]) & (row < table[s : s + 1, 1:2])
+        mask[:, s * cols : (s + 1) * cols] = jnp.where(inside, 1.0, 0.0).astype(BF16)
     other = block_product(width, 0, 1, tokens, weight).astype(BF16)
     size = sends[0].shape[0]
     for i, send in enumerate(sends):
         send[...] = other[i * size : (i + 1) * size]
+
+
+def near_keep_kernel(width, tokens, weight, after, keep):
     keep[...] = block_product(width, 0, 0, tokens, weight)
 
 
@@ -259,38 +261,35 @@
     )(keep, *gots)
     got_hidden = pair(hidden_send)
 
-    def base(kernel, shapes, after, name):
-        blocks = math.prod(shapes[0].shape[:-2]) * CORES
+    def base(kernel, shapes, after, name, blocks):
         return pl.pallas_call(
             kernel,
             out_shape=shapes,
-            in_specs=[VMEM] * 3,
+            in_specs=[VMEM] * (1 + len(after)) + [ANY],
             out_specs=[VMEM] * len(shapes),
             compiler_params=params(),
             cost_estimate=cost(
                 2 * rows * depth * out_block * blocks, 2 * depth * (rows + out_block * blocks)
             ),
             name=name,
-        )(tokens, base_weight, after)
+        )(tokens, base_weight, *after)
 
     parts = 2
-    far_keep, mask, *far_send = base(
-        functools.partial(far_base_kernel, width, owners),
-        [
-            jax.ShapeDtypeStruct((width - 1, rows, out_block), F32),
-            jax.ShapeDtypeStruct((rows, owners * cols), BF16),
-        ]
+    far_keep, *far_send = base(
+        functools.partial(far_base_kernel, width),
+        [jax.ShapeDtypeStruct((width - 1, rows, out_block), F32)]
         + [jax.ShapeDtypeStruct((width - 1, rows // parts, out_block), BF16)] * parts,
-        ordered([table], picks[0])[0],
+        [picks[0]],
         "far_base",
+        CORES * (width - 1),
     )
-
-    near_keep, *near_send = base(
-        functools.partial(near_base_kernel, width),
-        [jax.ShapeDtypeStruct((rows, out_block), F32)]
+    mask, *near_send = base(
+        functools.partial(near_send_kernel, width, owners),
+        [jax.ShapeDtypeStruct((rows, owners * cols), BF16)]
         + [jax.ShapeDtypeStruct((rows // parts, out_block), BF16)] * parts,
-        ordered([hidden], far_keep)[0],
-        "near_base",
+        [table, ordered([hidden], far_keep, down_basis)[0]],
+        "near_send",
+        1,
     )
 
     packed = pl.pallas_call(
@@ -301,7 +300,7 @@
         compiler_params=params(),
         cost_estimate=cost(0, 0),
         name="pack",
-    )(*mine, near_keep)
+    )(*mine, mask)
     got_packed = pair(packed)
     far_got = [pair(a) for a in far_send]
 
@@ -322,6 +321,13 @@
     far_gots = [along_x(outs[i], i // halves + 1) for i in range(halves * (width - 1))]
 
     near_got = [pair(a) for a in ordered(near_send, core_out)]
+    (near_keep,) = base(
+        functools.partial(near_keep_kernel, width),
+        [jax.ShapeDtypeStruct((rows, out_block), F32)],
+        [core_out],
+        "near_keep",
+        1,
+    )
     near = pl.pallas_call(
         near_kernel,
         out_shape=jax.ShapeDtypeStruct((rows, out_block), F32),

time: 30.8 us -> 29.2 us (0.948)
  local copies, waits for them, and re-layouts: 1.25 us -> 0.05 us
  waiting for transfers between devices: 9.66 us -> 9.18 us
  starting transfers between devices: 9.56 us -> 9.23 us
  matrix products: 2.58 us -> 2.89 us
    unnamed x15, local copies, waits for them, and re-layouts: 1.25 us -> 0.05 us
    ppermute x6, waiting for transfers between devices: 2.11 us -> 1.49 us  [pair(): return lax.ppermute(a, 'tensor', [(i, i ^ 1) for i in range(tensor)])]
    ppermute x3, waiting for transfers between devices: 0.01 us -> 0.34 us  [along_dp(): return lax.ppermute(a, 'dp', [(i, i ^ shift) for i in range(owners)])]
    ppermute x6, starting transfers between devices: 1.71 us -> 1.38 us  [pair(): return lax.ppermute(a, 'tensor', [(i, i ^ 1) for i in range(tensor)])]
    dot_general x1, matrix products: 2.58 us -> 2.89 us  [local(): part = jnp.dot(tokens, down_basis, preferred_element_type=F32)]
    pallas_call x2 -> x3, Pallas kernels: 3.58 us -> 3.8 us  [base(): pl.pallas_call(kernel, out_shape=shapes, in_specs=[VMEM] * (1 + len(after...]
  transfers between devices with their start and end apart: 11 -> 11, of which waited for: 4 -> 4; matrix products, arithmetic and copies ran while one was open for 0% -> 0% of each run, Pallas kernels for 19% -> 21%
where the time goes in v4:
time: 29.2 us; the launch traced here: 29.1 us
  starting transfers between devices  9.23 us (32%)
  waiting for transfers between devices  9.18 us (31%)
  Pallas kernels  7.59 us (26%)
  matrix products  2.89 us (10%)
    ppermute x2, waiting for transfers between devices, along_x(): lax.ppermute(a, 'tensor', [(i, (i + shift * CORES) % tensor) for i in ran...  7.35 us
    ppermute x3, starting transfers between devices, along_dp(): return lax.ppermute(a, 'dp', [(i, i ^ shift) for i in range(owners)])  4.23 us
    pallas_call x3, Pallas kernels, base(): pl.pallas_call(kernel, out_shape=shapes, in_specs=[VMEM] * (1 + len(after...  3.8 us
    ppermute x2, starting transfers between devices, along_x(): lax.ppermute(a, 'tensor', [(i, (i + shift * CORES) % tensor) for i in ran...  3.62 us
    dot_general x1, matrix products, local(): part = jnp.dot(tokens, down_basis, preferred_element_type=F32)  2.89 us
    pallas_call x1, Pallas kernels, local(): pl.pallas_call(functools.partial(pick_kernel, (owners, req_dev, per_owner...  2.03 us
    ppermute x6, waiting for transfers between devices, pair(): return lax.ppermute(a, 'tensor', [(i, i ^ 1) for i in range(tensor)])  1.49 us
    ppermute x6, starting transfers between devices, pair(): return lax.ppermute(a, 'tensor', [(i, i ^ 1) for i in range(tensor)])  1.38 us
  transfers between devices with their start and end apart: 11, of which 4 were waited for; matrix products, arithmetic and copies ran while one was open for 0% of the time, Pallas kernels for 21%

profile of v4, /device:TPU:0, one launch (start us, length us, event | category | flops | bytes accessed | tf_op | source)
XLA Modules:
  0.0 29.1 jit_solution(5809268401906929178)
XLA Ops:
  0.0 0.0 copy-start.3
  0.0 0.0 copy-start.4
  0.0 0.0 copy-start.6
  0.0 0.0 copy-start.5
  0.0 2.9 %fusion.part = f32[640,256]{1,0:T(8,128)S(1)} fusion(bf16[640,2048]{1,0:T(8,128)(2,1)} %tokens.5, bf16[2048,256]{1,0:T(8,128)(2,1)} %refs_2_.1), kind=kOutput, calls=%fused_computation | convolution fusion | flops 671088640 | bytes 4325376 | tf_op jit(solution)/shard_map/dot_general | solution.py:217
  2.9 0.0 copy-done.3
  2.9 0.1 split.1
  3.0 3.0 %collective-permute-start = (bf16[1152,128]{1,0:T(8,128)(2,1)S(1)}, bf16[1152,128]{1,0:T(8,128)(2,1)S(1)}, u32[]{:S(2)}, u32[]{:S(2)}) collective-permute-start(bf16[1152,128]{1,0:T(8,128)(2,1)S(1)} %get-tuple-element.30), channel_id=1, source_target_pairs={{0,2},{1,3},{2,0},{3,1},{4,6},{5,7},{6,4},{7,5},{8,10},{9,11},{10,... | collective-permute-start | bytes 884744 | tf_op jit(solution)/shard_map/ppermute | solution.py:210
  6.0 0.0 copy-done.4
  6.0 0.0 copy-done.6
  6.0 0.0 copy-done.5
  6.1 0.0 copy-start
  6.1 0.0 copy-start.1
  6.1 2.0 %pick.1 = (bf16[64,256]{1,0:T(8,128)(2,1)S(1)}, bf16[64,256]{1,0:T(8,128)(2,1)S(1)}, bf16[64,256]{1,0:T(8,128)(2,1)S(1)}, bf16[64,256]{1,0:T(8,128)(2,1)S(1)}, s32[8,128]{1,0:T(8,128)S(1)}) custom-call(s32[16]{0:T(128)S(1)} %copy-done.5, s32[16]{0:T(128)S(1)} %copy-done.6, s32[2048]{0:T(1024)S(1)} %copy-done.4, bf16[512,64,256]{2,1,0:T(8,128)(2,1)} %bank.1, ...), custom_call_target="tpu_custom_call" | custom-call | bytes 2097152 | tf_op jit(solution)/shard_map/pick/pallas_call | solution.py:231
  8.1 2.7 %collective-permute-start.2 = (bf16[64,256]{1,0:T(8,128)(2,1)S(1)}, bf16[64,256]{1,0:T(8,128)(2,1)S(1)}, u32[]{:S(2)}, u32[]{:S(2)}) collective-permute-start(bf16[64,256]{1,0:T(8,128)(2,1)S(1)} %get-tuple-element.40), channel_id=1, source_target_pairs={{0,8},{4,12},{8,0},{12,4},{1,9},{5,13},{9,1},{13,5},{2,10},{6,14},... | collective-permute-start | bytes 98312 | tf_op jit(solution)/shard_map/ppermute | solution.py:215
  10.8 1.3 %collective-permute-start.3 = (bf16[64,256]{1,0:T(8,128)(2,1)S(1)}, bf16[64,256]{1,0:T(8,128)(2,1)S(1)}, u32[]{:S(2)}, u32[]{:S(2)}) collective-permute-start(bf16[64,256]{1,0:T(8,128)(2,1)S(1)} %get-tuple-element.41), channel_id=1, source_target_pairs={{0,12},{4,8},{8,4},{12,0},{1,13},{5,9},{9,5},{13,1},{2,14},{6,10},... | collective-permute-start | bytes 98312 | tf_op jit(solution)/shard_map/ppermute | solution.py:215
  12.1 0.2 collective-permute-start.4
  12.4 0.0 copy-done
  12.4 0.0 copy-done.1
  12.4 0.0 copy-start.2
  12.4 1.6 %far_base.1 = (f32[1,640,256]{2,1,0:T(8,128)S(1)}, bf16[1,320,256]{2,1,0:T(8,128)(2,1)S(1)}, bf16[1,320,256]{2,1,0:T(8,128)(2,1)S(1)}) custom-call(bf16[640,2048]{1,0:T(8,128)(2,1)S(1)} %copy-done.1, bf16[2048,1024]{1,0:T(8,128)(2,1)S(1)} %copy-done, bf16[64,256]{1,0:T(8,128)(2,1)S(1)} %get-tuple-element.36.after.refs_0_), custom_call_target="tpu_custom_call" | custom-call | flops 1342177280 | bytes 4718592 | tf_op jit(solution)/shard_map/far_base/pallas_call | solution.py:265
  13.9 0.1 collective-permute-start.6
  14.0 0.0 collective-permute-done.rest_0_
  14.0 0.5 %collective-permute-start.7 = (bf16[1,320,256]{2,1,0:T(8,128)(2,1)S(1)}, bf16[1,320,256]{2,1,0:T(8,128)(2,1)S(1)}, u32[]{:S(2)}, u32[]{:S(2)}) collective-permute-start(bf16[1,320,256]{2,1,0:T(8,128)(2,1)S(1)} %get-tuple-element.44), channel_id=1, source_target_pairs={{0,1},{1,0},{2,3},{3,2},{4,5},{5,4},{6,7},{7,6},{8,9},{9,8},{10,11... | collective-permute-start | bytes 491528 | tf_op jit(solution)/shard_map/ppermute | solution.py:207
  14.6 0.0 copy-done.2
  14.6 0.0 collective-permute-done.2.refs_1_
  14.6 0.2 collective-permute-start.1
  14.8 1.4 %near_send.1 = (bf16[640,512]{1,0:T(8,128)(2,1)S(1)}, bf16[320,256]{1,0:T(8,128)(2,1)S(1)}, bf16[320,256]{1,0:T(8,128)(2,1)S(1)}) custom-call(bf16[640,2048]{1,0:T(8,128)(2,1)S(1)} %copy-done.1, bf16[2048,1024]{1,0:T(8,128)(2,1)S(1)} %copy-done, s32[8,128]{1,0:T(8,128)S(1)} %get-tuple-element.29.table, f32[640,128]{1,0:T(8,128)S(1)} %ordered.4.after), custom_call_target="tpu_custom_call" | custom-call | flops 671088640 | bytes 3670016 | tf_op jit(solution)/shard_map/near_send/pallas_call | solution.py:265
  16.2 0.3 %collective-permute-done.3.refs_2_ = bf16[64,256]{1,0:T(8,128)(2,1)S(1)} collective-permute-done((bf16[64,256]{1,0:T(8,128)(2,1)S(1)}, bf16[64,256]{1,0:T(8,128)(2,1)S(1)}, u32[]{:S(2)}, u32[]{:S(2)}) %collective-permute-start.3) | collective-permute-done | bytes 32800 | tf_op jit(solution)/shard_map/ppermute | solution.py:215
  16.5 0.0 collective-permute-done.4.refs_3_
  16.5 0.2 collective-permute-start.5
  16.7 0.0 collective-permute-done.6.rest_2_
  16.7 0.0 collective-permute-done.7.rest_3_
  16.7 1.2 %collective-permute-done.5.others = bf16[4,64,256]{2,1,0:T(8,128)(2,1)S(1)} collective-permute-done((bf16[4,64,256]{2,1,0:T(8,128)(2,1)S(1)}, bf16[4,64,256]{2,1,0:T(8,128)(2,1)S(1)}, u32[]{:S(2)}, u32[]{:S(2)}) %collective-permute-start.5) | collective-permute-done | bytes 131104 | tf_op jit(solution)/shard_map/ppermute | solution.py:207
  17.9 0.0 collective-permute-done.1.got_hidden
  17.9 0.6 %far.1 = (bf16[640,256]{1,0:T(8,128)(2,1)S(1)}, bf16[640,256]{1,0:T(8,128)(2,1)S(1)}) custom-call(bf16[640,512]{1,0:T(8,128)(2,1)S(1)} %get-tuple-element.38.refs_4_.mask, f32[640,128]{1,0:T(8,128)S(1)} %get-tuple-element.31.hidden, bf16[640,128]{1,0:T(8,128)(2,1)S(1)} %collective-permute-done.1.got_hidden, bf16[4,64,256]{2,1,0:T(8,128)(2,1)S(1)} %pack.1.mine, ...), custom_call_target="tpu_custom_call" | custom-call | flops 251658240 | bytes 1638400 | tf_op jit(solution)/shard_map/far/pallas_call | solution.py:309
  18.5 0.6 %collective-permute-start.10 = (bf16[640,256]{1,0:T(8,128)(2,1)S(1)}, bf16[640,256]{1,0:T(8,128)(2,1)S(1)}, u32[]{:S(2)}, u32[]{:S(2)}) collective-permute-start(bf16[640,256]{1,0:T(8,128)(2,1)S(1)} %get-tuple-element.50), channel_id=1, source_target_pairs={{0,2},{1,3},{2,0},{3,1},{4,6},{5,7},{6,4},{7,5},{8,10},{9,11},{10,... | collective-permute-start | bytes 983048 | tf_op jit(solution)/shard_map/ppermute | solution.py:210
  19.1 0.0 collective-permute-start.8
  19.1 0.5 %collective-permute-start.9 = (bf16[320,256]{1,0:T(8,128)(2,1)S(1)}, bf16[320,256]{1,0:T(8,128)(2,1)S(1)}, u32[]{:S(2)}, u32[]{:S(2)}) collective-permute-start(bf16[320,256]{1,0:T(8,128)(2,1)S(1)} %get-tuple-element.49), channel_id=1, source_target_pairs={{0,1},{1,0},{2,3},{3,2},{4,5},{5,4},{6,7},{7,6},{8,9},{9,8},{10,11... | collective-permute-start | bytes 491528 | tf_op jit(solution)/shard_map/ppermute | solution.py:207
  19.6 0.9 %near_keep.1.keep = f32[640,256]{1,0:T(8,128)S(1)} custom-call(bf16[640,2048]{1,0:T(8,128)(2,1)S(1)} %copy-done.1, bf16[2048,1024]{1,0:T(8,128)(2,1)S(1)} %copy-done, bf16[640,256]{1,0:T(8,128)(2,1)S(1)} %get-tuple-element.45.after.refs_2_.part), custom_call_target="tpu_custom_call" | custom-call | flops 671088640 | bytes 3670016 | tf_op jit(solution)/shard_map/near_keep/pallas_call | solution.py:265
  20.5 0.0 collective-permute-done.8.rest_0_
  20.5 0.2 collective-permute-done.9.rest_1_
  20.7 0.2 near.1
  21.0 7.3 %collective-permute-done.10.rest_0_ = bf16[640,256]{1,0:T(8,128)(2,1)S(1)} collective-permute-done((bf16[640,256]{1,0:T(8,128)(2,1)S(1)}, bf16[640,256]{1,0:T(8,128)(2,1)S(1)}, u32[]{:S(2)}, u32[]{:S(2)}) %collective-permute-start.10) | collective-permute-done | bytes 327712 | tf_op jit(solution)/shard_map/ppermute | solution.py:210
  28.3 0.8 %final.1 = bf16[640,256]{1,0:T(8,128)(2,1)} custom-call(f32[640,256]{1,0:T(8,128)S(1)} %near.1, bf16[640,256]{1,0:T(8,128)(2,1)S(1)} %collective-permute-done.10.rest_0_), custom_call_target="tpu_custom_call" | custom-call | bytes 1310720 | tf_op jit(solution)/shard_map/final/pallas_call | solution.py:341
  (6 shorter events, 0.1 us)
Async XLA Ops:
  0.0 2.9 %copy-start.3 = (bf16[256,256]{1,0:T(8,128)(2,1)S(1)}, bf16[256,256]{1,0:T(8,128)(2,1)}, u32[]{:S(2)}) copy-start(bf16[256,256]{1,0:T(8,128)(2,1)} %up.3) | copy-start | bytes 393220
  0.0 6.0 %copy-start.4 = (s32[2048]{0:T(1024)S(1)}, s32[2048]{0:T(1024)}, u32[]{:S(2)}) copy-start(s32[2048]{0:T(1024)} %slots.1) | copy-start | bytes 24580
  0.0 6.0 %copy-start.6 = (s32[16]{0:T(128)S(1)}, s32[16]{0:T(128)}, u32[]{:S(2)}) copy-start(s32[16]{0:T(128)} %lengths.1) | copy-start | bytes 196
  0.0 6.0 %copy-start.5 = (s32[16]{0:T(128)S(1)}, s32[16]{0:T(128)}, u32[]{:S(2)}) copy-start(s32[16]{0:T(128)} %adapters.1) | copy-start | bytes 196
  3.0 11.0 %collective-permute-start = (bf16[1152,128]{1,0:T(8,128)(2,1)S(1)}, bf16[1152,128]{1,0:T(8,128)(2,1)S(1)}, u32[]{:S(2)}, u32[]{:S(2)}) collective-permute-start(bf16[1152,128]{1,0:T(8,128)(2,1)S(1)} %get-tuple-element.30), channel_id=1, source_target_pairs={{0,2},{1,3},{2,0},{3,1},{4,6},{5,7},{6,4},{7,5},{8,10},{9,11},{10,... | collective-permute-start | bytes 884744 | tf_op jit(solution)/shard_map/ppermute | solution.py:210
  6.1 6.3 %copy-start = (bf16[2048,1024]{1,0:T(8,128)(2,1)S(1)}, bf16[2048,1024]{1,0:T(8,128)(2,1)}, u32[]{:S(2)}) copy-start(bf16[2048,1024]{1,0:T(8,128)(2,1)} %weight.5) | copy-start | bytes 12582916
  6.1 6.3 %copy-start.1 = (bf16[640,2048]{1,0:T(8,128)(2,1)S(1)}, bf16[640,2048]{1,0:T(8,128)(2,1)}, u32[]{:S(2)}) copy-start(bf16[640,2048]{1,0:T(8,128)(2,1)} %tokens.5) | copy-start | bytes 7864324
  8.1 6.5 %collective-permute-start.2 = (bf16[64,256]{1,0:T(8,128)(2,1)S(1)}, bf16[64,256]{1,0:T(8,128)(2,1)S(1)}, u32[]{:S(2)}, u32[]{:S(2)}) collective-permute-start(bf16[64,256]{1,0:T(8,128)(2,1)S(1)} %get-tuple-element.40), channel_id=1, source_target_pairs={{0,8},{4,12},{8,0},{12,4},{1,9},{5,13},{9,1},{13,5},{2,10},{6,14},... | collective-permute-start | bytes 98312 | tf_op jit(solution)/shard_map/ppermute | solution.py:215
  10.8 5.7 %collective-permute-start.3 = (bf16[64,256]{1,0:T(8,128)(2,1)S(1)}, bf16[64,256]{1,0:T(8,128)(2,1)S(1)}, u32[]{:S(2)}, u32[]{:S(2)}) collective-permute-start(bf16[64,256]{1,0:T(8,128)(2,1)S(1)} %get-tuple-element.41), channel_id=1, source_target_pairs={{0,12},{4,8},{8,4},{12,0},{1,13},{5,9},{9,5},{13,1},{2,14},{6,10},... | collective-permute-start | bytes 98312 | tf_op jit(solution)/shard_map/ppermute | solution.py:215
  12.1 4.4 %collective-permute-start.4 = (bf16[64,256]{1,0:T(8,128)(2,1)S(1)}, bf16[64,256]{1,0:T(8,128)(2,1)S(1)}, u32[]{:S(2)}, u32[]{:S(2)}) collective-permute-start(bf16[64,256]{1,0:T(8,128)(2,1)S(1)} %get-tuple-element.42), channel_id=1, source_target_pairs={{0,4},{4,0},{8,12},{12,8},{1,5},{5,1},{9,13},{13,9},{2,6},{6,2},{1... | collective-permute-start | bytes 98312 | tf_op jit(solution)/shard_map/ppermute | solution.py:215
  12.4 2.2 %copy-start.2 = (bf16[2048,256]{1,0:T(8,128)(2,1)S(1)}, bf16[2048,256]{1,0:T(8,128)(2,1)}, u32[]{:S(2)}) copy-start(bf16[2048,256]{1,0:T(8,128)(2,1)} %refs_2_.1) | copy-start | bytes 3145732
  13.9 2.8 %collective-permute-start.6 = (bf16[1,320,256]{2,1,0:T(8,128)(2,1)S(1)}, bf16[1,320,256]{2,1,0:T(8,128)(2,1)S(1)}, u32[]{:S(2)}, u32[]{:S(2)}) collective-permute-start(bf16[1,320,256]{2,1,0:T(8,128)(2,1)S(1)} %get-tuple-element.43), channel_id=1, source_target_pairs={{0,1},{1,0},{2,3},{3,2},{4,5},{5,4},{6,7},{7,6},{8,9},{9,8},{10,11... | collective-permute-start | bytes 491528 | tf_op jit(solution)/shard_map/ppermute | solution.py:207
  14.0 2.7 %collective-permute-start.7 = (bf16[1,320,256]{2,1,0:T(8,128)(2,1)S(1)}, bf16[1,320,256]{2,1,0:T(8,128)(2,1)S(1)}, u32[]{:S(2)}, u32[]{:S(2)}) collective-permute-start(bf16[1,320,256]{2,1,0:T(8,128)(2,1)S(1)} %get-tuple-element.44), channel_id=1, source_target_pairs={{0,1},{1,0},{2,3},{3,2},{4,5},{5,4},{6,7},{7,6},{8,9},{9,8},{10,11... | collective-permute-start | bytes 491528 | tf_op jit(solution)/shard_map/ppermute | solution.py:207
  14.6 3.3 %collective-permute-start.1 = (bf16[640,128]{1,0:T(8,128)(2,1)S(1)}, bf16[640,128]{1,0:T(8,128)(2,1)S(1)}, u32[]{:S(2)}, u32[]{:S(2)}) collective-permute-start(bf16[640,128]{1,0:T(8,128)(2,1)S(1)} %get-tuple-element.39), channel_id=1, source_target_pairs={{0,1},{1,0},{2,3},{3,2},{4,5},{5,4},{6,7},{7,6},{8,9},{9,8},{10,11... | collective-permute-start | bytes 491528 | tf_op jit(solution)/shard_map/ppermute | solution.py:207
  16.5 1.4 %collective-permute-start.5 = (bf16[4,64,256]{2,1,0:T(8,128)(2,1)S(1)}, bf16[4,64,256]{2,1,0:T(8,128)(2,1)S(1)}, u32[]{:S(2)}, u32[]{:S(2)}) collective-permute-start(bf16[4,64,256]{2,1,0:T(8,128)(2,1)S(1)} %pack.1.mine), channel_id=1, source_target_pairs={{0,1},{1,0},{2,3},{3,2},{4,5},{5,4},{6,7},{7,6},{8,9},{9,8},{10,11... | collective-permute-start | bytes 393224 | tf_op jit(solution)/shard_map/ppermute | solution.py:207
  18.5 9.8 %collective-permute-start.10 = (bf16[640,256]{1,0:T(8,128)(2,1)S(1)}, bf16[640,256]{1,0:T(8,128)(2,1)S(1)}, u32[]{:S(2)}, u32[]{:S(2)}) collective-permute-start(bf16[640,256]{1,0:T(8,128)(2,1)S(1)} %get-tuple-element.50), channel_id=1, source_target_pairs={{0,2},{1,3},{2,0},{3,1},{4,6},{5,7},{6,4},{7,5},{8,10},{9,11},{10,... | collective-permute-start | bytes 983048 | tf_op jit(solution)/shard_map/ppermute | solution.py:210
  19.1 1.4 %collective-permute-start.8 = (bf16[320,256]{1,0:T(8,128)(2,1)S(1)}, bf16[320,256]{1,0:T(8,128)(2,1)S(1)}, u32[]{:S(2)}, u32[]{:S(2)}) collective-permute-start(bf16[320,256]{1,0:T(8,128)(2,1)S(1)} %get-tuple-element.48), channel_id=1, source_target_pairs={{0,1},{1,0},{2,3},{3,2},{4,5},{5,4},{6,7},{7,6},{8,9},{9,8},{10,11... | collective-permute-start | bytes 491528 | tf_op jit(solution)/shard_map/ppermute | solution.py:207
  19.1 1.6 %collective-permute-start.9 = (bf16[320,256]{1,0:T(8,128)(2,1)S(1)}, bf16[320,256]{1,0:T(8,128)(2,1)S(1)}, u32[]{:S(2)}, u32[]{:S(2)}) collective-permute-start(bf16[320,256]{1,0:T(8,128)(2,1)S(1)} %get-tuple-element.49), channel_id=1, source_target_pairs={{0,1},{1,0},{2,3},{3,2},{4,5},{5,4},{6,7},{7,6},{8,9},{9,8},{10,11... | collective-permute-start | bytes 491528 | tf_op jit(solution)/shard_map/ppermute | solution.py:207

commit v5 on v4

--- a/solution.py
+++ b/solution.py
@@ -59,29 +59,39 @@
             send[pl.ds(rows + i * rank, rank), :] = up[:, i * cols : (i + 1) * cols]
 
 
-def pick_kernel(sizes, adapters, lengths, slots, bank, after, *rest):
+def pick_kernel(sizes, adapter_row, slot_rows, adapters, lengths, slots, bank, after, *rest):
     owners, req_dev, per_owner = sizes
     picks, (table, sem, int_sem) = rest[:owners], rest[owners : owners + 3]
-    copies = [
+    ints = [
         pltpu.make_async_copy(a, b, int_sem.at[i])
         for i, (a, b) in enumerate(zip((adapters, lengths, slots), rest[owners + 3 :]))
     ]
-    for copy in copies:
+    for copy in ints:
         copy.start()
-    for copy in copies:
-        copy.wait()
     adapters, lengths, slots = rest[owners + 3 :]
     me = lax.axis_index("dp")
+    local_slot = slot_rows[...] - me * per_owner
+    owned = (local_slot >= 0) & (local_slot < per_owner)
+    adapter = lax.broadcasted_iota(jnp.int32, local_slot.shape, 0) * local_slot.shape[1]
+    adapter = adapter + lax.broadcasted_iota(jnp.int32, local_slot.shape, 1)
+    adapter = jnp.where(owned, adapter, -1)
+    local_slot = local_slot.astype(F32)
+    served = []
+    for home in range(owners):
+        value = jnp.zeros(local_slot.shape, F32)
+        for q in range(home * req_dev, (home + 1) * req_dev):
+            value = jnp.where(adapter == adapter_row[0:1, q : q + 1], local_slot, value)
+        served.append(jnp.sum(value).astype(jnp.int32))
     copies = []
     for shift in range(owners):
-        home = me ^ shift
-        index = jnp.int32(0)
-        for q in range(req_dev):
-            slot = slots[adapters[home * req_dev + q]]
-            index = jnp.where(slot // per_owner == me, slot % per_owner, index)
+        index = served[0]
+        for home in range(1, owners):
+            index = jnp.where((me ^ shift) == home, served[home], index)
         copy = pltpu.make_async_copy(bank.at[index], picks[shift], sem.at[shift])
         copy.start()
         copies.append(copy)
+    for copy in ints:
+        copy.wait()
     start = jnp.int32(0)
     at = lax.broadcasted_iota(jnp.int32, table.shape, 0)
     lane = lax.broadcasted_iota(jnp.int32, table.shape, 1)
@@ -129,12 +139,15 @@
         keep[shift - 1] = block_product(width, shift, 0, tokens, weight)
 
 
-def near_send_kernel(width, owners, tokens, weight, table, after, mask, *sends):
-    rows, cols = tokens.shape[0], mask.shape[1] // owners
+def mask_kernel(table, after, mask):
+    rows, cols = after.shape
     row = lax.broadcasted_iota(jnp.int32, (rows, cols), 0)
-    for s in range(owners):
+    for s in range(mask.shape[1] // cols):
         inside = (row >= table[s : s + 1, 0:1]) & (row < table[s : s + 1, 1:2])
         mask[:, s * cols : (s + 1) * cols] = jnp.where(inside, 1.0, 0.0).astype(BF16)
+
+
+def near_send_kernel(width, tokens, weight, after, *sends):
     other = block_product(width, 0, 1, tokens, weight).astype(BF16)
     size = sends[0].shape[0]
     for i, send in enumerate(sends):
@@ -147,7 +160,7 @@
 
 def far_kernel(width, halves, mask, hidden, got_hidden, mine, others, *rest):
     ups, keep, rest = rest[: width - 1], rest[width - 1], rest[width:]
-    gots, rest = rest[: -halves * (width - 1) - 2], rest[-halves * (width - 1) - 2 :]
+    gots, rest = rest[: -halves * (width - 1) - 3], rest[-halves * (width - 1) - 2 :]
     outs, core_out, rhs = rest[:-2], rest[-2], rest[-1]
     core = lax.axis_index("tensor") % CORES
     owners = mask.shape[1] // hidden.shape[1]
@@ -232,7 +245,7 @@
         functools.partial(pick_kernel, (owners, req_dev, per_owner)),
         out_shape=[jax.ShapeDtypeStruct((block, rank), BF16)] * owners
         + [jax.ShapeDtypeStruct((max(owners, 8), 128), jnp.int32)],
-        in_specs=[ANY] * 5,
+        in_specs=[VMEM] * 2 + [ANY] * 5,
         out_specs=[VMEM] * (owners + 1),
         scratch_shapes=[
             pltpu.SemaphoreType.DMA((owners,)),
@@ -244,7 +257,15 @@
         compiler_params=params(38),
         cost_estimate=cost(0, 2 * MIB),
         name="pick",
-    )(request_adapter, request_length, core_slot, core_bank, keep)
+    )(
+        request_adapter.reshape(1, -1),
+        core_slot.reshape(-1, 128),
+        request_adapter,
+        request_length,
+        core_slot,
+        core_bank,
+        keep,
+    )
     table = outs[-1]
     picks = ordered(outs[:-1], read=30 * MIB)
     order = sorted(range(1, owners), key=lambda s: -s.bit_length())
@@ -283,14 +304,15 @@
         "far_base",
         CORES * (width - 1),
     )
-    mask, *near_send = base(
-        functools.partial(near_send_kernel, width, owners),
-        [jax.ShapeDtypeStruct((rows, owners * cols), BF16)]
-        + [jax.ShapeDtypeStruct((rows // parts, out_block), BF16)] * parts,
-        [table, ordered([hidden], far_keep, down_basis)[0]],
-        "near_send",
-        1,
-    )
+    mask = pl.pallas_call(
+        mask_kernel,
+        out_shape=jax.ShapeDtypeStruct((rows, owners * cols), BF16),
+        in_specs=[VMEM, ANY],
+        out_specs=VMEM,
+        compiler_params=params(),
+        cost_estimate=cost(0, 2 * rows * owners * cols),
+        name="mask",
+    )(table, ordered([hidden], far_keep, down_basis)[0])
 
     packed = pl.pallas_call(
         functools.partial(pack_kernel, [0] + order),
@@ -302,6 +324,13 @@
         name="pack",
     )(*mine, mask)
     got_packed = pair(packed)
+    near_send = base(
+        functools.partial(near_send_kernel, width),
+        [jax.ShapeDtypeStruct((rows // parts, out_block), BF16)] * parts,
+        [packed],
+        "near_send",
+        1,
+    )
     far_got = [pair(a) for a in far_send]
 
     halves = 1
@@ -310,13 +339,13 @@
         functools.partial(far_kernel, width, halves),
         out_shape=[jax.ShapeDtypeStruct((size, out_block), BF16)] * (halves * (width - 1))
         + [jax.ShapeDtypeStruct((rows, rank), BF16)],
-        in_specs=[VMEM] * (5 + width + parts),
+        in_specs=[VMEM] * (5 + width + parts) + [ANY],
         out_specs=[VMEM] * (halves * (width - 1) + 1),
         scratch_shapes=[pltpu.VMEM((owners * cols, rank), BF16)],
         compiler_params=params(),
         cost_estimate=cost(2 * rows * (owners * cols * rank + rank * out_block), rows * out_block * 10),
         name="far",
-    )(mask, hidden, got_hidden, packed, got_packed, *gots[::-1], far_keep, *far_got)
+    )(mask, hidden, got_hidden, packed, got_packed, *gots[::-1], far_keep, *far_got, near_send[0])
     core_out = outs[-1]
     far_gots = [along_x(outs[i], i // halves + 1) for i in range(halves * (width - 1))]
 

time: 29.2 us -> 28.4 us (0.973)
  Pallas kernels: 7.59 us -> 6.92 us
    ppermute x6, waiting for transfers between devices: 1.49 us -> 0.66 us  [pair(): return lax.ppermute(a, 'tensor', [(i, i ^ 1) for i in range(tensor)])]
    pallas_call x1, Pallas kernels: 2.03 us -> 1.23 us  [local(): pl.pallas_call(functools.partial(pick_kernel, (owners, req_dev, per_owner...]
    ppermute x3, waiting for transfers between devices: 0.34 us -> 1.11 us  [along_dp(): return lax.ppermute(a, 'dp', [(i, i ^ shift) for i in range(owners)])]
    pallas_call x0 -> x1, Pallas kernels: none -> 0.62 us  [local(): pl.pallas_call(mask_kernel, out_shape=jax.ShapeDtypeStruct((rows, owners...]
    pallas_call x3, Pallas kernels: 3.8 us -> 3.31 us  [base(): pl.pallas_call(kernel, out_shape=shapes, in_specs=[VMEM] * (1 + len(after...]
  transfers between devices with their start and end apart: 11 -> 11, of which waited for: 4 -> 4; matrix products, arithmetic and copies ran while one was open for 0% -> 0% of each run, Pallas kernels for 21% -> 19%
where the time goes in v5:
time: 28.4 us; the launch traced here: 28.3 us
  starting transfers between devices  9.14 us (32%)
  waiting for transfers between devices  9.12 us (32%)
  Pallas kernels  6.92 us (24%)
  matrix products  2.89 us (10%)
    ppermute x2, waiting for transfers between devices, along_x(): lax.ppermute(a, 'tensor', [(i, (i + shift * CORES) % tensor) for i in ran...  7.34 us
    ppermute x3, starting transfers between devices, along_dp(): return lax.ppermute(a, 'dp', [(i, i ^ shift) for i in range(owners)])  4.23 us
    ppermute x2, starting transfers between devices, along_x(): lax.ppermute(a, 'tensor', [(i, (i + shift * CORES) % tensor) for i in ran...  3.61 us
    pallas_call x3, Pallas kernels, base(): pl.pallas_call(kernel, out_shape=shapes, in_specs=[VMEM] * (1 + len(after...  3.31 us
    dot_general x1, matrix products, local(): part = jnp.dot(tokens, down_basis, preferred_element_type=F32)  2.89 us
    ppermute x6, starting transfers between devices, pair(): return lax.ppermute(a, 'tensor', [(i, i ^ 1) for i in range(tensor)])  1.29 us
    pallas_call x1, Pallas kernels, local(): pl.pallas_call(functools.partial(pick_kernel, (owners, req_dev, per_owner...  1.23 us
    ppermute x3, waiting for transfers between devices, along_dp(): return lax.ppermute(a, 'dp', [(i, i ^ shift) for i in range(owners)])  1.11 us
  transfers between devices with their start and end apart: 11, of which 4 were waited for; matrix products, arithmetic and copies ran while one was open for 0% of the time, Pallas kernels for 19%

profile of v5, /device:TPU:0, one launch (start us, length us, event | category | flops | bytes accessed | tf_op | source)
XLA Modules:
  0.0 28.3 jit_solution(5166427281498215587)
XLA Ops:
  0.0 0.0 copy-start.3
  0.0 0.0 copy-start.5
  0.0 0.0 copy-start.4
  0.0 0.0 copy-start.6
  0.0 2.9 %fusion.part = f32[640,256]{1,0:T(8,128)S(1)} fusion(bf16[640,2048]{1,0:T(8,128)(2,1)} %tokens.5, bf16[2048,256]{1,0:T(8,128)(2,1)} %refs_2_.1), kind=kOutput, calls=%fused_computation | convolution fusion | flops 671088640 | bytes 4325376 | tf_op jit(solution)/shard_map/dot_general | solution.py:230
  2.9 0.0 copy-done.3
  2.9 0.1 split.1
  3.0 3.0 %collective-permute-start = (bf16[1152,128]{1,0:T(8,128)(2,1)S(1)}, bf16[1152,128]{1,0:T(8,128)(2,1)S(1)}, u32[]{:S(2)}, u32[]{:S(2)}) collective-permute-start(bf16[1152,128]{1,0:T(8,128)(2,1)S(1)} %get-tuple-element.29), channel_id=1, source_target_pairs={{0,2},{1,3},{2,0},{3,1},{4,6},{5,7},{6,4},{7,5},{8,10},{9,11},{10,... | collective-permute-start | bytes 884744 | tf_op jit(solution)/shard_map/ppermute | solution.py:223
  6.0 0.0 copy-done.5
  6.0 0.0 copy-done.4
  6.0 0.0 copy-done.6
  6.1 0.0 copy-start
  6.1 0.0 copy-start.1
  6.1 1.2 %pick.1 = (bf16[64,256]{1,0:T(8,128)(2,1)S(1)}, bf16[64,256]{1,0:T(8,128)(2,1)S(1)}, bf16[64,256]{1,0:T(8,128)(2,1)S(1)}, bf16[64,256]{1,0:T(8,128)(2,1)S(1)}, s32[8,128]{1,0:T(8,128)S(1)}) custom-call(s32[1,16]{1,0:T(1,128)S(1)} %bitcast.5, s32[16,128]{1,0:T(8,128)S(1)} %bitcast.4, s32[16]{0:T(128)S(1)} %copy-done.5, s32[16]{0:T(128)S(1)} %copy-done.6, ...), custom_call_target="tpu_custom_call" | custom-call | bytes 2097152 | tf_op jit(solution)/shard_map/pick/pallas_call | solution.py:244
  7.3 2.7 %collective-permute-start.2 = (bf16[64,256]{1,0:T(8,128)(2,1)S(1)}, bf16[64,256]{1,0:T(8,128)(2,1)S(1)}, u32[]{:S(2)}, u32[]{:S(2)}) collective-permute-start(bf16[64,256]{1,0:T(8,128)(2,1)S(1)} %get-tuple-element.38), channel_id=1, source_target_pairs={{0,8},{4,12},{8,0},{12,4},{1,9},{5,13},{9,1},{13,5},{2,10},{6,14},... | collective-permute-start | bytes 98312 | tf_op jit(solution)/shard_map/ppermute | solution.py:228
  10.0 1.3 %collective-permute-start.3 = (bf16[64,256]{1,0:T(8,128)(2,1)S(1)}, bf16[64,256]{1,0:T(8,128)(2,1)S(1)}, u32[]{:S(2)}, u32[]{:S(2)}) collective-permute-start(bf16[64,256]{1,0:T(8,128)(2,1)S(1)} %get-tuple-element.39), channel_id=1, source_target_pairs={{0,12},{4,8},{8,4},{12,0},{1,13},{5,9},{9,5},{13,1},{2,14},{6,10},... | collective-permute-start | bytes 98312 | tf_op jit(solution)/shard_map/ppermute | solution.py:228
  11.3 0.2 collective-permute-start.4
  11.6 0.0 copy-done
  11.6 0.0 copy-done.1
  11.6 0.0 copy-start.2
  11.6 1.6 %far_base.1 = (f32[1,640,256]{2,1,0:T(8,128)S(1)}, bf16[1,320,256]{2,1,0:T(8,128)(2,1)S(1)}, bf16[1,320,256]{2,1,0:T(8,128)(2,1)S(1)}) custom-call(bf16[640,2048]{1,0:T(8,128)(2,1)S(1)} %copy-done.1, bf16[2048,1024]{1,0:T(8,128)(2,1)S(1)} %copy-done, bf16[64,256]{1,0:T(8,128)(2,1)S(1)} %get-tuple-element.35.after.refs_0_), custom_call_target="tpu_custom_call" | custom-call | flops 1342177280 | bytes 4718592 | tf_op jit(solution)/shard_map/far_base/pallas_call | solution.py:286
  13.1 0.1 collective-permute-start.6
  13.2 0.0 collective-permute-done.rest_0_
  13.2 0.5 %collective-permute-start.7 = (bf16[1,320,256]{2,1,0:T(8,128)(2,1)S(1)}, bf16[1,320,256]{2,1,0:T(8,128)(2,1)S(1)}, u32[]{:S(2)}, u32[]{:S(2)}) collective-permute-start(bf16[1,320,256]{2,1,0:T(8,128)(2,1)S(1)} %get-tuple-element.42), channel_id=1, source_target_pairs={{0,1},{1,0},{2,3},{3,2},{4,5},{5,4},{6,7},{7,6},{8,9},{9,8},{10,11... | collective-permute-start | bytes 491528 | tf_op jit(solution)/shard_map/ppermute | solution.py:220
  13.8 0.0 collective-permute-done.2.refs_1_
  13.8 0.2 collective-permute-start.1
  13.9 0.0 copy-done.2
  14.0 0.6 %mask.1.refs_4_ = bf16[640,512]{1,0:T(8,128)(2,1)S(1)} custom-call(s32[8,128]{1,0:T(8,128)S(1)} %get-tuple-element.28.table, f32[640,128]{1,0:T(8,128)S(1)} %ordered.4.after), custom_call_target="tpu_custom_call" | custom-call | bytes 655360 | tf_op jit(solution)/shard_map/mask/pallas_call | solution.py:307
  14.6 1.1 %collective-permute-done.3.refs_2_ = bf16[64,256]{1,0:T(8,128)(2,1)S(1)} collective-permute-done((bf16[64,256]{1,0:T(8,128)(2,1)S(1)}, bf16[64,256]{1,0:T(8,128)(2,1)S(1)}, u32[]{:S(2)}, u32[]{:S(2)}) %collective-permute-start.3) | collective-permute-done | bytes 32800 | tf_op jit(solution)/shard_map/ppermute | solution.py:228
  15.7 0.0 collective-permute-done.4.refs_3_
  15.7 0.1 collective-permute-start.5
  15.8 0.9 %near_send.1 = (bf16[320,256]{1,0:T(8,128)(2,1)S(1)}, bf16[320,256]{1,0:T(8,128)(2,1)S(1)}) custom-call(bf16[640,2048]{1,0:T(8,128)(2,1)S(1)} %copy-done.1, bf16[2048,1024]{1,0:T(8,128)(2,1)S(1)} %copy-done, bf16[4,64,256]{2,1,0:T(8,128)(2,1)S(1)} %pack.1.after.mine), custom_call_target="tpu_custom_call" | custom-call | flops 671088640 | bytes 3670016 | tf_op jit(solution)/shard_map/near_send/pallas_call | solution.py:286
  16.7 0.0 collective-permute-done.6.rest_2_
  16.7 0.0 collective-permute-done.7.rest_3_
  16.7 0.4 %collective-permute-done.5.others = bf16[4,64,256]{2,1,0:T(8,128)(2,1)S(1)} collective-permute-done((bf16[4,64,256]{2,1,0:T(8,128)(2,1)S(1)}, bf16[4,64,256]{2,1,0:T(8,128)(2,1)S(1)}, u32[]{:S(2)}, u32[]{:S(2)}) %collective-permute-start.5) | collective-permute-done | bytes 131104 | tf_op jit(solution)/shard_map/ppermute | solution.py:220
  17.1 0.0 collective-permute-done.1.got_hidden
  17.1 0.6 %far.1 = (bf16[640,256]{1,0:T(8,128)(2,1)S(1)}, bf16[640,256]{1,0:T(8,128)(2,1)S(1)}) custom-call(bf16[640,512]{1,0:T(8,128)(2,1)S(1)} %mask.1.refs_4_, f32[640,128]{1,0:T(8,128)S(1)} %get-tuple-element.30.hidden, bf16[640,128]{1,0:T(8,128)(2,1)S(1)} %collective-permute-done.1.got_hidden, bf16[4,64,256]{2,1,0:T(8,128)(2,1)S(1)} %pack.1.after.mine, ...), custom_call_target="tpu_custom_call" | custom-call | flops 251658240 | bytes 1638400 | tf_op jit(solution)/shard_map/far/pallas_call | solution.py:338
  17.7 0.6 %collective-permute-start.10 = (bf16[640,256]{1,0:T(8,128)(2,1)S(1)}, bf16[640,256]{1,0:T(8,128)(2,1)S(1)}, u32[]{:S(2)}, u32[]{:S(2)}) collective-permute-start(bf16[640,256]{1,0:T(8,128)(2,1)S(1)} %get-tuple-element.48), channel_id=1, source_target_pairs={{0,2},{1,3},{2,0},{3,1},{4,6},{5,7},{6,4},{7,5},{8,10},{9,11},{10,... | collective-permute-start | bytes 983048 | tf_op jit(solution)/shard_map/ppermute | solution.py:223
  18.3 0.0 collective-permute-start.8
  18.3 0.5 %collective-permute-start.9 = (bf16[320,256]{1,0:T(8,128)(2,1)S(1)}, bf16[320,256]{1,0:T(8,128)(2,1)S(1)}, u32[]{:S(2)}, u32[]{:S(2)}) collective-permute-start(bf16[320,256]{1,0:T(8,128)(2,1)S(1)} %get-tuple-element.47), channel_id=1, source_target_pairs={{0,1},{1,0},{2,3},{3,2},{4,5},{5,4},{6,7},{7,6},{8,9},{9,8},{10,11... | collective-permute-start | bytes 491528 | tf_op jit(solution)/shard_map/ppermute | solution.py:220
  18.8 0.9 %near_keep.1.keep = f32[640,256]{1,0:T(8,128)S(1)} custom-call(bf16[640,2048]{1,0:T(8,128)(2,1)S(1)} %copy-done.1, bf16[2048,1024]{1,0:T(8,128)(2,1)S(1)} %copy-done, bf16[640,256]{1,0:T(8,128)(2,1)S(1)} %get-tuple-element.44.after.refs_2_.part), custom_call_target="tpu_custom_call" | custom-call | flops 671088640 | bytes 3670016 | tf_op jit(solution)/shard_map/near_keep/pallas_call | solution.py:286
  19.7 0.0 collective-permute-done.8.rest_0_
  19.7 0.2 collective-permute-done.9.rest_1_
  19.9 0.2 near.1
  20.2 7.3 %collective-permute-done.10.rest_0_ = bf16[640,256]{1,0:T(8,128)(2,1)S(1)} collective-permute-done((bf16[640,256]{1,0:T(8,128)(2,1)S(1)}, bf16[640,256]{1,0:T(8,128)(2,1)S(1)}, u32[]{:S(2)}, u32[]{:S(2)}) %collective-permute-start.10) | collective-permute-done | bytes 327712 | tf_op jit(solution)/shard_map/ppermute | solution.py:223
  27.5 0.8 %final.1 = bf16[640,256]{1,0:T(8,128)(2,1)} custom-call(f32[640,256]{1,0:T(8,128)S(1)} %near.1, bf16[640,256]{1,0:T(8,128)(2,1)S(1)} %collective-permute-done.10.rest_0_), custom_call_target="tpu_custom_call" | custom-call | bytes 1310720 | tf_op jit(solution)/shard_map/final/pallas_call | solution.py:370
  (6 shorter events, 0.1 us)
Async XLA Ops:
  0.0 2.9 %copy-start.3 = (bf16[256,256]{1,0:T(8,128)(2,1)S(1)}, bf16[256,256]{1,0:T(8,128)(2,1)}, u32[]{:S(2)}) copy-start(bf16[256,256]{1,0:T(8,128)(2,1)} %up.3) | copy-start | bytes 393220
  0.0 6.0 %copy-start.5 = (s32[16]{0:T(128)S(1)}, s32[16]{0:T(128)}, u32[]{:S(2)}) copy-start(s32[16]{0:T(128)} %adapters.1) | copy-start | bytes 196
  0.0 6.0 %copy-start.4 = (s32[2048]{0:T(1024)S(1)}, s32[2048]{0:T(1024)}, u32[]{:S(2)}) copy-start(s32[2048]{0:T(1024)} %slots.1) | copy-start | bytes 24580
  0.0 6.0 %copy-start.6 = (s32[16]{0:T(128)S(1)}, s32[16]{0:T(128)}, u32[]{:S(2)}) copy-start(s32[16]{0:T(128)} %lengths.1) | copy-start | bytes 196
  3.0 10.2 %collective-permute-start = (bf16[1152,128]{1,0:T(8,128)(2,1)S(1)}, bf16[1152,128]{1,0:T(8,128)(2,1)S(1)}, u32[]{:S(2)}, u32[]{:S(2)}) collective-permute-start(bf16[1152,128]{1,0:T(8,128)(2,1)S(1)} %get-tuple-element.29), channel_id=1, source_target_pairs={{0,2},{1,3},{2,0},{3,1},{4,6},{5,7},{6,4},{7,5},{8,10},{9,11},{10,... | collective-permute-start | bytes 884744 | tf_op jit(solution)/shard_map/ppermute | solution.py:223
  6.1 5.5 %copy-start = (bf16[2048,1024]{1,0:T(8,128)(2,1)S(1)}, bf16[2048,1024]{1,0:T(8,128)(2,1)}, u32[]{:S(2)}) copy-start(bf16[2048,1024]{1,0:T(8,128)(2,1)} %weight.5) | copy-start | bytes 12582916
  6.1 5.5 %copy-start.1 = (bf16[640,2048]{1,0:T(8,128)(2,1)S(1)}, bf16[640,2048]{1,0:T(8,128)(2,1)}, u32[]{:S(2)}) copy-start(bf16[640,2048]{1,0:T(8,128)(2,1)} %tokens.5) | copy-start | bytes 7864324
  7.3 6.4 %collective-permute-start.2 = (bf16[64,256]{1,0:T(8,128)(2,1)S(1)}, bf16[64,256]{1,0:T(8,128)(2,1)S(1)}, u32[]{:S(2)}, u32[]{:S(2)}) collective-permute-start(bf16[64,256]{1,0:T(8,128)(2,1)S(1)} %get-tuple-element.38), channel_id=1, source_target_pairs={{0,8},{4,12},{8,0},{12,4},{1,9},{5,13},{9,1},{13,5},{2,10},{6,14},... | collective-permute-start | bytes 98312 | tf_op jit(solution)/shard_map/ppermute | solution.py:228
  10.0 5.7 %collective-permute-start.3 = (bf16[64,256]{1,0:T(8,128)(2,1)S(1)}, bf16[64,256]{1,0:T(8,128)(2,1)S(1)}, u32[]{:S(2)}, u32[]{:S(2)}) collective-permute-start(bf16[64,256]{1,0:T(8,128)(2,1)S(1)} %get-tuple-element.39), channel_id=1, source_target_pairs={{0,12},{4,8},{8,4},{12,0},{1,13},{5,9},{9,5},{13,1},{2,14},{6,10},... | collective-permute-start | bytes 98312 | tf_op jit(solution)/shard_map/ppermute | solution.py:228
  11.3 4.4 %collective-permute-start.4 = (bf16[64,256]{1,0:T(8,128)(2,1)S(1)}, bf16[64,256]{1,0:T(8,128)(2,1)S(1)}, u32[]{:S(2)}, u32[]{:S(2)}) collective-permute-start(bf16[64,256]{1,0:T(8,128)(2,1)S(1)} %get-tuple-element.40), channel_id=1, source_target_pairs={{0,4},{4,0},{8,12},{12,8},{1,5},{5,1},{9,13},{13,9},{2,6},{6,2},{1... | collective-permute-start | bytes 98312 | tf_op jit(solution)/shard_map/ppermute | solution.py:228
  11.6 2.4 %copy-start.2 = (bf16[2048,256]{1,0:T(8,128)(2,1)S(1)}, bf16[2048,256]{1,0:T(8,128)(2,1)}, u32[]{:S(2)}) copy-start(bf16[2048,256]{1,0:T(8,128)(2,1)} %refs_2_.1) | copy-start | bytes 3145732
  13.1 3.6 %collective-permute-start.6 = (bf16[1,320,256]{2,1,0:T(8,128)(2,1)S(1)}, bf16[1,320,256]{2,1,0:T(8,128)(2,1)S(1)}, u32[]{:S(2)}, u32[]{:S(2)}) collective-permute-start(bf16[1,320,256]{2,1,0:T(8,128)(2,1)S(1)} %get-tuple-element.41), channel_id=1, source_target_pairs={{0,1},{1,0},{2,3},{3,2},{4,5},{5,4},{6,7},{7,6},{8,9},{9,8},{10,11... | collective-permute-start | bytes 491528 | tf_op jit(solution)/shard_map/ppermute | solution.py:220
  13.2 3.5 %collective-permute-start.7 = (bf16[1,320,256]{2,1,0:T(8,128)(2,1)S(1)}, bf16[1,320,256]{2,1,0:T(8,128)(2,1)S(1)}, u32[]{:S(2)}, u32[]{:S(2)}) collective-permute-start(bf16[1,320,256]{2,1,0:T(8,128)(2,1)S(1)} %get-tuple-element.42), channel_id=1, source_target_pairs={{0,1},{1,0},{2,3},{3,2},{4,5},{5,4},{6,7},{7,6},{8,9},{9,8},{10,11... | collective-permute-start | bytes 491528 | tf_op jit(solution)/shard_map/ppermute | solution.py:220
  13.8 3.4 %collective-permute-start.1 = (bf16[640,128]{1,0:T(8,128)(2,1)S(1)}, bf16[640,128]{1,0:T(8,128)(2,1)S(1)}, u32[]{:S(2)}, u32[]{:S(2)}) collective-permute-start(bf16[640,128]{1,0:T(8,128)(2,1)S(1)} %get-tuple-element.37), channel_id=1, source_target_pairs={{0,1},{1,0},{2,3},{3,2},{4,5},{5,4},{6,7},{7,6},{8,9},{9,8},{10,11... | collective-permute-start | bytes 491528 | tf_op jit(solution)/shard_map/ppermute | solution.py:220
  15.7 1.4 %collective-permute-start.5 = (bf16[4,64,256]{2,1,0:T(8,128)(2,1)S(1)}, bf16[4,64,256]{2,1,0:T(8,128)(2,1)S(1)}, u32[]{:S(2)}, u32[]{:S(2)}) collective-permute-start(bf16[4,64,256]{2,1,0:T(8,128)(2,1)S(1)} %pack.1.after.mine), channel_id=1, source_target_pairs={{0,1},{1,0},{2,3},{3,2},{4,5},{5,4},{6,7},{7,6},{8,9},{9,8},{10,11... | collective-permute-start | bytes 393224 | tf_op jit(solution)/shard_map/ppermute | solution.py:220
  17.7 9.8 %collective-permute-start.10 = (bf16[640,256]{1,0:T(8,128)(2,1)S(1)}, bf16[640,256]{1,0:T(8,128)(2,1)S(1)}, u32[]{:S(2)}, u32[]{:S(2)}) collective-permute-start(bf16[640,256]{1,0:T(8,128)(2,1)S(1)} %get-tuple-element.48), channel_id=1, source_target_pairs={{0,2},{1,3},{2,0},{3,1},{4,6},{5,7},{6,4},{7,5},{8,10},{9,11},{10,... | collective-permute-start | bytes 983048 | tf_op jit(solution)/shard_map/ppermute | solution.py:223
  18.3 1.4 %collective-permute-start.8 = (bf16[320,256]{1,0:T(8,128)(2,1)S(1)}, bf16[320,256]{1,0:T(8,128)(2,1)S(1)}, u32[]{:S(2)}, u32[]{:S(2)}) collective-permute-start(bf16[320,256]{1,0:T(8,128)(2,1)S(1)} %get-tuple-element.46), channel_id=1, source_target_pairs={{0,1},{1,0},{2,3},{3,2},{4,5},{5,4},{6,7},{7,6},{8,9},{9,8},{10,11... | collective-permute-start | bytes 491528 | tf_op jit(solution)/shard_map/ppermute | solution.py:220
  18.3 1.6 %collective-permute-start.9 = (bf16[320,256]{1,0:T(8,128)(2,1)S(1)}, bf16[320,256]{1,0:T(8,128)(2,1)S(1)}, u32[]{:S(2)}, u32[]{:S(2)}) collective-permute-start(bf16[320,256]{1,0:T(8,128)(2,1)S(1)} %get-tuple-element.47), channel_id=1, source_target_pairs={{0,1},{1,0},{2,3},{3,2},{4,5},{5,4},{6,7},{7,6},{8,9},{9,8},{10,11... | collective-permute-start | bytes 491528 | tf_op jit(solution)/shard_map/ppermute | solution.py:220

commit v6 on v5

--- a/solution.py
+++ b/solution.py
@@ -195,14 +195,24 @@
 
 
 def final_kernel(halves, near, *rest):
-    gots, out = rest[:-1], rest[-1]
-    size = near.shape[0] // halves
-    for i in range(halves):
-        rows = pl.ds(i * size, size)
-        total = near[rows, :]
-        for got in gots[i::halves]:
-            total = total + got[...].astype(F32)
-        out[rows, :] = total.astype(BF16)
+    gots, (out, buf, sem) = rest[:-3], rest[-3:]
+    rows = near.shape[0]
+    size = rows // 2
+    copies = []
+    for i in range(2):
+        at = slice(i * size, (i + 1) * size)
+        total = near[at, :]
+        for got in gots:
+            total = total + got[at, :].astype(F32)
+        buf[at, :] = total.astype(BF16)
+        copies.append(
+            pltpu.make_async_copy(
+                buf.at[pl.ds(i * size, size)], out.at[pl.ds(i * size, size)], sem.at[i]
+            )
+        )
+        copies[-1].start()
+    for copy in copies:
+        copy.wait()
 
 
 def local(
@@ -371,7 +381,8 @@
         functools.partial(final_kernel, halves),
         out_shape=jax.ShapeDtypeStruct((rows, out_block), BF16),
         in_specs=[VMEM] * (1 + len(far_gots)),
-        out_specs=VMEM,
+        out_specs=ANY,
+        scratch_shapes=[pltpu.VMEM((rows, out_block), BF16), pltpu.SemaphoreType.DMA((2,))],
         compiler_params=params(),
         cost_estimate=cost(0, rows * out_block * 8),
         name="final",

time: 28.4 us -> 28.4 us (level)
  no operation moved by 1% of the time
where the time goes in v6:
time: 28.4 us; the launch traced here: 28.3 us
  starting transfers between devices  9.14 us (32%)
  waiting for transfers between devices  9.12 us (32%)
  Pallas kernels  6.9 us (24%)
  matrix products  2.89 us (10%)
    ppermute x2, waiting for transfers between devices, along_x(): lax.ppermute(a, 'tensor', [(i, (i + shift * CORES) % tensor) for i in ran...  7.34 us
    ppermute x3, starting transfers between devices, along_dp(): return lax.ppermute(a, 'dp', [(i, i ^ shift) for i in range(owners)])  4.23 us
    ppermute x2, starting transfers between devices, along_x(): lax.ppermute(a, 'tensor', [(i, (i + shift * CORES) % tensor) for i in ran...  3.61 us
    pallas_call x3, Pallas kernels, base(): pl.pallas_call(kernel, out_shape=shapes, in_specs=[VMEM] * (1 + len(after...  3.31 us
    dot_general x1, matrix products, local(): part = jnp.dot(tokens, down_basis, preferred_element_type=F32)  2.89 us
    ppermute x6, starting transfers between devices, pair(): return lax.ppermute(a, 'tensor', [(i, i ^ 1) for i in range(tensor)])  1.29 us
    pallas_call x1, Pallas kernels, local(): pl.pallas_call(functools.partial(pick_kernel, (owners, req_dev, per_owner...  1.23 us
    ppermute x3, waiting for transfers between devices, along_dp(): return lax.ppermute(a, 'dp', [(i, i ^ shift) for i in range(owners)])  1.11 us
  transfers between devices with their start and end apart: 11, of which 4 were waited for; matrix products, arithmetic and copies ran while one was open for 0% of the time, Pallas kernels for 19%

profile of v6, /device:TPU:0, one launch (start us, length us, event | category | flops | bytes accessed | tf_op | source)
XLA Modules:
  0.0 28.3 jit_solution(6826966872441504163)
XLA Ops:
  0.0 0.0 copy-start.3
  0.0 0.0 copy-start.5
  0.0 0.0 copy-start.4
  0.0 0.0 copy-start.6
  0.0 2.9 %fusion.part = f32[640,256]{1,0:T(8,128)S(1)} fusion(bf16[640,2048]{1,0:T(8,128)(2,1)} %tokens.5, bf16[2048,256]{1,0:T(8,128)(2,1)} %refs_2_.1), kind=kOutput, calls=%fused_computation | convolution fusion | flops 671088640 | bytes 4325376 | tf_op jit(solution)/shard_map/dot_general | solution.py:240
  2.9 0.0 copy-done.3
  2.9 0.1 split.1
  3.0 3.0 %collective-permute-start = (bf16[1152,128]{1,0:T(8,128)(2,1)S(1)}, bf16[1152,128]{1,0:T(8,128)(2,1)S(1)}, u32[]{:S(2)}, u32[]{:S(2)}) collective-permute-start(bf16[1152,128]{1,0:T(8,128)(2,1)S(1)} %get-tuple-element.29), channel_id=1, source_target_pairs={{0,2},{1,3},{2,0},{3,1},{4,6},{5,7},{6,4},{7,5},{8,10},{9,11},{10,... | collective-permute-start | bytes 884744 | tf_op jit(solution)/shard_map/ppermute | solution.py:233
  6.0 0.0 copy-done.5
  6.0 0.0 copy-done.4
  6.0 0.0 copy-done.6
  6.1 0.0 copy-start
  6.1 0.0 copy-start.1
  6.1 1.2 %pick.1 = (bf16[64,256]{1,0:T(8,128)(2,1)S(1)}, bf16[64,256]{1,0:T(8,128)(2,1)S(1)}, bf16[64,256]{1,0:T(8,128)(2,1)S(1)}, bf16[64,256]{1,0:T(8,128)(2,1)S(1)}, s32[8,128]{1,0:T(8,128)S(1)}) custom-call(s32[1,16]{1,0:T(1,128)S(1)} %bitcast.5, s32[16,128]{1,0:T(8,128)S(1)} %bitcast.4, s32[16]{0:T(128)S(1)} %copy-done.5, s32[16]{0:T(128)S(1)} %copy-done.6, ...), custom_call_target="tpu_custom_call" | custom-call | bytes 2097152 | tf_op jit(solution)/shard_map/pick/pallas_call | solution.py:254
  7.3 2.7 %collective-permute-start.2 = (bf16[64,256]{1,0:T(8,128)(2,1)S(1)}, bf16[64,256]{1,0:T(8,128)(2,1)S(1)}, u32[]{:S(2)}, u32[]{:S(2)}) collective-permute-start(bf16[64,256]{1,0:T(8,128)(2,1)S(1)} %get-tuple-element.38), channel_id=1, source_target_pairs={{0,8},{4,12},{8,0},{12,4},{1,9},{5,13},{9,1},{13,5},{2,10},{6,14},... | collective-permute-start | bytes 98312 | tf_op jit(solution)/shard_map/ppermute | solution.py:238
  10.0 1.3 %collective-permute-start.3 = (bf16[64,256]{1,0:T(8,128)(2,1)S(1)}, bf16[64,256]{1,0:T(8,128)(2,1)S(1)}, u32[]{:S(2)}, u32[]{:S(2)}) collective-permute-start(bf16[64,256]{1,0:T(8,128)(2,1)S(1)} %get-tuple-element.39), channel_id=1, source_target_pairs={{0,12},{4,8},{8,4},{12,0},{1,13},{5,9},{9,5},{13,1},{2,14},{6,10},... | collective-permute-start | bytes 98312 | tf_op jit(solution)/shard_map/ppermute | solution.py:238
  11.3 0.2 collective-permute-start.4
  11.6 0.0 copy-done
  11.6 0.0 copy-done.1
  11.6 0.0 copy-start.2
  11.6 1.6 %far_base.1 = (f32[1,640,256]{2,1,0:T(8,128)S(1)}, bf16[1,320,256]{2,1,0:T(8,128)(2,1)S(1)}, bf16[1,320,256]{2,1,0:T(8,128)(2,1)S(1)}) custom-call(bf16[640,2048]{1,0:T(8,128)(2,1)S(1)} %copy-done.1, bf16[2048,1024]{1,0:T(8,128)(2,1)S(1)} %copy-done, bf16[64,256]{1,0:T(8,128)(2,1)S(1)} %get-tuple-element.35.after.refs_0_), custom_call_target="tpu_custom_call" | custom-call | flops 1342177280 | bytes 4718592 | tf_op jit(solution)/shard_map/far_base/pallas_call | solution.py:296
  13.1 0.1 collective-permute-start.6
  13.2 0.0 collective-permute-done.rest_0_
  13.2 0.5 %collective-permute-start.7 = (bf16[1,320,256]{2,1,0:T(8,128)(2,1)S(1)}, bf16[1,320,256]{2,1,0:T(8,128)(2,1)S(1)}, u32[]{:S(2)}, u32[]{:S(2)}) collective-permute-start(bf16[1,320,256]{2,1,0:T(8,128)(2,1)S(1)} %get-tuple-element.42), channel_id=1, source_target_pairs={{0,1},{1,0},{2,3},{3,2},{4,5},{5,4},{6,7},{7,6},{8,9},{9,8},{10,11... | collective-permute-start | bytes 491528 | tf_op jit(solution)/shard_map/ppermute | solution.py:230
  13.8 0.0 collective-permute-done.2.refs_1_
  13.8 0.2 collective-permute-start.1
  13.9 0.0 copy-done.2
  14.0 0.6 %mask.1.refs_4_ = bf16[640,512]{1,0:T(8,128)(2,1)S(1)} custom-call(s32[8,128]{1,0:T(8,128)S(1)} %get-tuple-element.28.table, f32[640,128]{1,0:T(8,128)S(1)} %ordered.4.after), custom_call_target="tpu_custom_call" | custom-call | bytes 655360 | tf_op jit(solution)/shard_map/mask/pallas_call | solution.py:317
  14.6 1.1 %collective-permute-done.3.refs_2_ = bf16[64,256]{1,0:T(8,128)(2,1)S(1)} collective-permute-done((bf16[64,256]{1,0:T(8,128)(2,1)S(1)}, bf16[64,256]{1,0:T(8,128)(2,1)S(1)}, u32[]{:S(2)}, u32[]{:S(2)}) %collective-permute-start.3) | collective-permute-done | bytes 32800 | tf_op jit(solution)/shard_map/ppermute | solution.py:238
  15.7 0.0 collective-permute-done.4.refs_3_
  15.7 0.1 collective-permute-start.5
  15.8 0.9 %near_send.1 = (bf16[320,256]{1,0:T(8,128)(2,1)S(1)}, bf16[320,256]{1,0:T(8,128)(2,1)S(1)}) custom-call(bf16[640,2048]{1,0:T(8,128)(2,1)S(1)} %copy-done.1, bf16[2048,1024]{1,0:T(8,128)(2,1)S(1)} %copy-done, bf16[4,64,256]{2,1,0:T(8,128)(2,1)S(1)} %pack.1.after.mine), custom_call_target="tpu_custom_call" | custom-call | flops 671088640 | bytes 3670016 | tf_op jit(solution)/shard_map/near_send/pallas_call | solution.py:296
  16.7 0.0 collective-permute-done.6.rest_2_
  16.7 0.0 collective-permute-done.7.rest_3_
  16.7 0.4 %collective-permute-done.5.others = bf16[4,64,256]{2,1,0:T(8,128)(2,1)S(1)} collective-permute-done((bf16[4,64,256]{2,1,0:T(8,128)(2,1)S(1)}, bf16[4,64,256]{2,1,0:T(8,128)(2,1)S(1)}, u32[]{:S(2)}, u32[]{:S(2)}) %collective-permute-start.5) | collective-permute-done | bytes 131104 | tf_op jit(solution)/shard_map/ppermute | solution.py:230
  17.1 0.0 collective-permute-done.1.got_hidden
  17.1 0.6 %far.1 = (bf16[640,256]{1,0:T(8,128)(2,1)S(1)}, bf16[640,256]{1,0:T(8,128)(2,1)S(1)}) custom-call(bf16[640,512]{1,0:T(8,128)(2,1)S(1)} %mask.1.refs_4_, f32[640,128]{1,0:T(8,128)S(1)} %get-tuple-element.30.hidden, bf16[640,128]{1,0:T(8,128)(2,1)S(1)} %collective-permute-done.1.got_hidden, bf16[4,64,256]{2,1,0:T(8,128)(2,1)S(1)} %pack.1.after.mine, ...), custom_call_target="tpu_custom_call" | custom-call | flops 251658240 | bytes 1638400 | tf_op jit(solution)/shard_map/far/pallas_call | solution.py:348
  17.7 0.6 %collective-permute-start.10 = (bf16[640,256]{1,0:T(8,128)(2,1)S(1)}, bf16[640,256]{1,0:T(8,128)(2,1)S(1)}, u32[]{:S(2)}, u32[]{:S(2)}) collective-permute-start(bf16[640,256]{1,0:T(8,128)(2,1)S(1)} %get-tuple-element.48), channel_id=1, source_target_pairs={{0,2},{1,3},{2,0},{3,1},{4,6},{5,7},{6,4},{7,5},{8,10},{9,11},{10,... | collective-permute-start | bytes 983048 | tf_op jit(solution)/shard_map/ppermute | solution.py:233
  18.3 0.0 collective-permute-start.8
  18.3 0.5 %collective-permute-start.9 = (bf16[320,256]{1,0:T(8,128)(2,1)S(1)}, bf16[320,256]{1,0:T(8,128)(2,1)S(1)}, u32[]{:S(2)}, u32[]{:S(2)}) collective-permute-start(bf16[320,256]{1,0:T(8,128)(2,1)S(1)} %get-tuple-element.47), channel_id=1, source_target_pairs={{0,1},{1,0},{2,3},{3,2},{4,5},{5,4},{6,7},{7,6},{8,9},{9,8},{10,11... | collective-permute-start | bytes 491528 | tf_op jit(solution)/shard_map/ppermute | solution.py:230
  18.8 0.9 %near_keep.1.keep = f32[640,256]{1,0:T(8,128)S(1)} custom-call(bf16[640,2048]{1,0:T(8,128)(2,1)S(1)} %copy-done.1, bf16[2048,1024]{1,0:T(8,128)(2,1)S(1)} %copy-done, bf16[640,256]{1,0:T(8,128)(2,1)S(1)} %get-tuple-element.44.after.refs_2_.part), custom_call_target="tpu_custom_call" | custom-call | flops 671088640 | bytes 3670016 | tf_op jit(solution)/shard_map/near_keep/pallas_call | solution.py:296
  19.7 0.0 collective-permute-done.8.rest_0_
  19.7 0.2 collective-permute-done.9.rest_1_
  19.9 0.2 near.1
  20.2 7.3 %collective-permute-done.10.rest_0_ = bf16[640,256]{1,0:T(8,128)(2,1)S(1)} collective-permute-done((bf16[640,256]{1,0:T(8,128)(2,1)S(1)}, bf16[640,256]{1,0:T(8,128)(2,1)S(1)}, u32[]{:S(2)}, u32[]{:S(2)}) %collective-permute-start.10) | collective-permute-done | bytes 327712 | tf_op jit(solution)/shard_map/ppermute | solution.py:233
  27.5 0.8 %final.1 = bf16[640,256]{1,0:T(8,128)(2,1)} custom-call(f32[640,256]{1,0:T(8,128)S(1)} %near.1, bf16[640,256]{1,0:T(8,128)(2,1)S(1)} %collective-permute-done.10.rest_0_), custom_call_target="tpu_custom_call" | custom-call | bytes 1310720 | tf_op jit(solution)/shard_map/final/pallas_call | solution.py:380
  (6 shorter events, 0.1 us)
Async XLA Ops:
  0.0 2.9 %copy-start.3 = (bf16[256,256]{1,0:T(8,128)(2,1)S(1)}, bf16[256,256]{1,0:T(8,128)(2,1)}, u32[]{:S(2)}) copy-start(bf16[256,256]{1,0:T(8,128)(2,1)} %up.3) | copy-start | bytes 393220
  0.0 6.0 %copy-start.5 = (s32[16]{0:T(128)S(1)}, s32[16]{0:T(128)}, u32[]{:S(2)}) copy-start(s32[16]{0:T(128)} %adapters.1) | copy-start | bytes 196
  0.0 6.0 %copy-start.4 = (s32[2048]{0:T(1024)S(1)}, s32[2048]{0:T(1024)}, u32[]{:S(2)}) copy-start(s32[2048]{0:T(1024)} %slots.1) | copy-start | bytes 24580
  0.0 6.0 %copy-start.6 = (s32[16]{0:T(128)S(1)}, s32[16]{0:T(128)}, u32[]{:S(2)}) copy-start(s32[16]{0:T(128)} %lengths.1) | copy-start | bytes 196
  3.0 10.2 %collective-permute-start = (bf16[1152,128]{1,0:T(8,128)(2,1)S(1)}, bf16[1152,128]{1,0:T(8,128)(2,1)S(1)}, u32[]{:S(2)}, u32[]{:S(2)}) collective-permute-start(bf16[1152,128]{1,0:T(8,128)(2,1)S(1)} %get-tuple-element.29), channel_id=1, source_target_pairs={{0,2},{1,3},{2,0},{3,1},{4,6},{5,7},{6,4},{7,5},{8,10},{9,11},{10,... | collective-permute-start | bytes 884744 | tf_op jit(solution)/shard_map/ppermute | solution.py:233
  6.1 5.5 %copy-start = (bf16[2048,1024]{1,0:T(8,128)(2,1)S(1)}, bf16[2048,1024]{1,0:T(8,128)(2,1)}, u32[]{:S(2)}) copy-start(bf16[2048,1024]{1,0:T(8,128)(2,1)} %weight.5) | copy-start | bytes 12582916
  6.1 5.5 %copy-start.1 = (bf16[640,2048]{1,0:T(8,128)(2,1)S(1)}, bf16[640,2048]{1,0:T(8,128)(2,1)}, u32[]{:S(2)}) copy-start(bf16[640,2048]{1,0:T(8,128)(2,1)} %tokens.5) | copy-start | bytes 7864324
  7.3 6.4 %collective-permute-start.2 = (bf16[64,256]{1,0:T(8,128)(2,1)S(1)}, bf16[64,256]{1,0:T(8,128)(2,1)S(1)}, u32[]{:S(2)}, u32[]{:S(2)}) collective-permute-start(bf16[64,256]{1,0:T(8,128)(2,1)S(1)} %get-tuple-element.38), channel_id=1, source_target_pairs={{0,8},{4,12},{8,0},{12,4},{1,9},{5,13},{9,1},{13,5},{2,10},{6,14},... | collective-permute-start | bytes 98312 | tf_op jit(solution)/shard_map/ppermute | solution.py:238
  10.0 5.7 %collective-permute-start.3 = (bf16[64,256]{1,0:T(8,128)(2,1)S(1)}, bf16[64,256]{1,0:T(8,128)(2,1)S(1)}, u32[]{:S(2)}, u32[]{:S(2)}) collective-permute-start(bf16[64,256]{1,0:T(8,128)(2,1)S(1)} %get-tuple-element.39), channel_id=1, source_target_pairs={{0,12},{4,8},{8,4},{12,0},{1,13},{5,9},{9,5},{13,1},{2,14},{6,10},... | collective-permute-start | bytes 98312 | tf_op jit(solution)/shard_map/ppermute | solution.py:238
  11.3 4.4 %collective-permute-start.4 = (bf16[64,256]{1,0:T(8,128)(2,1)S(1)}, bf16[64,256]{1,0:T(8,128)(2,1)S(1)}, u32[]{:S(2)}, u32[]{:S(2)}) collective-permute-start(bf16[64,256]{1,0:T(8,128)(2,1)S(1)} %get-tuple-element.40), channel_id=1, source_target_pairs={{0,4},{4,0},{8,12},{12,8},{1,5},{5,1},{9,13},{13,9},{2,6},{6,2},{1... | collective-permute-start | bytes 98312 | tf_op jit(solution)/shard_map/ppermute | solution.py:238
  11.6 2.4 %copy-start.2 = (bf16[2048,256]{1,0:T(8,128)(2,1)S(1)}, bf16[2048,256]{1,0:T(8,128)(2,1)}, u32[]{:S(2)}) copy-start(bf16[2048,256]{1,0:T(8,128)(2,1)} %refs_2_.1) | copy-start | bytes 3145732
  13.1 3.6 %collective-permute-start.6 = (bf16[1,320,256]{2,1,0:T(8,128)(2,1)S(1)}, bf16[1,320,256]{2,1,0:T(8,128)(2,1)S(1)}, u32[]{:S(2)}, u32[]{:S(2)}) collective-permute-start(bf16[1,320,256]{2,1,0:T(8,128)(2,1)S(1)} %get-tuple-element.41), channel_id=1, source_target_pairs={{0,1},{1,0},{2,3},{3,2},{4,5},{5,4},{6,7},{7,6},{8,9},{9,8},{10,11... | collective-permute-start | bytes 491528 | tf_op jit(solution)/shard_map/ppermute | solution.py:230
  13.2 3.5 %collective-permute-start.7 = (bf16[1,320,256]{2,1,0:T(8,128)(2,1)S(1)}, bf16[1,320,256]{2,1,0:T(8,128)(2,1)S(1)}, u32[]{:S(2)}, u32[]{:S(2)}) collective-permute-start(bf16[1,320,256]{2,1,0:T(8,128)(2,1)S(1)} %get-tuple-element.42), channel_id=1, source_target_pairs={{0,1},{1,0},{2,3},{3,2},{4,5},{5,4},{6,7},{7,6},{8,9},{9,8},{10,11... | collective-permute-start | bytes 491528 | tf_op jit(solution)/shard_map/ppermute | solution.py:230
  13.8 3.4 %collective-permute-start.1 = (bf16[640,128]{1,0:T(8,128)(2,1)S(1)}, bf16[640,128]{1,0:T(8,128)(2,1)S(1)}, u32[]{:S(2)}, u32[]{:S(2)}) collective-permute-start(bf16[640,128]{1,0:T(8,128)(2,1)S(1)} %get-tuple-element.37), channel_id=1, source_target_pairs={{0,1},{1,0},{2,3},{3,2},{4,5},{5,4},{6,7},{7,6},{8,9},{9,8},{10,11... | collective-permute-start | bytes 491528 | tf_op jit(solution)/shard_map/ppermute | solution.py:230
  15.7 1.4 %collective-permute-start.5 = (bf16[4,64,256]{2,1,0:T(8,128)(2,1)S(1)}, bf16[4,64,256]{2,1,0:T(8,128)(2,1)S(1)}, u32[]{:S(2)}, u32[]{:S(2)}) collective-permute-start(bf16[4,64,256]{2,1,0:T(8,128)(2,1)S(1)} %pack.1.after.mine), channel_id=1, source_target_pairs={{0,1},{1,0},{2,3},{3,2},{4,5},{5,4},{6,7},{7,6},{8,9},{9,8},{10,11... | collective-permute-start | bytes 393224 | tf_op jit(solution)/shard_map/ppermute | solution.py:230
  17.7 9.8 %collective-permute-start.10 = (bf16[640,256]{1,0:T(8,128)(2,1)S(1)}, bf16[640,256]{1,0:T(8,128)(2,1)S(1)}, u32[]{:S(2)}, u32[]{:S(2)}) collective-permute-start(bf16[640,256]{1,0:T(8,128)(2,1)S(1)} %get-tuple-element.48), channel_id=1, source_target_pairs={{0,2},{1,3},{2,0},{3,1},{4,6},{5,7},{6,4},{7,5},{8,10},{9,11},{10,... | collective-permute-start | bytes 983048 | tf_op jit(solution)/shard_map/ppermute | solution.py:233
  18.3 1.4 %collective-permute-start.8 = (bf16[320,256]{1,0:T(8,128)(2,1)S(1)}, bf16[320,256]{1,0:T(8,128)(2,1)S(1)}, u32[]{:S(2)}, u32[]{:S(2)}) collective-permute-start(bf16[320,256]{1,0:T(8,128)(2,1)S(1)} %get-tuple-element.46), channel_id=1, source_target_pairs={{0,1},{1,0},{2,3},{3,2},{4,5},{5,4},{6,7},{7,6},{8,9},{9,8},{10,11... | collective-permute-start | bytes 491528 | tf_op jit(solution)/shard_map/ppermute | solution.py:230
  18.3 1.6 %collective-permute-start.9 = (bf16[320,256]{1,0:T(8,128)(2,1)S(1)}, bf16[320,256]{1,0:T(8,128)(2,1)S(1)}, u32[]{:S(2)}, u32[]{:S(2)}) collective-permute-start(bf16[320,256]{1,0:T(8,128)(2,1)S(1)} %get-tuple-element.47), channel_id=1, source_target_pairs={{0,1},{1,0},{2,3},{3,2},{4,5},{5,4},{6,7},{7,6},{8,9},{9,8},{10,11... | collective-permute-start | bytes 491528 | tf_op jit(solution)/shard_map/ppermute | solution.py:230

commit v7 on v5

--- a/solution.py
+++ b/solution.py
@@ -158,51 +158,52 @@
     keep[...] = block_product(width, 0, 0, tokens, weight)
 
 
-def far_kernel(width, halves, mask, hidden, got_hidden, mine, others, *rest):
+def far_kernel(width, at, mask, hidden, got_hidden, mine, others, *rest):
     ups, keep, rest = rest[: width - 1], rest[width - 1], rest[width:]
-    gots, rest = rest[: -halves * (width - 1) - 3], rest[-halves * (width - 1) - 2 :]
+    gots, rest = rest[: -width - 2], rest[-width - 1 :]
     outs, core_out, rhs = rest[:-2], rest[-2], rest[-1]
     core = lax.axis_index("tensor") % CORES
     owners = mask.shape[1] // hidden.shape[1]
-    rank = core_out.shape[1]
-    block = hidden.shape[1] // CORES
-    owners = mask.shape[1] // hidden.shape[1]
+    size, rank = core_out.shape
+    rows, block = hidden.shape[0], hidden.shape[1] // CORES
     for s in range(owners):
-        for cores, at in ((mine, core), (others, 1 - core)):
-            rhs[pl.ds(pl.multiple_of((s * CORES + at) * block, block), block), :] = cores[s]
-    total = (hidden[...] + got_hidden[...].astype(F32)).astype(BF16)
-    lhs = jnp.concatenate([total] * owners, axis=1) * mask[...]
+        for cores, half in ((mine, core), (others, 1 - core)):
+            to = pl.multiple_of((s * CORES + half) * block, block)
+            rhs[pl.ds(to, block), :] = cores[s]
+    total = (hidden[at : at + size, :] + got_hidden[at : at + size, :].astype(F32)).astype(BF16)
+    lhs = jnp.concatenate([total] * owners, axis=1) * mask[at : at + size, :]
     part = jnp.dot(lhs, rhs[...], preferred_element_type=F32).astype(BF16)
     core_out[...] = part
-    rows = part.shape[0]
-    size = rows // halves
     for i in range(width - 1):
         up = jnp.concatenate(
-            [ups[i][pl.ds(at, rank), :] for at in range(rows, ups[i].shape[0], rank)], axis=1
+            [ups[i][pl.ds(r, rank), :] for r in range(rows, ups[i].shape[0], rank)], axis=1
         )
         lifted = jnp.dot(part, up, preferred_element_type=F32)
-        got = jnp.concatenate([a[i] for a in gots], axis=0).astype(F32)
-        sent = (keep[i] + got + lifted).astype(BF16)
-        for j in range(halves):
-            outs[i * halves + j][...] = sent[j * size : (j + 1) * size]
-
-
-def near_kernel(up, keep, part, *rest):
+        got = jnp.concatenate([a[i] for a in gots], axis=0)[at : at + size].astype(F32)
+        outs[i][...] = (keep[i, at : at + size, :] + got + lifted).astype(BF16)
+
+
+def near_kernel(parts, up, keep, *rest):
+    core_outs, gots, out = rest[:-parts - 1], rest[-parts - 1 : -1], rest[-1]
+    got = jnp.concatenate([a[...] for a in gots], axis=0).astype(F32)
+    at = 0
+    for part in core_outs:
+        to = at + part.shape[0]
+        lifted = jnp.dot(part[...], up[...], preferred_element_type=F32)
+        out[at:to, :] = keep[at:to, :] + got[at:to] + lifted
+        at = to
+
+
+def final_kernel(pieces, near, *rest):
     gots, out = rest[:-1], rest[-1]
-    lifted = jnp.dot(part[...], up[...], preferred_element_type=F32)
-    got = jnp.concatenate([a[...] for a in gots], axis=0).astype(F32)
-    out[...] = keep[...] + got + lifted
-
-
-def final_kernel(halves, near, *rest):
-    gots, out = rest[:-1], rest[-1]
-    size = near.shape[0] // halves
-    for i in range(halves):
-        rows = pl.ds(i * size, size)
-        total = near[rows, :]
-        for got in gots[i::halves]:
+    at = 0
+    for i in range(pieces):
+        to = at + gots[i].shape[0]
+        total = near[at:to, :]
+        for got in gots[i::pieces]:
             total = total + got[...].astype(F32)
-        out[rows, :] = total.astype(BF16)
+        out[at:to, :] = total.astype(BF16)
+        at = to
 
 
 def local(
@@ -333,42 +334,48 @@
     )
     far_got = [pair(a) for a in far_send]
 
-    halves = 1
-    size = rows // halves
-    outs = pl.pallas_call(
-        functools.partial(far_kernel, width, halves),
-        out_shape=[jax.ShapeDtypeStruct((size, out_block), BF16)] * (halves * (width - 1))
-        + [jax.ShapeDtypeStruct((rows, rank), BF16)],
-        in_specs=[VMEM] * (5 + width + parts) + [ANY],
-        out_specs=[VMEM] * (halves * (width - 1) + 1),
-        scratch_shapes=[pltpu.VMEM((owners * cols, rank), BF16)],
-        compiler_params=params(),
-        cost_estimate=cost(2 * rows * (owners * cols * rank + rank * out_block), rows * out_block * 10),
-        name="far",
-    )(mask, hidden, got_hidden, packed, got_packed, *gots[::-1], far_keep, *far_got, near_send[0])
-    core_out = outs[-1]
-    far_gots = [along_x(outs[i], i // halves + 1) for i in range(halves * (width - 1))]
-
-    near_got = [pair(a) for a in ordered(near_send, core_out)]
+    first = rows * 3 // 5 // 16 * 16
+    pieces = [(0, first), (first, rows - first)]
+    core_outs, sent = [], []
+    for at, size in pieces:
+        outs = pl.pallas_call(
+            functools.partial(far_kernel, width, at),
+            out_shape=[jax.ShapeDtypeStruct((size, out_block), BF16)] * (width - 1)
+            + [jax.ShapeDtypeStruct((size, rank), BF16)],
+            in_specs=[VMEM] * (5 + width + parts) + [ANY],
+            out_specs=[VMEM] * width,
+            scratch_shapes=[pltpu.VMEM((owners * cols, rank), BF16)],
+            compiler_params=params(),
+            cost_estimate=cost(2 * size * (owners * cols * rank + rank * out_block), size * out_block * 10),
+            name="far",
+        )(
+            mask, hidden, got_hidden, packed, got_packed, *gots[::-1], far_keep, *far_got,
+            core_outs[-1] if core_outs else near_send[0],
+        )
+        sent.append([along_x(outs[s - 1], s) for s in range(1, width)])
+        core_outs.append(outs[-1])
+    far_gots = [piece[s] for s in range(width - 1) for piece in sent]
+
+    near_got = [pair(a) for a in ordered(near_send, core_outs[0])]
     (near_keep,) = base(
         functools.partial(near_keep_kernel, width),
         [jax.ShapeDtypeStruct((rows, out_block), F32)],
-        [core_out],
+        [core_outs[0]],
         "near_keep",
         1,
     )
     near = pl.pallas_call(
-        near_kernel,
+        functools.partial(near_kernel, parts),
         out_shape=jax.ShapeDtypeStruct((rows, out_block), F32),
-        in_specs=[VMEM] * (3 + parts),
+        in_specs=[VMEM] * (2 + len(pieces) + parts),
         out_specs=VMEM,
         compiler_params=params(),
         cost_estimate=cost(2 * rows * rank * out_block, rows * out_block * 12),
         name="near",
-    )(up_basis, near_keep, core_out, *near_got)
+    )(up_basis, near_keep, *core_outs, *near_got)
 
     return pl.pallas_call(
-        functools.partial(final_kernel, halves),
+        functools.partial(final_kernel, len(pieces)),
         out_shape=jax.ShapeDtypeStruct((rows, out_block), BF16),
         in_specs=[VMEM] * (1 + len(far_gots)),
         out_specs=VMEM,

time: 28.4 us -> 28.3 us (level)
  waiting for transfers between devices: 9.12 us -> 7.11 us
  starting transfers between devices: 9.14 us -> 10.7 us
  Pallas kernels: 6.92 us -> 7.25 us
    ppermute x2 -> x3, waiting for transfers between devices: 7.34 us -> 5.58 us  [along_x(): lax.ppermute(a, 'tensor', [(i, (i + shift * CORES) % tensor) for i in ran...]
    ppermute x2 -> x3, starting transfers between devices: 3.61 us -> 5.17 us  [along_x(): lax.ppermute(a, 'tensor', [(i, (i + shift * CORES) % tensor) for i in ran...]
    pallas_call x3 -> x4, Pallas kernels: 1.59 us -> 1.92 us  [the longest x2 0.87 us: local(): pl.pallas_call(functools.partial(far_kernel, width, at), out_shape=[jax.S...]
  transfers between devices with their start and end apart: 11 -> 12, of which waited for: 4 -> 3; matrix products, arithmetic and copies ran while one was open for 0% -> 0% of each run, Pallas kernels for 19% -> 21%
where the time goes in v7:
time: 28.3 us; the launch traced here: 28.2 us
  starting transfers between devices  10.7 us (38%)
  Pallas kernels  7.25 us (26%)
  waiting for transfers between devices  7.11 us (25%)
  matrix products  2.89 us (10%)
    ppermute x3, waiting for transfers between devices, along_x(): lax.ppermute(a, 'tensor', [(i, (i + shift * CORES) % tensor) for i in ran...  5.58 us
    ppermute x3, starting transfers between devices, along_x(): lax.ppermute(a, 'tensor', [(i, (i + shift * CORES) % tensor) for i in ran...  5.17 us
    ppermute x3, starting transfers between devices, along_dp(): return lax.ppermute(a, 'dp', [(i, i ^ shift) for i in range(owners)])  4.23 us
    pallas_call x3, Pallas kernels, base(): pl.pallas_call(kernel, out_shape=shapes, in_specs=[VMEM] * (1 + len(after...  3.31 us
    dot_general x1, matrix products, local(): part = jnp.dot(tokens, down_basis, preferred_element_type=F32)  2.89 us
    ppermute x6, starting transfers between devices, pair(): return lax.ppermute(a, 'tensor', [(i, i ^ 1) for i in range(tensor)])  1.29 us
    pallas_call x1, Pallas kernels, local(): pl.pallas_call(functools.partial(pick_kernel, (owners, req_dev, per_owner...  1.23 us
    ppermute x3, waiting for transfers between devices, along_dp(): return lax.ppermute(a, 'dp', [(i, i ^ shift) for i in range(owners)])  1.11 us
  transfers between devices with their start and end apart: 12, of which 3 were waited for; matrix products, arithmetic and copies ran while one was open for 0% of the time, Pallas kernels for 21%

profile of v7, /device:TPU:0, one launch (start us, length us, event | category | flops | bytes accessed | tf_op | source)
XLA Modules:
  0.0 28.2 jit_solution(5539898317438278188)
XLA Ops:
  0.0 0.0 copy-start.3
  0.0 0.0 copy-start.5
  0.0 0.0 copy-start.4
  0.0 0.0 copy-start.6
  0.0 2.9 %fusion.part = f32[640,256]{1,0:T(8,128)S(1)} fusion(bf16[640,2048]{1,0:T(8,128)(2,1)} %tokens.5, bf16[2048,256]{1,0:T(8,128)(2,1)} %refs_2_.1), kind=kOutput, calls=%fused_computation | convolution fusion | flops 671088640 | bytes 4325376 | tf_op jit(solution)/shard_map/dot_general | solution.py:231
  2.9 0.0 copy-done.3
  2.9 0.1 split.1
  3.0 3.0 %collective-permute-start = (bf16[1152,128]{1,0:T(8,128)(2,1)S(1)}, bf16[1152,128]{1,0:T(8,128)(2,1)S(1)}, u32[]{:S(2)}, u32[]{:S(2)}) collective-permute-start(bf16[1152,128]{1,0:T(8,128)(2,1)S(1)} %get-tuple-element.31), channel_id=1, source_target_pairs={{0,2},{1,3},{2,0},{3,1},{4,6},{5,7},{6,4},{7,5},{8,10},{9,11},{10,... | collective-permute-start | bytes 884744 | tf_op jit(solution)/shard_map/ppermute | solution.py:224
  6.0 0.0 copy-done.5
  6.0 0.0 copy-done.4
  6.0 0.0 copy-done.6
  6.1 0.0 copy-start
  6.1 0.0 copy-start.1
  6.1 1.2 %pick.1 = (bf16[64,256]{1,0:T(8,128)(2,1)S(1)}, bf16[64,256]{1,0:T(8,128)(2,1)S(1)}, bf16[64,256]{1,0:T(8,128)(2,1)S(1)}, bf16[64,256]{1,0:T(8,128)(2,1)S(1)}, s32[8,128]{1,0:T(8,128)S(1)}) custom-call(s32[1,16]{1,0:T(1,128)S(1)} %bitcast.5, s32[16,128]{1,0:T(8,128)S(1)} %bitcast.4, s32[16]{0:T(128)S(1)} %copy-done.5, s32[16]{0:T(128)S(1)} %copy-done.6, ...), custom_call_target="tpu_custom_call" | custom-call | bytes 2097152 | tf_op jit(solution)/shard_map/pick/pallas_call | solution.py:245
  7.3 2.7 %collective-permute-start.2 = (bf16[64,256]{1,0:T(8,128)(2,1)S(1)}, bf16[64,256]{1,0:T(8,128)(2,1)S(1)}, u32[]{:S(2)}, u32[]{:S(2)}) collective-permute-start(bf16[64,256]{1,0:T(8,128)(2,1)S(1)} %get-tuple-element.40), channel_id=1, source_target_pairs={{0,8},{4,12},{8,0},{12,4},{1,9},{5,13},{9,1},{13,5},{2,10},{6,14},... | collective-permute-start | bytes 98312 | tf_op jit(solution)/shard_map/ppermute | solution.py:229
  10.0 1.3 %collective-permute-start.3 = (bf16[64,256]{1,0:T(8,128)(2,1)S(1)}, bf16[64,256]{1,0:T(8,128)(2,1)S(1)}, u32[]{:S(2)}, u32[]{:S(2)}) collective-permute-start(bf16[64,256]{1,0:T(8,128)(2,1)S(1)} %get-tuple-element.41), channel_id=1, source_target_pairs={{0,12},{4,8},{8,4},{12,0},{1,13},{5,9},{9,5},{13,1},{2,14},{6,10},... | collective-permute-start | bytes 98312 | tf_op jit(solution)/shard_map/ppermute | solution.py:229
  11.3 0.2 collective-permute-start.4
  11.6 0.0 copy-done
  11.6 0.0 copy-done.1
  11.6 1.6 %far_base.1 = (f32[1,640,256]{2,1,0:T(8,128)S(1)}, bf16[1,320,256]{2,1,0:T(8,128)(2,1)S(1)}, bf16[1,320,256]{2,1,0:T(8,128)(2,1)S(1)}) custom-call(bf16[640,2048]{1,0:T(8,128)(2,1)S(1)} %copy-done.1, bf16[2048,1024]{1,0:T(8,128)(2,1)S(1)} %copy-done, bf16[64,256]{1,0:T(8,128)(2,1)S(1)} %get-tuple-element.37.after.refs_0_), custom_call_target="tpu_custom_call" | custom-call | flops 1342177280 | bytes 4718592 | tf_op jit(solution)/shard_map/far_base/pallas_call | solution.py:287
  13.1 0.1 collective-permute-start.6
  13.2 0.0 collective-permute-done.rest_0_
  13.2 0.5 %collective-permute-start.7 = (bf16[1,320,256]{2,1,0:T(8,128)(2,1)S(1)}, bf16[1,320,256]{2,1,0:T(8,128)(2,1)S(1)}, u32[]{:S(2)}, u32[]{:S(2)}) collective-permute-start(bf16[1,320,256]{2,1,0:T(8,128)(2,1)S(1)} %get-tuple-element.44), channel_id=1, source_target_pairs={{0,1},{1,0},{2,3},{3,2},{4,5},{5,4},{6,7},{7,6},{8,9},{9,8},{10,11... | collective-permute-start | bytes 491528 | tf_op jit(solution)/shard_map/ppermute | solution.py:221
  13.8 0.0 collective-permute-done.2.refs_1_
  13.8 0.2 collective-permute-start.1
  13.9 0.0 copy-done.2
  14.0 0.6 %mask.1.refs_4_ = bf16[640,512]{1,0:T(8,128)(2,1)S(1)} custom-call(s32[8,128]{1,0:T(8,128)S(1)} %get-tuple-element.30.table, f32[640,128]{1,0:T(8,128)S(1)} %ordered.4.after), custom_call_target="tpu_custom_call" | custom-call | bytes 655360 | tf_op jit(solution)/shard_map/mask/pallas_call | solution.py:308
  14.6 1.1 %collective-permute-done.3.refs_2_ = bf16[64,256]{1,0:T(8,128)(2,1)S(1)} collective-permute-done((bf16[64,256]{1,0:T(8,128)(2,1)S(1)}, bf16[64,256]{1,0:T(8,128)(2,1)S(1)}, u32[]{:S(2)}, u32[]{:S(2)}) %collective-permute-start.3) | collective-permute-done | bytes 32800 | tf_op jit(solution)/shard_map/ppermute | solution.py:229
  15.7 0.0 collective-permute-done.4.refs_3_
  15.7 0.1 collective-permute-start.5
  15.8 0.9 %near_send.1 = (bf16[320,256]{1,0:T(8,128)(2,1)S(1)}, bf16[320,256]{1,0:T(8,128)(2,1)S(1)}) custom-call(bf16[640,2048]{1,0:T(8,128)(2,1)S(1)} %copy-done.1, bf16[2048,1024]{1,0:T(8,128)(2,1)S(1)} %copy-done, bf16[4,64,256]{2,1,0:T(8,128)(2,1)S(1)} %pack.1.after.mine), custom_call_target="tpu_custom_call" | custom-call | flops 671088640 | bytes 3670016 | tf_op jit(solution)/shard_map/near_send/pallas_call | solution.py:287
  16.7 0.0 collective-permute-done.6.rest_2_
  16.7 0.0 collective-permute-done.7.rest_3_
  16.7 0.4 %collective-permute-done.5.others = bf16[4,64,256]{2,1,0:T(8,128)(2,1)S(1)} collective-permute-done((bf16[4,64,256]{2,1,0:T(8,128)(2,1)S(1)}, bf16[4,64,256]{2,1,0:T(8,128)(2,1)S(1)}, u32[]{:S(2)}, u32[]{:S(2)}) %collective-permute-start.5) | collective-permute-done | bytes 131104 | tf_op jit(solution)/shard_map/ppermute | solution.py:221
  17.1 0.0 collective-permute-done.1.got_hidden
  17.1 0.5 %far.2 = (bf16[384,256]{1,0:T(8,128)(2,1)S(1)}, bf16[384,256]{1,0:T(8,128)(2,1)S(1)}) custom-call(bf16[640,512]{1,0:T(8,128)(2,1)S(1)} %mask.1.refs_4_, f32[640,128]{1,0:T(8,128)S(1)} %get-tuple-element.32.hidden, bf16[640,128]{1,0:T(8,128)(2,1)S(1)} %collective-permute-done.1.got_hidden, bf16[4,64,256]{2,1,0:T(8,128)(2,1)S(1)} %pack.1.after.mine, ...), custom_call_target="tpu_custom_call" | custom-call | flops 150994944 | bytes 983040 | tf_op jit(solution)/shard_map/far/pallas_call | solution.py:341
  17.6 0.6 %collective-permute-start.10 = (bf16[384,256]{1,0:T(8,128)(2,1)S(1)}, bf16[384,256]{1,0:T(8,128)(2,1)S(1)}, u32[]{:S(2)}, u32[]{:S(2)}) collective-permute-start(bf16[384,256]{1,0:T(8,128)(2,1)S(1)} %get-tuple-element.51), channel_id=1, source_target_pairs={{0,2},{1,3},{2,0},{3,1},{4,6},{5,7},{6,4},{7,5},{8,10},{9,11},{10,... | collective-permute-start | bytes 589832 | tf_op jit(solution)/shard_map/ppermute | solution.py:224
  18.2 0.0 collective-permute-start.8
  18.2 0.5 %collective-permute-start.9 = (bf16[320,256]{1,0:T(8,128)(2,1)S(1)}, bf16[320,256]{1,0:T(8,128)(2,1)S(1)}, u32[]{:S(2)}, u32[]{:S(2)}) collective-permute-start(bf16[320,256]{1,0:T(8,128)(2,1)S(1)} %get-tuple-element.50), channel_id=1, source_target_pairs={{0,1},{1,0},{2,3},{3,2},{4,5},{5,4},{6,7},{7,6},{8,9},{9,8},{10,11... | collective-permute-start | bytes 491528 | tf_op jit(solution)/shard_map/ppermute | solution.py:221
  18.7 0.4 %far.3 = (bf16[256,256]{1,0:T(8,128)(2,1)S(1)}, bf16[256,256]{1,0:T(8,128)(2,1)S(1)}) custom-call(bf16[640,512]{1,0:T(8,128)(2,1)S(1)} %mask.1.refs_4_, f32[640,128]{1,0:T(8,128)S(1)} %get-tuple-element.32.hidden, bf16[640,128]{1,0:T(8,128)(2,1)S(1)} %collective-permute-done.1.got_hidden, bf16[4,64,256]{2,1,0:T(8,128)(2,1)S(1)} %pack.1.after.mine, ...), custom_call_target="tpu_custom_call" | custom-call | flops 100663296 | bytes 655360 | tf_op jit(solution)/shard_map/far/pallas_call | solution.py:341
  19.1 1.6 %collective-permute-start.11 = (bf16[256,256]{1,0:T(8,128)(2,1)S(1)}, bf16[256,256]{1,0:T(8,128)(2,1)S(1)}, u32[]{:S(2)}, u32[]{:S(2)}) collective-permute-start(bf16[256,256]{1,0:T(8,128)(2,1)S(1)} %get-tuple-element.52), channel_id=1, source_target_pairs={{0,2},{1,3},{2,0},{3,1},{4,6},{5,7},{6,4},{7,5},{8,10},{9,11},{10,... | collective-permute-start | bytes 393224 | tf_op jit(solution)/shard_map/ppermute | solution.py:224
  20.7 0.9 %near_keep.1.keep = f32[640,256]{1,0:T(8,128)S(1)} custom-call(bf16[640,2048]{1,0:T(8,128)(2,1)S(1)} %copy-done.1, bf16[2048,1024]{1,0:T(8,128)(2,1)S(1)} %copy-done, bf16[384,256]{1,0:T(8,128)(2,1)S(1)} %get-tuple-element.46.after.rest_4_.refs_2_.rest_0_), custom_call_target="tpu_custom_call" | custom-call | flops 671088640 | bytes 3670016 | tf_op jit(solution)/shard_map/near_keep/pallas_call | solution.py:287
  21.5 0.0 collective-permute-done.8.rest_2_
  21.6 0.0 collective-permute-done.9.rest_3_
  21.6 0.3 near.1
  21.8 5.6 %collective-permute-done.11.rest_1_ = bf16[256,256]{1,0:T(8,128)(2,1)S(1)} collective-permute-done((bf16[256,256]{1,0:T(8,128)(2,1)S(1)}, bf16[256,256]{1,0:T(8,128)(2,1)S(1)}, u32[]{:S(2)}, u32[]{:S(2)}) %collective-permute-start.11) | collective-permute-done | bytes 131104 | tf_op jit(solution)/shard_map/ppermute | solution.py:224
  27.4 0.0 collective-permute-done.10.rest_0_
  27.4 0.8 %final.1 = bf16[640,256]{1,0:T(8,128)(2,1)} custom-call(f32[640,256]{1,0:T(8,128)S(1)} %near.1, bf16[384,256]{1,0:T(8,128)(2,1)S(1)} %collective-permute-done.10.rest_0_, bf16[256,256]{1,0:T(8,128)(2,1)S(1)} %collective-permute-done.11.rest_1_), custom_call_target="tpu_custom_call" | custom-call | bytes 1310720 | tf_op jit(solution)/shard_map/final/pallas_call | solution.py:377
  (7 shorter events, 0.1 us)
Async XLA Ops:
  0.0 2.9 %copy-start.3 = (bf16[256,256]{1,0:T(8,128)(2,1)S(1)}, bf16[256,256]{1,0:T(8,128)(2,1)}, u32[]{:S(2)}) copy-start(bf16[256,256]{1,0:T(8,128)(2,1)} %up.3) | copy-start | bytes 393220
  0.0 6.0 %copy-start.5 = (s32[16]{0:T(128)S(1)}, s32[16]{0:T(128)}, u32[]{:S(2)}) copy-start(s32[16]{0:T(128)} %adapters.1) | copy-start | bytes 196
  0.0 6.0 %copy-start.4 = (s32[2048]{0:T(1024)S(1)}, s32[2048]{0:T(1024)}, u32[]{:S(2)}) copy-start(s32[2048]{0:T(1024)} %slots.1) | copy-start | bytes 24580
  0.0 6.0 %copy-start.6 = (s32[16]{0:T(128)S(1)}, s32[16]{0:T(128)}, u32[]{:S(2)}) copy-start(s32[16]{0:T(128)} %lengths.1) | copy-start | bytes 196
  3.0 10.2 %collective-permute-start = (bf16[1152,128]{1,0:T(8,128)(2,1)S(1)}, bf16[1152,128]{1,0:T(8,128)(2,1)S(1)}, u32[]{:S(2)}, u32[]{:S(2)}) collective-permute-start(bf16[1152,128]{1,0:T(8,128)(2,1)S(1)} %get-tuple-element.31), channel_id=1, source_target_pairs={{0,2},{1,3},{2,0},{3,1},{4,6},{5,7},{6,4},{7,5},{8,10},{9,11},{10,... | collective-permute-start | bytes 884744 | tf_op jit(solution)/shard_map/ppermute | solution.py:224
  6.1 5.5 %copy-start = (bf16[2048,1024]{1,0:T(8,128)(2,1)S(1)}, bf16[2048,1024]{1,0:T(8,128)(2,1)}, u32[]{:S(2)}) copy-start(bf16[2048,1024]{1,0:T(8,128)(2,1)} %weight.5) | copy-start | bytes 12582916
  6.1 5.5 %copy-start.1 = (bf16[640,2048]{1,0:T(8,128)(2,1)S(1)}, bf16[640,2048]{1,0:T(8,128)(2,1)}, u32[]{:S(2)}) copy-start(bf16[640,2048]{1,0:T(8,128)(2,1)} %tokens.5) | copy-start | bytes 7864324
  7.3 6.4 %collective-permute-start.2 = (bf16[64,256]{1,0:T(8,128)(2,1)S(1)}, bf16[64,256]{1,0:T(8,128)(2,1)S(1)}, u32[]{:S(2)}, u32[]{:S(2)}) collective-permute-start(bf16[64,256]{1,0:T(8,128)(2,1)S(1)} %get-tuple-element.40), channel_id=1, source_target_pairs={{0,8},{4,12},{8,0},{12,4},{1,9},{5,13},{9,1},{13,5},{2,10},{6,14},... | collective-permute-start | bytes 98312 | tf_op jit(solution)/shard_map/ppermute | solution.py:229
  10.0 5.7 %collective-permute-start.3 = (bf16[64,256]{1,0:T(8,128)(2,1)S(1)}, bf16[64,256]{1,0:T(8,128)(2,1)S(1)}, u32[]{:S(2)}, u32[]{:S(2)}) collective-permute-start(bf16[64,256]{1,0:T(8,128)(2,1)S(1)} %get-tuple-element.41), channel_id=1, source_target_pairs={{0,12},{4,8},{8,4},{12,0},{1,13},{5,9},{9,5},{13,1},{2,14},{6,10},... | collective-permute-start | bytes 98312 | tf_op jit(solution)/shard_map/ppermute | solution.py:229
  11.3 4.4 %collective-permute-start.4 = (bf16[64,256]{1,0:T(8,128)(2,1)S(1)}, bf16[64,256]{1,0:T(8,128)(2,1)S(1)}, u32[]{:S(2)}, u32[]{:S(2)}) collective-permute-start(bf16[64,256]{1,0:T(8,128)(2,1)S(1)} %get-tuple-element.42), channel_id=1, source_target_pairs={{0,4},{4,0},{8,12},{12,8},{1,5},{5,1},{9,13},{13,9},{2,6},{6,2},{1... | collective-permute-start | bytes 98312 | tf_op jit(solution)/shard_map/ppermute | solution.py:229
  11.6 2.4 %copy-start.2 = (bf16[2048,256]{1,0:T(8,128)(2,1)S(1)}, bf16[2048,256]{1,0:T(8,128)(2,1)}, u32[]{:S(2)}) copy-start(bf16[2048,256]{1,0:T(8,128)(2,1)} %refs_2_.1) | copy-start | bytes 3145732
  13.1 3.6 %collective-permute-start.6 = (bf16[1,320,256]{2,1,0:T(8,128)(2,1)S(1)}, bf16[1,320,256]{2,1,0:T(8,128)(2,1)S(1)}, u32[]{:S(2)}, u32[]{:S(2)}) collective-permute-start(bf16[1,320,256]{2,1,0:T(8,128)(2,1)S(1)} %get-tuple-element.43), channel_id=1, source_target_pairs={{0,1},{1,0},{2,3},{3,2},{4,5},{5,4},{6,7},{7,6},{8,9},{9,8},{10,11... | collective-permute-start | bytes 491528 | tf_op jit(solution)/shard_map/ppermute | solution.py:221
  13.2 3.5 %collective-permute-start.7 = (bf16[1,320,256]{2,1,0:T(8,128)(2,1)S(1)}, bf16[1,320,256]{2,1,0:T(8,128)(2,1)S(1)}, u32[]{:S(2)}, u32[]{:S(2)}) collective-permute-start(bf16[1,320,256]{2,1,0:T(8,128)(2,1)S(1)} %get-tuple-element.44), channel_id=1, source_target_pairs={{0,1},{1,0},{2,3},{3,2},{4,5},{5,4},{6,7},{7,6},{8,9},{9,8},{10,11... | collective-permute-start | bytes 491528 | tf_op jit(solution)/shard_map/ppermute | solution.py:221
  13.8 3.4 %collective-permute-start.1 = (bf16[640,128]{1,0:T(8,128)(2,1)S(1)}, bf16[640,128]{1,0:T(8,128)(2,1)S(1)}, u32[]{:S(2)}, u32[]{:S(2)}) collective-permute-start(bf16[640,128]{1,0:T(8,128)(2,1)S(1)} %get-tuple-element.39), channel_id=1, source_target_pairs={{0,1},{1,0},{2,3},{3,2},{4,5},{5,4},{6,7},{7,6},{8,9},{9,8},{10,11... | collective-permute-start | bytes 491528 | tf_op jit(solution)/shard_map/ppermute | solution.py:221
  15.7 1.4 %collective-permute-start.5 = (bf16[4,64,256]{2,1,0:T(8,128)(2,1)S(1)}, bf16[4,64,256]{2,1,0:T(8,128)(2,1)S(1)}, u32[]{:S(2)}, u32[]{:S(2)}) collective-permute-start(bf16[4,64,256]{2,1,0:T(8,128)(2,1)S(1)} %pack.1.after.mine), channel_id=1, source_target_pairs={{0,1},{1,0},{2,3},{3,2},{4,5},{5,4},{6,7},{7,6},{8,9},{9,8},{10,11... | collective-permute-start | bytes 393224 | tf_op jit(solution)/shard_map/ppermute | solution.py:221
  17.6 9.8 %collective-permute-start.10 = (bf16[384,256]{1,0:T(8,128)(2,1)S(1)}, bf16[384,256]{1,0:T(8,128)(2,1)S(1)}, u32[]{:S(2)}, u32[]{:S(2)}) collective-permute-start(bf16[384,256]{1,0:T(8,128)(2,1)S(1)} %get-tuple-element.51), channel_id=1, source_target_pairs={{0,2},{1,3},{2,0},{3,1},{4,6},{5,7},{6,4},{7,5},{8,10},{9,11},{10,... | collective-permute-start | bytes 589832 | tf_op jit(solution)/shard_map/ppermute | solution.py:224
  18.2 3.4 %collective-permute-start.8 = (bf16[320,256]{1,0:T(8,128)(2,1)S(1)}, bf16[320,256]{1,0:T(8,128)(2,1)S(1)}, u32[]{:S(2)}, u32[]{:S(2)}) collective-permute-start(bf16[320,256]{1,0:T(8,128)(2,1)S(1)} %get-tuple-element.49), channel_id=1, source_target_pairs={{0,1},{1,0},{2,3},{3,2},{4,5},{5,4},{6,7},{7,6},{8,9},{9,8},{10,11... | collective-permute-start | bytes 491528 | tf_op jit(solution)/shard_map/ppermute | solution.py:221
  18.2 3.4 %collective-permute-start.9 = (bf16[320,256]{1,0:T(8,128)(2,1)S(1)}, bf16[320,256]{1,0:T(8,128)(2,1)S(1)}, u32[]{:S(2)}, u32[]{:S(2)}) collective-permute-start(bf16[320,256]{1,0:T(8,128)(2,1)S(1)} %get-tuple-element.50), channel_id=1, source_target_pairs={{0,1},{1,0},{2,3},{3,2},{4,5},{5,4},{6,7},{7,6},{8,9},{9,8},{10,11... | collective-permute-start | bytes 491528 | tf_op jit(solution)/shard_map/ppermute | solution.py:221
  19.1 8.3 %collective-permute-start.11 = (bf16[256,256]{1,0:T(8,128)(2,1)S(1)}, bf16[256,256]{1,0:T(8,128)(2,1)S(1)}, u32[]{:S(2)}, u32[]{:S(2)}) collective-permute-start(bf16[256,256]{1,0:T(8,128)(2,1)S(1)} %get-tuple-element.52), channel_id=1, source_target_pairs={{0,2},{1,3},{2,0},{3,1},{4,6},{5,7},{6,4},{7,5},{8,10},{9,11},{10,... | collective-permute-start | bytes 393224 | tf_op jit(solution)/shard_map/ppermute | solution.py:224
